TPU v7x, 256 devices: a whole 4x4x8 slice. The times are simulated.
256 devices in a mesh: seq: 4 (over x), batch: 64 (over y, z, core).
Axes of the slice: x: 4, y: 4, z: 8, core: 2. Of those that a mesh axis runs over, the one named last changes fastest.
Arguments:
- history: bfloat16 [64, 512, 512], P('batch', 'seq'), may hold values from -6 to 6
- out_cotangent: bfloat16 [64, 512, 512], P('batch', 'seq'), may hold values from -6 to 6
- lengths: int32 [64], P('batch'), may hold values from 1 to 512, as said below
- bucket_of: int32 [512], replicated, may hold values from 0 to 127, as said below
- position_bias: float32 [4, 128], replicated, may hold values from -4 to 4
- norm_gain: float32 [512], replicated, may hold values from 0.1 to 1.9
- uvqk_weight: bfloat16 [512, 2048], replicated, may hold values from -0.25 to 0.25
- out_gain: float32 [512], replicated, may hold values from 0.1 to 1.9
- out_weight: bfloat16 [512, 512], replicated, may hold values from -0.25 to 0.25
Outputs:
- output: bfloat16 [64, 512, 512], P('batch', 'seq')
- grad_input: bfloat16 [64, 512, 512], P('batch', 'seq')
- grad_uvqk_weight: float32 [512, 2048], replicated
- grad_out_weight: float32 [512, 512], replicated
- grad_position_bias: float32 [4, 128], replicated
- grad_norm_gain: float32 [512], replicated
- grad_out_gain: float32 [512], replicated
Inputs may be any that keep to these rules, and one draw needn't show every extreme that they name: `lengths`: one history in every draw has length exactly 512. `bucket_of`: nondecreasing in the distance, 0 at distance 0 and 127 at distance 512 - 1.
All inputs are finite; a program needn't handle non-finite values.
Results may differ from a plain program's by a relative error of at most 0.0082.
Values may be sent and summed in bfloat16 or wider, within the bound.
No kernel may reach another device: no remote copies, remote signals or barrier semaphores. Data moves between devices by JAX's collectives and lax.ppermute only.
A program may use at most 128 MiB of HBM per device.

v0:
```python
import math

import jax
import jax.numpy as jnp
from jax import lax
from jax.sharding import PartitionSpec as P

NORM_EPS = 1e-05


def normalize(values):
    centered = values - jnp.mean(values, axis=-1, keepdims=True)
    inv_scale = lax.rsqrt(jnp.mean(centered * centered, axis=-1, keepdims=True) + NORM_EPS)
    return (centered * inv_scale, inv_scale)


def silu_slope(values):
    sigmoid = jax.nn.sigmoid(values)
    return sigmoid * (1.0 + values * (1.0 - sigmoid))


def norm_backward(grad_normed, normed, inv_scale):
    return inv_scale * (
        grad_normed
        - jnp.mean(grad_normed, axis=-1, keepdims=True)
        - normed * jnp.mean(grad_normed * normed, axis=-1, keepdims=True)
    )


def diagonal_sums(tile):
    head_count, query_count, key_count = tile.shape
    reversed_tile = tile[..., ::-1]
    padded_width = query_count + key_count
    padded = jnp.pad(reversed_tile, ((0, 0), (0, 0), (0, padded_width - key_count)))
    flattened = padded.reshape(head_count, query_count * padded_width)[
        :, : query_count * (padded_width - 1)
    ]
    return flattened.reshape(head_count, query_count, padded_width - 1).sum(axis=1)


def shards(
    history,
    out_cotangent,
    lengths,
    bucket_of,
    position_bias,
    norm_gain,
    uvqk_weight,
    out_gain,
    out_weight,
):
    row_count = history.shape[1]
    model_width = history.shape[2]
    head_count = position_bias.shape[0]
    bucket_count = position_bias.shape[1]
    head_dim = model_width // head_count
    history_len = bucket_of.shape[0]
    score_scale = 1.0 / math.sqrt(head_dim)
    length = lengths[0]
    query_start = lax.axis_index("seq") * row_count
    onehot = (bucket_of[:, None] == jnp.arange(bucket_count, dtype=jnp.int32)[None, :]).astype(
        jnp.float32
    )
    bias_by_distance = jnp.dot(position_bias, onehot.T, precision=lax.Precision.HIGHEST)

    def bias_tile(first_query, query_count, key_count):
        distance = (first_query + jnp.arange(query_count, dtype=jnp.int32))[:, None] - jnp.arange(
            key_count, dtype=jnp.int32
        )[None, :]
        return jnp.take(bias_by_distance, jnp.clip(distance, 0, history_len - 1), axis=1)

    def visible_tile(first_query, query_count, key_count):
        query_pos = first_query + jnp.arange(query_count, dtype=jnp.int32)
        key_pos = jnp.arange(key_count, dtype=jnp.int32)
        return (key_pos[None, :] <= query_pos[:, None]) & (query_pos[:, None] < length)

    def split_heads(block):
        return block.reshape(block.shape[0], head_count, head_dim)

    def tile_scores(query_block, key_block, first_query):
        raw_scores = jnp.einsum(
            "ihd,jhd->hij", query_block, key_block, preferred_element_type=jnp.float32
        )
        scores = raw_scores * score_scale + bias_tile(
            first_query, query_block.shape[0], key_block.shape[0]
        )
        visible = visible_tile(first_query, query_block.shape[0], key_block.shape[0])[None]
        return (scores, visible)

    history_wide = history[0].astype(jnp.float32)
    normed, inv_in = normalize(history_wide)
    scaled_low = (normed * norm_gain).astype(jnp.bfloat16)
    projected = jnp.dot(scaled_low, uvqk_weight, preferred_element_type=jnp.float32)
    activated = jax.nn.silu(projected)
    gating = activated[:, :model_width]
    value_low = activated[:, model_width : 2 * model_width].astype(jnp.bfloat16)
    query_low = activated[:, 2 * model_width : 3 * model_width].astype(jnp.bfloat16)
    key_low = activated[:, 3 * model_width :].astype(jnp.bfloat16)
    query_heads = split_heads(query_low)
    zero_rows = jnp.zeros((row_count, model_width), jnp.float32)
    key_piece = lax.all_gather(key_low, "seq", axis=0, tiled=True)
    value_piece = lax.all_gather(value_low, "seq", axis=0, tiled=True)
    key_block = split_heads(key_piece)
    value_block = split_heads(value_piece)
    scores, visible = tile_scores(query_heads, key_block, query_start)
    weights_low = jnp.where(visible, jax.nn.silu(scores), 0.0).astype(jnp.bfloat16)
    mixed_part = jnp.einsum(
        "hij,jhd->ihd", weights_low, value_block, preferred_element_type=jnp.float32
    )
    mixed_sum = mixed_part.reshape(row_count, model_width)
    mixed_normed, inv_mixed = normalize(mixed_sum)
    gated_low = (mixed_normed * out_gain * gating).astype(jnp.bfloat16)
    output = (
        history_wide + jnp.dot(gated_low, out_weight, preferred_element_type=jnp.float32)
    ).astype(jnp.bfloat16)
    cotangent = out_cotangent[0]
    grad_out_weight = jnp.dot(gated_low.T, cotangent, preferred_element_type=jnp.float32)
    grad_gated = jnp.dot(cotangent, out_weight.T, preferred_element_type=jnp.float32)
    grad_out_gain = jnp.sum(grad_gated * mixed_normed * gating, axis=0)
    grad_gating = grad_gated * mixed_normed * out_gain
    grad_mixed_low = norm_backward(grad_gated * out_gain * gating, mixed_normed, inv_mixed).astype(
        jnp.bfloat16
    )
    grad_heads = split_heads(grad_mixed_low)
    pad_left = row_count + 512
    zero_buffer = jnp.zeros((head_count, pad_left + history_len), jnp.float32)
    backward_init = (zero_rows, zero_buffer, jnp.zeros((history_len, 2 * model_width), jnp.float32))
    distance_sums = backward_init[1]
    key_piece = lax.all_gather(key_low, "seq", axis=0, tiled=True)
    value_piece = lax.all_gather(value_low, "seq", axis=0, tiled=True)
    smaller = min(512, key_piece.shape[0])
    key_block = split_heads(key_piece)
    value_block = split_heads(value_piece)
    scores, visible = tile_scores(query_heads, key_block, query_start)
    weights_low = jnp.where(visible, jax.nn.silu(scores), 0.0).astype(jnp.bfloat16)
    grad_weights = jnp.einsum(
        "ihd,jhd->hij", grad_heads, value_block, preferred_element_type=jnp.float32
    )
    grad_scores = jnp.where(visible, grad_weights * silu_slope(scores), 0.0)
    grad_scores_low = grad_scores.astype(jnp.bfloat16)
    query_term = (
        jnp.einsum(
            "hij,jhd->ihd", grad_scores_low, key_block, preferred_element_type=jnp.float32
        ).reshape(row_count, model_width)
        * score_scale
    )
    diagonal = diagonal_sums(grad_scores)
    key_term = (
        jnp.einsum(
            "hij,ihd->jhd", grad_scores_low, query_heads, preferred_element_type=jnp.float32
        ).reshape(smaller, model_width)
        * score_scale
    )
    value_term = jnp.einsum(
        "hij,ihd->jhd", weights_low, grad_heads, preferred_element_type=jnp.float32
    ).reshape(smaller, model_width)
    grad_query = query_term
    place = query_start - (smaller - 1) + pad_left
    distance_sums = lax.dynamic_update_slice_in_dim(distance_sums, diagonal, place, 1)
    key_terms = jnp.concatenate([key_term, value_term], axis=1)
    back_result = (grad_query, distance_sums, key_terms)
    grad_query = back_result[0]
    distance_grad = back_result[1][:, pad_left:]
    own_terms = lax.psum_scatter(back_result[2], "seq", scatter_dimension=0, tiled=True)
    grad_key = own_terms[:, :model_width]
    grad_value = own_terms[:, model_width:]
    grad_projected_low = (
        jnp.concatenate([grad_gating, grad_value, grad_query, grad_key], axis=1)
        * silu_slope(projected)
    ).astype(jnp.bfloat16)
    grad_uvqk = jnp.dot(scaled_low.T, grad_projected_low, preferred_element_type=jnp.float32)
    grad_scaled = jnp.dot(grad_projected_low, uvqk_weight.T, preferred_element_type=jnp.float32)
    grad_norm_gain = jnp.sum(grad_scaled * normed, axis=0)
    grad_input = (
        cotangent.astype(jnp.float32) + norm_backward(grad_scaled * norm_gain, normed, inv_in)
    ).astype(jnp.bfloat16)
    grad_bias = jnp.dot(distance_grad, onehot, precision=lax.Precision.HIGHEST)
    summed = lax.psum(
        (grad_uvqk, grad_out_weight, grad_bias, grad_norm_gain, grad_out_gain), ("seq", "batch")
    )
    factor = 1.0 / math.sqrt(lax.axis_size("batch") * history_len)
    return (
        output[None],
        grad_input[None],
        summed[0] * factor,
        summed[1] * factor,
        summed[2] * factor,
        summed[3] * factor,
        summed[4] * factor,
    )


def solution(mesh):
    return jax.shard_map(
        shards,
        mesh=mesh,
        in_specs=(
            P("batch", "seq", None),
            P("batch", "seq", None),
            P("batch"),
            P(),
            P(),
            P(),
            P(),
            P(),
            P(),
        ),
        out_specs=(P("batch", "seq", None), P("batch", "seq", None), P(), P(), P(), P(), P()),
        check_vma=False,
    )
```

profile of v0, /device:TPU:1, one launch (start us, length us, event | category | flops | bytes accessed | tf_op | source)
XLA Modules:
  0.0 623.4 jit_solution(17857113924569547384)
XLA Ops:
  7.2 1.1 convert_reduce_fusion
  8.4 1.1 fusion.25
  12.5 215.5 %gather_fusion = f32[65536,4]{1,0:T(8,128)} fusion(f32[4,512]{0,1:T(8,128)S(1)} %copy.32, s32[65536]{0:T(1024)S(1)} %broadcast_clamp_fusion), kind=kCustom, calls=%fused_computation.clone | custom fusion | bytes 2359296 | tf_op jit(solution)/shard_map/jit(_take)/gather | solution.py:70
  228.0 20.3 %copy.44 = f32[128,512,4]{1,0,2:T(8,128)} copy(f32[128,512,4]{2,1,0:T(8,128)} %bitcast.116) | data formatting | bytes 2097152 | tf_op jit(solution)/shard_map/jit(_take)/gather | solution.py:70
  248.3 1.8 fusion.49
  250.3 12.3 %all_gather.9 = bf16[512,512]{1,0:T(8,128)(2,1)S(1)} all-gather(bf16[128,512]{1,0:T(8,128)(2,1)S(1)} %get-tuple-element.27), channel_id=1, replica_groups=mesh['seq'=4,'batch'=64] {'seq'}, dimensions={0}, use_global_device_ids=true | all-gather | bytes 655360 | tf_op jit(solution)/shard_map/all_gather | solution.py:101
  262.9 10.7 %all_gather.8 = bf16[512,512]{1,0:T(8,128)(2,1)S(1)} all-gather(bf16[128,512]{1,0:T(8,128)(2,1)S(1)} %get-tuple-element.26), channel_id=1, replica_groups=mesh['seq'=4,'batch'=64] {'seq'}, dimensions={0}, use_global_device_ids=true | all-gather | bytes 655360 | tf_op jit(solution)/shard_map/all_gather | solution.py:102
  273.5 3.0 select_convert_fusion
  277.8 2.6 multiply_reduce_fusion
  282.0 1.4 fusion.54
  283.4 1.3 copy.47
  284.7 2.1 fusion
  286.8 1.3 convolution_multiply_fusion
  288.0 2.6 copy.46
  290.6 3.1 pad_maximum_fusion
  293.8 2.1 convolution_multiply_fusion.3
  295.8 1.8 copy.48
  297.6 1.3 fusion.38
  298.9 34.4 %reduce-scatter.2.cloned.1.call-done = f32[128,1024]{1,0:T(8,128)} async-done(((f32[512,1024]{1,0:T(8,128)}), f32[128,1024]{1,0:T(8,128)}) %reduce-scatter.2.cloned.1.call-update) | async-done | bytes 524304 | tf_op jit(solution)/shard_map/reduce_scatter | solution.py:164
  333.3 1.1 fusion.51
  334.4 1.8 fusion.4
  336.9 2.8 fusion.45
  339.8 6.0 rev.3
  345.8 1.3 pad_bitcast_fusion
  347.9 1.1 slice.43
  349.1 2.9 reshape.147
  352.6 2.0 fusion.3
  355.6 2.0 fusion.24
  357.6 77.0 %all-reduce.1 = (f32[4,128]{1,0:T(4,128)S(1)}, f32[512]{0:T(512)S(1)}, f32[512]{0:T(512)S(1)}) all-reduce(f32[4,128]{1,0:T(4,128)S(1)} %fusion.33, f32[512]{0:T(512)S(1)} %get-tuple-element.8, f32[512]{0:T(512)S(1)} %copy-done.16), channel_id=1, replica_groups=mesh['seq'=4,'batch'=64] {'seq','batch'}, use_global_device_ids=true, to_apply=%region_12.14 | all-reduce | flops 1536 | bytes 12288 | tf_op jit(solution)/shard_map/psum | solution.py:178
  437.1 173.4 %all-reduce.5.cloned.1.call-done = (f32[512,2048]{1,0:T(8,128)}, f32[512,512]{1,0:T(8,128)}) async-done(((f32[512,2048]{1,0:T(8,128)}, f32[512,512]{1,0:T(8,128)}), (f32[512,2048]{1,0:T(8,128)}, f32[512,512]{1,0:T(8,128)})) %all-reduce.5.cloned.1.call-update) | async-done | bytes 5242896 | tf_op jit(solution)/shard_map/psum | solution.py:178
  610.5 5.0 broadcast_multiply_fusion
  615.5 1.1 broadcast_multiply_fusion.1
  (74 shorter events, 11.3 us)
Async XLA Ops:
  7.2 241.1 %copy-start = (bf16[512,2048]{1,0:T(8,128)(2,1)S(1)}, bf16[512,2048]{1,0:T(8,128)(2,1)}, u32[]{:S(2)}) copy-start(bf16[512,2048]{1,0:T(8,128)(2,1)} %param.17) | copy-start | bytes 6291460
  7.2 326.1 %reduce-scatter.2.cloned.1.call-start = ((), (), s32[]{:S(2)}) async-start(), calls=%async_computation.1 | async-start | bytes 2621440 | tf_op jit(solution)/shard_map/reduce_scatter | solution.py:164
  8.4 327.7 %copy-start.14 = (f32[128]{0:T(128)}, f32[128]{0:T(128)S(1)}, u32[]{:S(2)}) copy-start(f32[128]{0:T(128)S(1)} %broadcast_multiply_fusion.11) | copy-start | bytes 1540
  9.5 326.6 %copy-start.17 = (f32[128]{0:T(128)}, f32[128]{0:T(128)S(1)}, u32[]{:S(2)}) copy-start(f32[128]{0:T(128)S(1)} %add_rsqrt_fusion.1) | copy-start | bytes 1540
  228.0 20.3 %copy-start.2 = (bf16[1,128,512]{2,1,0:T(8,128)(2,1)S(1)}, bf16[1,128,512]{2,1,0:T(8,128)(2,1)}, u32[]{:S(2)}) copy-start(bf16[1,128,512]{2,1,0:T(8,128)(2,1)} %param.11) | copy-start | bytes 393220
  228.0 20.3 %copy-start.13 = (f32[512]{0:T(512)S(1)}, f32[512]{0:T(512)}, u32[]{:S(2)}) copy-start(f32[512]{0:T(512)} %param.16) | copy-start | bytes 6148
  250.3 23.2 %copy-start.11 = (bf16[128,512]{0,1:T(8,128)(2,1)}, bf16[128,512]{0,1:T(8,128)(2,1)S(1)}, u32[]{:S(2)}) copy-start(bf16[128,512]{0,1:T(8,128)(2,1)S(1)} %copy.49) | copy-start | bytes 393220
  262.9 13.7 %copy-start.4 = (bf16[512,512]{0,1:T(8,128)(2,1)}, bf16[512,512]{0,1:T(8,128)(2,1)S(1)}, u32[]{:S(2)}) copy-start(bf16[512,512]{0,1:T(8,128)(2,1)S(1)} %copy.50) | copy-start | bytes 1572868
  273.5 3.0 copy-start.3
  276.5 1.0 copy-start.5
  276.6 1.2 copy-start.6
  276.6 1.2 copy-start.7
  280.4 17.2 %copy-start.9 = (bf16[128,512]{1,0:T(8,128)(2,1)}, bf16[128,512]{1,0:T(8,128)(2,1)S(1)}, u32[]{:S(2)}) copy-start(bf16[128,512]{1,0:T(8,128)(2,1)S(1)} %get-tuple-element.22) | copy-start | bytes 393220
  284.7 2.1 copy-start.12
  293.7 316.8 %all-reduce.5.cloned.1.call-start = ((), (), s32[]{:S(2)}) async-start(), calls=%async_computation.2 | async-start | bytes 10485760 | tf_op jit(solution)/shard_map/psum | solution.py:178
  336.1 0.8 copy-start.1
  352.1 5.5 copy-start.16
  352.1 84.2 %copy-start.8 = (bf16[1,128,512]{2,1,0:T(8,128)(2,1)S(1)}, bf16[1,128,512]{2,1,0:T(8,128)(2,1)}, u32[]{:S(2)}) copy-start(bf16[1,128,512]{2,1,0:T(8,128)(2,1)} %param.12) | copy-start | bytes 393220
  352.1 84.2 %copy-start.15 = (f32[128]{0:T(128)S(1)}, f32[128]{0:T(128)}, u32[]{:S(2)}) copy-start(f32[128]{0:T(128)} %copy-done.14) | copy-start | bytes 1540
  352.1 84.2 %copy-start.18 = (f32[128]{0:T(128)S(1)}, f32[128]{0:T(128)}, u32[]{:S(2)}) copy-start(f32[128]{0:T(128)} %copy-done.17) | copy-start | bytes 1540
  610.5 5.0 copy-start.10
Sparse Core Ops, SparseCore 0:
  293.8 39.4 reduce-scatter.1
  340.3 270.1 all-reduce.4
where the time goes:
time: 625 us; the launch traced here: 623 us
  local copies, waits for them, and re-layouts  258 us (41%)
  waiting for transfers between devices  208 us (33%)
  blocking collectives  100 us (16%)
  matrix products  24.7 us (4%)
  other arithmetic  18.3 us (3%)
  between operations  15 us (2%)
    gather x2, local copies, waits for them, and re-layouts, bias_tile(): jnp.take(bias_by_distance, jnp.clip(distance, 0, history_len - 1), axis=1)  236 us
    psum x1, waiting for transfers between devices, shards(): lax.psum((grad_uvqk, grad_out_weight, grad_bias, grad_norm_gain, grad_out...  173 us
    psum x1, blocking collectives, shards(): lax.psum((grad_uvqk, grad_out_weight, grad_bias, grad_norm_gain, grad_out...  77 us
    reduce_scatter x1, waiting for transfers between devices, shards(): lax.psum_scatter(back_result[2], 'seq', scatter_dimension=0, tiled=True)  34.4 us
  transfers between devices with their start and end apart: 2, of which 2 were waited for; matrix products, arithmetic and copies ran while one was open for 4% of the time, Pallas kernels for 0%

commit v1 on v0

v1 whole, which is shorter than its diff:
```python
import functools
import math

import jax
import jax.numpy as jnp
from jax import lax
from jax.experimental import pallas as pl
from jax.experimental.pallas import tpu as pltpu
from jax.sharding import PartitionSpec as P

NORM_EPS = 1e-05
BF = jnp.bfloat16
F32 = jnp.float32
VMEM_LIMIT = 56 * 1024 * 1024
HIDDEN = -1e9


def normalize(values):
    centered = values - jnp.mean(values, axis=-1, keepdims=True)
    inv_scale = lax.rsqrt(jnp.mean(centered * centered, axis=-1, keepdims=True) + NORM_EPS)
    return (centered * inv_scale, inv_scale)


def norm_backward(grad_normed, normed, inv_scale):
    return inv_scale * (
        grad_normed
        - jnp.mean(grad_normed, axis=-1, keepdims=True)
        - normed * jnp.mean(grad_normed * normed, axis=-1, keepdims=True)
    )


def sigmoid(values):
    return 0.5 * jnp.tanh(0.5 * values) + 0.5


def dot_nn(left, right):
    return lax.dot_general(left, right, (((1,), (0,)), ((), ())), preferred_element_type=F32)


def dot_nt(left, right):
    return lax.dot_general(left, right, (((1,), (1,)), ((), ())), preferred_element_type=F32)


def dot_tn(left, right):
    return lax.dot_general(left, right, (((0,), (0,)), ((), ())), preferred_element_type=F32)


def three_parts(values):
    high = values.astype(BF)
    rest = values - high.astype(F32)
    middle = rest.astype(BF)
    low = (rest - middle.astype(F32)).astype(BF)
    return high, middle, low


def as_rows(row, parts):
    width = row.shape[1] // parts
    return jnp.concatenate([row[:, p * width : (p + 1) * width] for p in range(parts)], axis=0)


def layer_kernel(
    seq_size,
    length_ref,
    own_ref,
    own_cot_ref,
    *refs,
):
    pieces = refs[: seq_size - 1]
    (
        bucket_ref,
        bias_ref,
        in_gain_ref,
        uvqk_ref,
        out_gain_ref,
        out_w_ref,
        output_ref,
        grad_input_ref,
        send_ref,
        keep_ref,
        hist_s,
        cot_s,
        scaled_s,
        gate_s,
        slope_s,
        vqk_s,
        tile_s,
        gated_s,
        weights_s,
        grads_s,
        score_slope_s,
        grad_mixed_s,
        proj_grad_s,
        diag_s,
    ) = refs[seq_size - 1 :]
    rows, width = own_ref.shape
    total = rows * seq_size
    heads, buckets = bias_ref.shape
    head_dim = width // heads
    scale = 1.0 / math.sqrt(head_dim)
    me = lax.axis_index("seq")
    core = lax.rem(lax.axis_index("batch"), 2)
    length = length_ref[0]
    own_rows = pl.ds(pl.multiple_of(me * rows, rows), rows)

    hist_s[own_rows, :] = own_ref[...]
    cot_s[own_rows, :] = own_cot_ref[...]
    for step, piece in zip((1, 3, 2), pieces):
        source = lax.rem(me + seq_size - step, seq_size)
        place = pl.ds(pl.multiple_of(source * rows, rows), rows)
        hist_s[place, :] = piece[:, :width]
        cot_s[place, :] = piece[:, width:]

    span = total + rows
    offset = total - rows
    turned = offset - lax.broadcasted_iota(jnp.int32, (total, span), 1)
    turned = jnp.where(turned < 0, turned + span, turned)
    pick = (lax.broadcasted_iota(jnp.int32, (total, span), 0) == turned).astype(F32).astype(BF)
    bucket_rows = jnp.broadcast_to(bucket_ref[...].astype(F32), (8, total)).astype(BF)
    bucket_row = dot_nn(bucket_rows, pick)[:1, :]
    column = offset - lax.broadcasted_iota(jnp.int32, (1, span), 1)
    seen = jnp.where(column < 0, column + span, column) < total
    bucket_row = jnp.where(seen, bucket_row, -1.0)
    onehot = (
        lax.broadcasted_iota(jnp.int32, (buckets, span), 0).astype(F32)
        == jnp.broadcast_to(bucket_row, (buckets, span))
    ).astype(F32).astype(BF)
    bias_rows = jnp.concatenate([bias_ref[...], jnp.zeros((8 - heads, buckets), F32)], axis=0)
    by_distance = sum(dot_nn(part, onehot) for part in three_parts(bias_rows))
    by_distance = jnp.where(seen, by_distance, HIDDEN)
    for h in range(heads):
        skewed = pltpu.roll(
            jnp.broadcast_to(by_distance[h : h + 1, :], (rows, span)), 0, 1, stride=1, stride_axis=0
        )
        tile_s[h] = skewed[:, :total]
        diag_s[h] = jnp.zeros((rows, total), F32)

    in_gain = in_gain_ref[...]
    out_gain = out_gain_ref[...]
    grad_out_gain = jnp.zeros((1, width), F32)

    for i in range(seq_size):
        here = slice(i * rows, (i + 1) * rows)
        ends = (i + 1) * rows
        first = total - ends
        normed, _ = normalize(hist_s[here, :].astype(F32))
        scaled = (normed * in_gain).astype(BF)
        scaled_s[here, :] = scaled
        for part in range(4):
            projected = dot_nn(scaled, uvqk_ref[:, part * width : (part + 1) * width])
            sig = sigmoid(projected)
            activated = projected * sig
            slope_s[part, here, :] = sig + activated * (1.0 - sig)
            if part == 0:
                gate_s[here, :] = activated
            else:
                vqk_s[part - 1, here, :] = activated.astype(BF)
        mixed_parts = []
        for h in range(heads):
            lanes = slice(h * head_dim, (h + 1) * head_dim)
            scores = dot_nt(vqk_s[1, here, lanes], vqk_s[2, :ends, lanes]) * scale
            scores = scores + tile_s[h, :, first:]
            sig = sigmoid(scores)
            weights = scores * sig
            score_slope_s[h, :, :ends] = sig + weights * (1.0 - sig)
            weights_low = weights.astype(BF)
            weights_s[h, here, :ends] = weights_low
            mixed_parts.append(dot_nn(weights_low, vqk_s[0, :ends, lanes]))
        valid = (lax.broadcasted_iota(jnp.int32, (rows, 1), 0) + i * rows) < length
        mixed = jnp.where(valid, jnp.concatenate(mixed_parts, axis=1), 0.0)
        mixed_normed, inv_mixed = normalize(mixed)
        gating = gate_s[here, :]
        gated_s[here, :] = (mixed_normed * out_gain * gating).astype(BF)
        grad_gated = dot_nt(cot_s[here, :], out_w_ref[...])
        times_normed = grad_gated * mixed_normed
        grad_out_gain = grad_out_gain + jnp.sum(times_normed * gating, axis=0, keepdims=True)
        proj_grad_s[0, here, :] = (times_normed * out_gain * slope_s[0, here, :]).astype(BF)
        grad_mixed = norm_backward(grad_gated * out_gain * gating, mixed_normed, inv_mixed)
        grad_mixed_low = jnp.where(valid, grad_mixed, 0.0).astype(BF)
        grad_mixed_s[here, :] = grad_mixed_low
        for h in range(heads):
            lanes = slice(h * head_dim, (h + 1) * head_dim)
            grad_weights = dot_nt(grad_mixed_low[:, lanes], vqk_s[0, :ends, lanes])
            grad_scores = grad_weights * score_slope_s[h, :, :ends]
            diag_s[h, :, first:] += grad_scores
            grad_scores_low = grad_scores.astype(BF)
            grads_s[h, here, :ends] = grad_scores_low
            grad_query = dot_nn(grad_scores_low, vqk_s[2, :ends, lanes]) * scale
            proj_grad_s[2, here, lanes] = (grad_query * slope_s[2, here, lanes]).astype(BF)

    for j in range(seq_size):
        here = slice(j * rows, (j + 1) * rows)
        later = slice(j * rows, total)
        for h in range(heads):
            lanes = slice(h * head_dim, (h + 1) * head_dim)
            grad_key = dot_tn(grads_s[h, later, here], vqk_s[1, later, lanes]) * scale
            proj_grad_s[3, here, lanes] = (grad_key * slope_s[3, here, lanes]).astype(BF)
            grad_value = dot_tn(weights_s[h, later, here], grad_mixed_s[later, lanes])
            proj_grad_s[1, here, lanes] = (grad_value * slope_s[1, here, lanes]).astype(BF)

    half = total // 2
    block = width // 4
    own_block = proj_grad_s[me]
    cot_block = cot_s[:, pl.ds(pl.multiple_of(me * block, block), block)]
    for ref, side in ((send_ref, 1 - core), (keep_ref, core)):
        lanes = pl.ds(pl.multiple_of(side * half, half), half)
        uvqk_term = dot_tn(scaled_s[:, lanes], own_block)
        for b in range(4):
            ref[b * half : (b + 1) * half, :] = uvqk_term[:, b * block : (b + 1) * block].astype(
                ref.dtype
            )
        out_term = dot_tn(gated_s[:, lanes], cot_block)
        ref[4 * half : 5 * half, :] = out_term.astype(ref.dtype)

    normed, inv_in = normalize(hist_s[own_rows, :].astype(F32))
    grad_scaled = jnp.zeros((rows, width), F32)
    for part in range(4):
        grad_scaled = grad_scaled + dot_nt(
            proj_grad_s[part, own_rows, :], uvqk_ref[:, part * width : (part + 1) * width]
        )
    grad_in_gain = jnp.sum(grad_scaled * normed, axis=0, keepdims=True)
    grad_input = cot_s[own_rows, :].astype(F32) + norm_backward(
        grad_scaled * in_gain, normed, inv_in
    )
    grad_input_ref[...] = grad_input.astype(BF)
    output = hist_s[own_rows, :].astype(F32) + dot_nn(gated_s[own_rows, :], out_w_ref[...])
    output_ref[...] = output.astype(BF)

    bias_sums = []
    for h in range(heads):
        folded = jnp.concatenate([diag_s[h], jnp.zeros((rows, span - total), F32)], axis=1)
        count = rows // 2
        while count >= 8:
            folded = folded[:count, :] + pltpu.roll(folded[count:, :], span - count, 1)
            count //= 2
        while count >= 1:
            folded = folded + pltpu.roll(pltpu.roll(folded, 8 - count, 0), span - count, 1)
            count //= 2
        bias_sums.append(folded[:1, :])
    bias_sums = jnp.concatenate(bias_sums + [jnp.zeros((8 - heads, span), F32)], axis=0)
    grad_bias = sum(dot_nt(part, onehot) for part in three_parts(bias_sums))[:heads, :]
    small = jnp.concatenate(
        [
            grad_bias,
            as_rows(grad_in_gain, 4),
            as_rows(grad_out_gain, 4),
            jnp.zeros((4, buckets), F32),
        ],
        axis=0,
    )
    row = lax.broadcasted_iota(jnp.int32, small.shape, 0)
    mine = (row == me) | ((row >= 4) & (row < 8)) | (row == 8 + me)
    small = jnp.where(mine, small, 0.0)
    send_ref[5 * half :, :] = small.astype(BF)
    keep_ref[5 * half :, :] = small


def after_core_kernel(keep_ref, got_ref, own_ref, one_ref, three_ref, two_ref):
    body = keep_ref.shape[0] - 16
    half = body // 5
    part = half // 4
    y = lax.axis_index("batch") // (lax.axis_size("batch") // 4)
    small = keep_ref[body:, :].astype(BF).astype(F32) + got_ref[body:, :].astype(F32)
    for ref, step in ((own_ref, 0), (one_ref, 1), (three_ref, 3), (two_ref, 2)):
        there = lax.rem(y + step, 4)
        for b in range(5):
            place = pl.ds(pl.multiple_of(b * half + there * part, part), part)
            ref[b * part : (b + 1) * part, :] = (
                keep_ref[place, :] + got_ref[place, :].astype(F32)
            ).astype(ref.dtype)
        ref[5 * part :, :] = small.astype(ref.dtype)


def after_y_kernel(own_ref, one_ref, three_ref, two_ref, sum_ref):
    body = own_ref.shape[0] - 16
    got = lambda ref, place: ref[place, :].astype(F32)
    for place, own in (
        (slice(0, body), own_ref[:body, :]),
        (slice(body, None), own_ref[body:, :].astype(BF).astype(F32)),
    ):
        sum_ref[place, :] = (
            (own + got(two_ref, place)) + (got(one_ref, place) + got(three_ref, place))
        ).astype(BF)


def pair_sum_kernel(left_ref, right_ref, sum_ref):
    sum_ref[...] = (left_ref[...].astype(F32) + right_ref[...].astype(F32)).astype(BF)


def ring_sum_kernel(own_ref, two_ref, six_ref, four_ref, sum_ref):
    sum_ref[...] = (
        (own_ref[...].astype(F32) + four_ref[...].astype(F32))
        + (two_ref[...].astype(F32) + six_ref[...].astype(F32))
    ).astype(BF)


def after_x_kernel(
    factor, own_ref, one_ref, three_ref, two_ref, all_ref, bias_ref, in_gain_ref, out_gain_ref
):
    body = own_ref.shape[0] - 16
    me = lax.axis_index("seq")
    for ref, step in ((own_ref, 0), (one_ref, 1), (three_ref, 3), (two_ref, 2)):
        source = lax.rem(me + 4 - step, 4)
        all_ref[pl.ds(pl.multiple_of(source * body, body), body), :] = ref[:body, :]
    small = lambda ref: ref[body:, :].astype(F32)
    summed = ((small(own_ref) + small(two_ref)) + (small(one_ref) + small(three_ref))) * factor
    bias_ref[...] = summed[:4, :]
    in_gain_ref[...] = summed[4:8, :]
    out_gain_ref[...] = summed[8:12, :]


def unpack_kernel(factor, *refs):
    uvqk_ref, out_ref = refs[8:]
    part = refs[0].shape[0] // 20
    width = uvqk_ref.shape[1] // 4
    block = width // 4
    batch = lax.axis_index("batch")
    core = lax.rem(batch, 2)
    y = batch // (lax.axis_size("batch") // 4)
    for side in range(2):
        at_core = core if side == 0 else 1 - core
        for number, step in enumerate((0, 1, 3, 2)):
            ref = refs[side * 4 + number]
            from_y = lax.rem(y + 4 - step, 4)
            place = pl.ds(pl.multiple_of((at_core * 4 + from_y) * part, part), part)
            for s in range(4):
                for b in range(5):
                    start = (s * 5 + b) * part
                    values = ref[start : start + part, :].astype(F32) * factor
                    if b < 4:
                        uvqk_ref[
                            place, s * width + b * block : s * width + (b + 1) * block
                        ] = values
                    else:
                        out_ref[place, s * block : (s + 1) * block] = values


PARAMS = pltpu.CompilerParams(vmem_limit_bytes=VMEM_LIMIT)


def shards(
    history,
    out_cotangent,
    lengths,
    bucket_of,
    position_bias,
    norm_gain,
    uvqk_weight,
    out_gain,
    out_weight,
):
    rows, width = history.shape[1:]
    heads, buckets = position_bias.shape
    seq_size = lax.axis_size("seq")
    batch_size = lax.axis_size("batch")
    total = rows * seq_size
    z_size = batch_size // 8
    factor = 1.0 / math.sqrt(batch_size * total)

    def along_x(values, step):
        return lax.ppermute(values, "seq", [(i, (i + step) % seq_size) for i in range(seq_size)])

    def along_batch(values, move):
        pairs = []
        for b in range(batch_size):
            y, z, c = b // (2 * z_size), (b // 2) % z_size, b % 2
            y, z, c = move(y, z, c)
            pairs.append((b, (y * z_size + z) * 2 + c))
        return lax.ppermute(values, "batch", pairs)

    def along_y(values, step):
        return along_batch(values, lambda y, z, c: ((y + step) % 4, z, c))

    def along_z(values, step):
        return along_batch(values, lambda y, z, c: (y, (z + step) % z_size, c))

    packed = jnp.concatenate([history[0], out_cotangent[0]], axis=1)
    pieces = [along_x(packed, step) for step in (1, 3, 2)]

    half = total // 2
    body = 5 * half
    shape = jax.ShapeDtypeStruct
    vmem = pl.BlockSpec(memory_space=pltpu.VMEM)
    smem = pl.BlockSpec(memory_space=pltpu.SMEM)
    output, grad_input, send, keep = pl.pallas_call(
        functools.partial(layer_kernel, seq_size),
        out_shape=[
            shape((rows, width), BF),
            shape((rows, width), BF),
            shape((body + 16, buckets), BF),
            shape((body + 16, buckets), F32),
        ],
        in_specs=[smem] + [vmem] * (seq_size + 7),
        out_specs=[vmem] * 4,
        scratch_shapes=[
            pltpu.VMEM((total, width), BF),
            pltpu.VMEM((total, width), BF),
            pltpu.VMEM((total, width), BF),
            pltpu.VMEM((total, width), F32),
            pltpu.VMEM((4, total, width), F32),
            pltpu.VMEM((3, total, width), BF),
            pltpu.VMEM((heads, rows, total), F32),
            pltpu.VMEM((total, width), BF),
            pltpu.VMEM((heads, total, total), BF),
            pltpu.VMEM((heads, total, total), BF),
            pltpu.VMEM((heads, rows, total), F32),
            pltpu.VMEM((total, width), BF),
            pltpu.VMEM((4, total, width), BF),
            pltpu.VMEM((heads, rows, total), F32),
        ],
        compiler_params=PARAMS,
        name="layer",
    )(
        lengths,
        history[0],
        out_cotangent[0],
        *pieces,
        bucket_of.reshape(1, total),
        position_bias,
        norm_gain.reshape(1, width),
        uvqk_weight,
        out_gain.reshape(1, width),
        out_weight,
    )

    got = along_batch(send, lambda y, z, c: (y, z, 1 - c))
    part = half // 4
    chunk = (5 * part + 16, buckets)
    own, *parts = pl.pallas_call(
        after_core_kernel,
        out_shape=[shape(chunk, F32)] + [shape(chunk, BF)] * 3,
        compiler_params=PARAMS,
        name="after_core",
    )(keep, got)
    parts = [along_y(values, step) for values, step in zip(parts, (1, 3, 2))]
    summed = pl.pallas_call(
        after_y_kernel, out_shape=shape(chunk, BF), compiler_params=PARAMS, name="after_y"
    )(own, *parts)
    other = along_batch(summed, lambda y, z, c: (y, z ^ 1, c))
    summed = pl.pallas_call(
        pair_sum_kernel, out_shape=shape(chunk, BF), compiler_params=PARAMS, name="pair_sum"
    )(summed, other)
    ring = [along_z(summed, step) for step in (2, 6, 4)]
    summed = pl.pallas_call(
        ring_sum_kernel, out_shape=shape(chunk, BF), compiler_params=PARAMS, name="ring_sum"
    )(summed, *ring)
    blocks = [along_x(summed, step) for step in (1, 3, 2)]
    gathered, grad_bias, grad_in_gain, grad_out_gain = pl.pallas_call(
        functools.partial(after_x_kernel, factor),
        out_shape=[shape((20 * part, buckets), BF)] + [shape((4, buckets), F32)] * 3,
        compiler_params=PARAMS,
        name="after_x",
    )(summed, *blocks)
    columns = [gathered] + [along_y(gathered, step) for step in (1, 3, 2)]
    others = [along_batch(values, lambda y, z, c: (y, z, 1 - c)) for values in columns]
    grad_uvqk, grad_out_weight = pl.pallas_call(
        functools.partial(unpack_kernel, factor),
        out_shape=[shape((width, 4 * width), F32), shape((width, width), F32)],
        compiler_params=PARAMS,
        name="unpack",
    )(*columns, *others)
    return (
        output[None],
        grad_input[None],
        grad_uvqk,
        grad_out_weight,
        grad_bias,
        grad_in_gain.reshape(width),
        grad_out_gain.reshape(width),
    )


def solution(mesh):
    return jax.shard_map(
        shards,
        mesh=mesh,
        in_specs=(
            P("batch", "seq", None),
            P("batch", "seq", None),
            P("batch"),
            P(),
            P(),
            P(),
            P(),
            P(),
            P(),
        ),
        out_specs=(P("batch", "seq", None), P("batch", "seq", None), P(), P(), P(), P(), P()),
        check_vma=False,
    )
```

time: 625 us -> 108 us (0.17)
  local copies, waits for them, and re-layouts: 258 us -> 5.35 us
  waiting for transfers between devices: 208 us -> 28.7 us
  blocking collectives: 100 us -> 0 us
  starting transfers between devices: 0.08 us -> 44.1 us
  Pallas kernels: 0 us -> 26.9 us
  matrix products: 24.7 us -> 0 us
  other arithmetic: 18.3 us -> 0.99 us
  between operations: 15 us -> 1.38 us
    gather x2 -> x0, local copies, waits for them, and re-layouts: 236 us -> none  [bias_tile(): jnp.take(bias_by_distance, jnp.clip(distance, 0, history_len - 1), axis=1)]
    psum x1 -> x0, waiting for transfers between devices: 173 us -> none  [shards(): lax.psum((grad_uvqk, grad_out_weight, grad_bias, grad_norm_gain, grad_out...]
    psum x1 -> x0, blocking collectives: 77 us -> none  [shards(): lax.psum((grad_uvqk, grad_out_weight, grad_bias, grad_norm_gain, grad_out...]
    ppermute x0 -> x21, starting transfers between devices: none -> 44.1 us  [the longest x15 35 us: along_batch(): return lax.ppermute(values, 'batch', pairs)]
    reduce_scatter x1 -> x0, waiting for transfers between devices: 34.4 us -> none  [shards(): lax.psum_scatter(back_result[2], 'seq', scatter_dimension=0, tiled=True)]
    ppermute x0 -> x21, waiting for transfers between devices: none -> 28.7 us  [the longest x6 15.1 us: along_x(): lax.ppermute(values, 'seq', [(i, (i + step) % seq_size) for i in range(se...]
    pallas_call x0 -> x7, Pallas kernels: none -> 26.9 us  [the longest x1 13.6 us: shards(): pl.pallas_call(functools.partial(layer_kernel, seq_size), out_shape=[shap...]
    dot_general x14 -> x0, matrix products: 24.7 us -> none  [the longest x1 3 us: tile_scores(): jnp.einsum('ihd,jhd->hij', query_block, key_block, preferred_element_type...]
  transfers between devices with their start and end apart: 2 -> 21, of which waited for: 2 -> 14; matrix products, arithmetic and copies ran while one was open for 4% -> 0% of each run, Pallas kernels for 0% -> 0%
where the time goes in v1:
time: 108 us; the launch traced here: 107 us
  starting transfers between devices  44.1 us (41%)
  waiting for transfers between devices  28.7 us (27%)
  Pallas kernels  26.9 us (25%)
  local copies, waits for them, and re-layouts  5.35 us (5%)
  between operations  1.38 us (1%)
    ppermute x15, starting transfers between devices, along_batch(): return lax.ppermute(values, 'batch', pairs)  35 us
    ppermute x6, waiting for transfers between devices, along_x(): lax.ppermute(values, 'seq', [(i, (i + step) % seq_size) for i in range(se...  15.1 us
    pallas_call x1, Pallas kernels, shards(): pl.pallas_call(functools.partial(layer_kernel, seq_size), out_shape=[shap...  13.6 us
    ppermute x15, waiting for transfers between devices, along_batch(): return lax.ppermute(values, 'batch', pairs)  13.5 us
    ppermute x6, starting transfers between devices, along_x(): lax.ppermute(values, 'seq', [(i, (i + step) % seq_size) for i in range(se...  9.12 us
    unnamed x42, local copies, waits for them, and re-layouts  5.35 us
    pallas_call x1, Pallas kernels, shards(): pl.pallas_call(functools.partial(unpack_kernel, factor), out_shape=[shape...  4.51 us
  transfers between devices with their start and end apart: 21, of which 14 were waited for; matrix products, arithmetic and copies ran while one was open for 0% of the time, Pallas kernels for 0%

profile of v1, /device:TPU:1, one launch (start us, length us, event | category | flops | bytes accessed | tf_op | source)
XLA Modules:
  0.0 107.4 jit_solution(329212883840668024)
XLA Ops:
  0.6 1.0 pad_maximum_fusion
  1.6 3.7 %collective-permute-start.2 = (bf16[128,1024]{1,0:T(8,128)(2,1)S(1)}, bf16[128,1024]{1,0:T(8,128)(2,1)S(1)}, u32[]{:S(2)}, u32[]{:S(2)}) collective-permute-start(bf16[128,1024]{1,0:T(8,128)(2,1)S(1)} %pad_maximum_fusion), channel_id=1, source_target_pairs={{0,128},{64,192},{128,0},{192,64},{1,129},{65,193},{129,1},{193,65... | collective-permute-start | bytes 786440 | tf_op jit(solution)/shard_map/ppermute | solution.py:360
  7.4 2.9 %collective-permute-done.2.refs_2_ = bf16[128,1024]{1,0:T(8,128)(2,1)S(1)} collective-permute-done((bf16[128,1024]{1,0:T(8,128)(2,1)S(1)}, bf16[128,1024]{1,0:T(8,128)(2,1)S(1)}, u32[]{:S(2)}, u32[]{:S(2)}) %collective-permute-start.2) | collective-permute-done | bytes 262176 | tf_op jit(solution)/shard_map/ppermute | solution.py:360
  10.3 6.7 %collective-permute-done.1.refs_1_ = bf16[128,1024]{1,0:T(8,128)(2,1)S(1)} collective-permute-done((bf16[128,1024]{1,0:T(8,128)(2,1)S(1)}, bf16[128,1024]{1,0:T(8,128)(2,1)S(1)}, u32[]{:S(2)}, u32[]{:S(2)}) %collective-permute-start.1) | collective-permute-done | bytes 262176 | tf_op jit(solution)/shard_map/ppermute | solution.py:360
  18.1 13.6 %layer.1 = (bf16[128,512]{1,0:T(8,128)(2,1)}, bf16[128,512]{1,0:T(8,128)(2,1)}, bf16[1296,128]{1,0:T(8,128)(2,1)}, f32[1296,128]{1,0:T(8,128)}) custom-call(s32[1]{0:T(128)S(6)} %copy.16.length_ref, bf16[128,512]{1,0:T(8,128)(2,1)} %bitcast.10, bf16[128,512]{1,0:T(8,128)(2,1)} %bitcast.12, bf16[128,1024]{1,0:T(8,128)(2,1)} %copy-done.10, ...), custom_call_target="tpu_custom_call" | custom-call | tf_op jit(solution)/shard_map/layer/pallas_call | solution.py:384
  31.7 1.3 %collective-permute-start.3 = (bf16[1296,128]{1,0:T(8,128)(2,1)}, bf16[1296,128]{1,0:T(8,128)(2,1)S(1)}, u32[]{:S(2)}, u32[]{:S(2)}) collective-permute-start(bf16[1296,128]{1,0:T(8,128)(2,1)} %get-tuple-element.24), channel_id=1, source_target_pairs={{0,1},{1,0},{2,3},{3,2},{4,5},{5,4},{6,7},{7,6},{8,9},{9,8},{10,11... | collective-permute-start | bytes 995336 | tf_op jit(solution)/shard_map/ppermute | solution.py:368
  33.1 1.5 %collective-permute-done.3.got_ref = bf16[1296,128]{1,0:T(8,128)(2,1)S(1)} collective-permute-done((bf16[1296,128]{1,0:T(8,128)(2,1)}, bf16[1296,128]{1,0:T(8,128)(2,1)S(1)}, u32[]{:S(2)}, u32[]{:S(2)}) %collective-permute-start.3) | collective-permute-done | bytes 331808 | tf_op jit(solution)/shard_map/ppermute | solution.py:368
  35.3 2.0 %after_core.1 = (f32[336,128]{1,0:T(8,128)}, bf16[336,128]{1,0:T(8,128)(2,1)}, bf16[336,128]{1,0:T(8,128)(2,1)}, bf16[336,128]{1,0:T(8,128)(2,1)}) custom-call(f32[1296,128]{1,0:T(8,128)} %get-tuple-element.23.keep_ref, bf16[1296,128]{1,0:T(8,128)(2,1)} %copy-done), custom_call_target="tpu_custom_call" | custom-call | tf_op jit(solution)/shard_map/after_core/pallas_call | solution.py:428
  37.3 1.2 %collective-permute-start.4 = (bf16[336,128]{1,0:T(8,128)(2,1)}, bf16[336,128]{1,0:T(8,128)(2,1)S(1)}, u32[]{:S(2)}, u32[]{:S(2)}) collective-permute-start(bf16[336,128]{1,0:T(8,128)(2,1)} %get-tuple-element.26), channel_id=1, source_target_pairs={{0,16},{1,17},{2,18},{3,19},{4,20},{5,21},{6,22},{7,23},{8,24},{9,... | collective-permute-start | bytes 258056 | tf_op jit(solution)/shard_map/ppermute | solution.py:368
  38.5 1.5 %collective-permute-start.5 = (bf16[336,128]{1,0:T(8,128)(2,1)}, bf16[336,128]{1,0:T(8,128)(2,1)S(1)}, u32[]{:S(2)}, u32[]{:S(2)}) collective-permute-start(bf16[336,128]{1,0:T(8,128)(2,1)} %get-tuple-element.27), channel_id=1, source_target_pairs={{0,48},{1,49},{2,50},{3,51},{4,52},{5,53},{6,54},{7,55},{8,56},{9,... | collective-permute-start | bytes 258056 | tf_op jit(solution)/shard_map/ppermute | solution.py:368
  39.9 1.6 %collective-permute-start.6 = (bf16[336,128]{1,0:T(8,128)(2,1)}, bf16[336,128]{1,0:T(8,128)(2,1)S(1)}, u32[]{:S(2)}, u32[]{:S(2)}) collective-permute-start(bf16[336,128]{1,0:T(8,128)(2,1)} %get-tuple-element.28), channel_id=1, source_target_pairs={{0,32},{1,33},{2,34},{3,35},{4,36},{5,37},{6,38},{7,39},{8,40},{9,... | collective-permute-start | bytes 258056 | tf_op jit(solution)/shard_map/ppermute | solution.py:368
  42.4 2.6 %collective-permute-done.6.two_ref = bf16[336,128]{1,0:T(8,128)(2,1)S(1)} collective-permute-done((bf16[336,128]{1,0:T(8,128)(2,1)}, bf16[336,128]{1,0:T(8,128)(2,1)S(1)}, u32[]{:S(2)}, u32[]{:S(2)}) %collective-permute-start.6) | collective-permute-done | bytes 86048 | tf_op jit(solution)/shard_map/ppermute | solution.py:368
  45.6 1.7 %after_y.1.left_ref = bf16[336,128]{1,0:T(8,128)(2,1)} custom-call(f32[336,128]{1,0:T(8,128)} %get-tuple-element.25.own_ref, bf16[336,128]{1,0:T(8,128)(2,1)} %copy-done.18, bf16[336,128]{1,0:T(8,128)(2,1)} %copy-done.19, bf16[336,128]{1,0:T(8,128)(2,1)} %copy-done.20), custom_call_target="tpu_custom_call" | custom-call | tf_op jit(solution)/shard_map/after_y/pallas_call | solution.py:435
  47.4 1.6 %collective-permute-start.7 = (bf16[336,128]{1,0:T(8,128)(2,1)}, bf16[336,128]{1,0:T(8,128)(2,1)S(1)}, u32[]{:S(2)}, u32[]{:S(2)}) collective-permute-start(bf16[336,128]{1,0:T(8,128)(2,1)} %after_y.1.left_ref), channel_id=1, source_target_pairs={{0,2},{1,3},{2,0},{3,1},{4,6},{5,7},{6,4},{7,5},{8,10},{9,11},{10,... | collective-permute-start | bytes 258056 | tf_op jit(solution)/shard_map/ppermute | solution.py:368
  49.0 2.1 %collective-permute-done.7.right_ref = bf16[336,128]{1,0:T(8,128)(2,1)S(1)} collective-permute-done((bf16[336,128]{1,0:T(8,128)(2,1)}, bf16[336,128]{1,0:T(8,128)(2,1)S(1)}, u32[]{:S(2)}, u32[]{:S(2)}) %collective-permute-start.7) | collective-permute-done | bytes 86048 | tf_op jit(solution)/shard_map/ppermute | solution.py:368
  51.7 1.6 %pair_sum.1.own_ref = bf16[336,128]{1,0:T(8,128)(2,1)} custom-call(bf16[336,128]{1,0:T(8,128)(2,1)} %after_y.1.left_ref, bf16[336,128]{1,0:T(8,128)(2,1)} %copy-done.17), custom_call_target="tpu_custom_call" | custom-call | tf_op jit(solution)/shard_map/pair_sum/pallas_call | solution.py:439
  53.3 6.7 %collective-permute-start.10 = (bf16[336,128]{1,0:T(8,128)(2,1)}, bf16[336,128]{1,0:T(8,128)(2,1)S(1)}, u32[]{:S(2)}, u32[]{:S(2)}) collective-permute-start(bf16[336,128]{1,0:T(8,128)(2,1)} %pair_sum.1.own_ref), channel_id=1, source_target_pairs={{0,8},{1,9},{2,10},{3,11},{4,12},{5,13},{6,14},{7,15},{8,0},{9,1},... | collective-permute-start | bytes 258056 | tf_op jit(solution)/shard_map/ppermute | solution.py:368
  60.0 2.4 %collective-permute-start.8 = (bf16[336,128]{1,0:T(8,128)(2,1)}, bf16[336,128]{1,0:T(8,128)(2,1)S(1)}, u32[]{:S(2)}, u32[]{:S(2)}) collective-permute-start(bf16[336,128]{1,0:T(8,128)(2,1)} %pair_sum.1.own_ref), channel_id=1, source_target_pairs={{0,4},{1,5},{2,6},{3,7},{4,8},{5,9},{6,10},{7,11},{8,12},{9,13},{1... | collective-permute-start | bytes 258056 | tf_op jit(solution)/shard_map/ppermute | solution.py:368
  62.4 5.1 %collective-permute-done.9.six_ref = bf16[336,128]{1,0:T(8,128)(2,1)S(1)} collective-permute-done((bf16[336,128]{1,0:T(8,128)(2,1)}, bf16[336,128]{1,0:T(8,128)(2,1)S(1)}, u32[]{:S(2)}, u32[]{:S(2)}) %collective-permute-start.9) | collective-permute-done | bytes 86048 | tf_op jit(solution)/shard_map/ppermute | solution.py:368
  68.7 1.7 %ring_sum.1.own_ref = bf16[336,128]{1,0:T(8,128)(2,1)} custom-call(bf16[336,128]{1,0:T(8,128)(2,1)} %pair_sum.1.own_ref, bf16[336,128]{1,0:T(8,128)(2,1)} %copy-done.16, bf16[336,128]{1,0:T(8,128)(2,1)} %copy-done.15, bf16[336,128]{1,0:T(8,128)(2,1)} %copy-done.13), custom_call_target="tpu_custom_call" | custom-call | tf_op jit(solution)/shard_map/ring_sum/pallas_call | solution.py:443
  70.4 2.5 %collective-permute-start.13 = (bf16[336,128]{1,0:T(8,128)(2,1)}, bf16[336,128]{1,0:T(8,128)(2,1)S(1)}, u32[]{:S(2)}, u32[]{:S(2)}) collective-permute-start(bf16[336,128]{1,0:T(8,128)(2,1)} %ring_sum.1.own_ref), channel_id=1, source_target_pairs={{0,128},{64,192},{128,0},{192,64},{1,129},{65,193},{129,1},{193,65... | collective-permute-start | bytes 258056 | tf_op jit(solution)/shard_map/ppermute | solution.py:360
  73.0 0.9 collective-permute-start.12
  74.4 1.1 collective-permute-done.13.two_ref
  75.5 1.0 collective-permute-done.12.three_ref
  76.5 3.1 %collective-permute-done.11.one_ref = bf16[336,128]{1,0:T(8,128)(2,1)S(1)} collective-permute-done((bf16[336,128]{1,0:T(8,128)(2,1)}, bf16[336,128]{1,0:T(8,128)(2,1)S(1)}, u32[]{:S(2)}, u32[]{:S(2)}) %collective-permute-start.11) | collective-permute-done | bytes 86048 | tf_op jit(solution)/shard_map/ppermute | solution.py:360
  80.2 1.8 %after_x.1 = (bf16[1280,128]{1,0:T(8,128)(2,1)}, f32[4,128]{1,0:T(4,128)}, f32[4,128]{1,0:T(4,128)}, f32[4,128]{1,0:T(4,128)}) custom-call(bf16[336,128]{1,0:T(8,128)(2,1)} %ring_sum.1.own_ref, bf16[336,128]{1,0:T(8,128)(2,1)} %copy-done.14, bf16[336,128]{1,0:T(8,128)(2,1)} %copy-done.12, bf16[336,128]{1,0:T(8,128)(2,1)} %copy-done.11), custom_call_target="tpu_custom_call" | custom-call | tf_op jit(solution)/shard_map/after_x/pallas_call | solution.py:447
  82.0 1.6 %collective-permute-start.16 = (bf16[1280,128]{1,0:T(8,128)(2,1)}, bf16[1280,128]{1,0:T(8,128)(2,1)S(1)}, u32[]{:S(2)}, u32[]{:S(2)}) collective-permute-start(bf16[1280,128]{1,0:T(8,128)(2,1)} %get-tuple-element.29.refs_0_), channel_id=1, source_target_pairs={{0,32},{1,33},{2,34},{3,35},{4,36},{5,37},{6,38},{7,39},{8,40},{9,... | collective-permute-start | bytes 983048 | tf_op jit(solution)/shard_map/ppermute | solution.py:368
  83.6 1.5 %collective-permute-start.15 = (bf16[1280,128]{1,0:T(8,128)(2,1)}, bf16[1280,128]{1,0:T(8,128)(2,1)S(1)}, u32[]{:S(2)}, u32[]{:S(2)}) collective-permute-start(bf16[1280,128]{1,0:T(8,128)(2,1)} %get-tuple-element.29.refs_0_), channel_id=1, source_target_pairs={{0,48},{1,49},{2,50},{3,51},{4,52},{5,53},{6,54},{7,55},{8,56},{9,... | collective-permute-start | bytes 983048 | tf_op jit(solution)/shard_map/ppermute | solution.py:368
  85.1 4.4 %collective-permute-start.17 = (bf16[1280,128]{1,0:T(8,128)(2,1)}, bf16[1280,128]{1,0:T(8,128)(2,1)S(1)}, u32[]{:S(2)}, u32[]{:S(2)}) collective-permute-start(bf16[1280,128]{1,0:T(8,128)(2,1)} %get-tuple-element.29.refs_0_), channel_id=1, source_target_pairs={{0,1},{1,0},{2,3},{3,2},{4,5},{5,4},{6,7},{7,6},{8,9},{9,8},{10,11... | collective-permute-start | bytes 983048 | tf_op jit(solution)/shard_map/ppermute | solution.py:368
  89.7 7.7 %collective-permute-start.20 = (bf16[1280,128]{1,0:T(8,128)(2,1)S(1)}, bf16[1280,128]{1,0:T(8,128)(2,1)S(1)}, u32[]{:S(2)}, u32[]{:S(2)}) collective-permute-start(bf16[1280,128]{1,0:T(8,128)(2,1)S(1)} %collective-permute-done.16.refs_3_), channel_id=1, source_target_pairs={{0,1},{1,0},{2,3},{3,2},{4,5},{5,4},{6,7},{7,6},{8,9},{9,8},{10,11... | collective-permute-start | bytes 983048 | tf_op jit(solution)/shard_map/ppermute | solution.py:368
  97.4 2.6 %collective-permute-start.19 = (bf16[1280,128]{1,0:T(8,128)(2,1)S(1)}, bf16[1280,128]{1,0:T(8,128)(2,1)S(1)}, u32[]{:S(2)}, u32[]{:S(2)}) collective-permute-start(bf16[1280,128]{1,0:T(8,128)(2,1)S(1)} %collective-permute-done.15.refs_2_), channel_id=1, source_target_pairs={{0,1},{1,0},{2,3},{3,2},{4,5},{5,4},{6,7},{7,6},{8,9},{9,8},{10,11... | collective-permute-start | bytes 983048 | tf_op jit(solution)/shard_map/ppermute | solution.py:368
  102.9 4.5 %unpack.1 = (f32[512,2048]{1,0:T(8,128)}, f32[512,512]{1,0:T(8,128)}) custom-call(bf16[1280,128]{1,0:T(8,128)(2,1)} %get-tuple-element.29.refs_0_, bf16[1280,128]{1,0:T(8,128)(2,1)} %copy-done.3, bf16[1280,128]{1,0:T(8,128)(2,1)} %copy-done.2, bf16[1280,128]{1,0:T(8,128)(2,1)} %copy-done.1, bf16[1280,128]{1,0:T(8,128)(2,1)} %copy-done.4, ...), custom_call_target="tpu_custom_call" | custom-call | tf_op jit(solution)/shard_map/unpack/pallas_call | solution.py:455
  (60 shorter events, 10.9 us)
Async XLA Ops:
  1.6 8.7 %collective-permute-start.2 = (bf16[128,1024]{1,0:T(8,128)(2,1)S(1)}, bf16[128,1024]{1,0:T(8,128)(2,1)S(1)}, u32[]{:S(2)}, u32[]{:S(2)}) collective-permute-start(bf16[128,1024]{1,0:T(8,128)(2,1)S(1)} %pad_maximum_fusion), channel_id=1, source_target_pairs={{0,128},{64,192},{128,0},{192,64},{1,129},{65,193},{129,1},{193,65... | collective-permute-start | bytes 786440 | tf_op jit(solution)/shard_map/ppermute | solution.py:360
  5.3 11.7 %collective-permute-start.1 = (bf16[128,1024]{1,0:T(8,128)(2,1)S(1)}, bf16[128,1024]{1,0:T(8,128)(2,1)S(1)}, u32[]{:S(2)}, u32[]{:S(2)}) collective-permute-start(bf16[128,1024]{1,0:T(8,128)(2,1)S(1)} %pad_maximum_fusion), channel_id=1, source_target_pairs={{0,192},{64,0},{128,64},{192,128},{1,193},{65,1},{129,65},{193,129... | collective-permute-start | bytes 786440 | tf_op jit(solution)/shard_map/ppermute | solution.py:360
  6.1 11.2 %collective-permute-start = (bf16[128,1024]{1,0:T(8,128)(2,1)S(1)}, bf16[128,1024]{1,0:T(8,128)(2,1)S(1)}, u32[]{:S(2)}, u32[]{:S(2)}) collective-permute-start(bf16[128,1024]{1,0:T(8,128)(2,1)S(1)} %pad_maximum_fusion), channel_id=1, source_target_pairs={{0,64},{64,128},{128,192},{192,0},{1,65},{65,129},{129,193},{193,1... | collective-permute-start | bytes 786440 | tf_op jit(solution)/shard_map/ppermute | solution.py:360
  10.3 7.1 %copy-start.8 = (bf16[128,1024]{1,0:T(8,128)(2,1)}, bf16[128,1024]{1,0:T(8,128)(2,1)S(1)}, u32[]{:S(2)}) copy-start(bf16[128,1024]{1,0:T(8,128)(2,1)S(1)} %collective-permute-done.2.refs_2_) | copy-start | bytes 786436
  31.7 2.8 %collective-permute-start.3 = (bf16[1296,128]{1,0:T(8,128)(2,1)}, bf16[1296,128]{1,0:T(8,128)(2,1)S(1)}, u32[]{:S(2)}, u32[]{:S(2)}) collective-permute-start(bf16[1296,128]{1,0:T(8,128)(2,1)} %get-tuple-element.24), channel_id=1, source_target_pairs={{0,1},{1,0},{2,3},{3,2},{4,5},{5,4},{6,7},{7,6},{8,9},{9,8},{10,11... | collective-permute-start | bytes 995336 | tf_op jit(solution)/shard_map/ppermute | solution.py:368
  37.3 5.2 %collective-permute-start.4 = (bf16[336,128]{1,0:T(8,128)(2,1)}, bf16[336,128]{1,0:T(8,128)(2,1)S(1)}, u32[]{:S(2)}, u32[]{:S(2)}) collective-permute-start(bf16[336,128]{1,0:T(8,128)(2,1)} %get-tuple-element.26), channel_id=1, source_target_pairs={{0,16},{1,17},{2,18},{3,19},{4,20},{5,21},{6,22},{7,23},{8,24},{9,... | collective-permute-start | bytes 258056 | tf_op jit(solution)/shard_map/ppermute | solution.py:368
  38.5 4.0 %collective-permute-start.5 = (bf16[336,128]{1,0:T(8,128)(2,1)}, bf16[336,128]{1,0:T(8,128)(2,1)S(1)}, u32[]{:S(2)}, u32[]{:S(2)}) collective-permute-start(bf16[336,128]{1,0:T(8,128)(2,1)} %get-tuple-element.27), channel_id=1, source_target_pairs={{0,48},{1,49},{2,50},{3,51},{4,52},{5,53},{6,54},{7,55},{8,56},{9,... | collective-permute-start | bytes 258056 | tf_op jit(solution)/shard_map/ppermute | solution.py:368
  39.9 5.1 %collective-permute-start.6 = (bf16[336,128]{1,0:T(8,128)(2,1)}, bf16[336,128]{1,0:T(8,128)(2,1)S(1)}, u32[]{:S(2)}, u32[]{:S(2)}) collective-permute-start(bf16[336,128]{1,0:T(8,128)(2,1)} %get-tuple-element.28), channel_id=1, source_target_pairs={{0,32},{1,33},{2,34},{3,35},{4,36},{5,37},{6,38},{7,39},{8,40},{9,... | collective-permute-start | bytes 258056 | tf_op jit(solution)/shard_map/ppermute | solution.py:368
  42.4 2.6 %copy-start.18 = (bf16[336,128]{1,0:T(8,128)(2,1)}, bf16[336,128]{1,0:T(8,128)(2,1)S(1)}, u32[]{:S(2)}) copy-start(bf16[336,128]{1,0:T(8,128)(2,1)S(1)} %collective-permute-done.4.one_ref) | copy-start | bytes 258052
  42.4 2.6 %copy-start.19 = (bf16[336,128]{1,0:T(8,128)(2,1)}, bf16[336,128]{1,0:T(8,128)(2,1)S(1)}, u32[]{:S(2)}) copy-start(bf16[336,128]{1,0:T(8,128)(2,1)S(1)} %collective-permute-done.5.three_ref) | copy-start | bytes 258052
  47.4 3.7 %collective-permute-start.7 = (bf16[336,128]{1,0:T(8,128)(2,1)}, bf16[336,128]{1,0:T(8,128)(2,1)S(1)}, u32[]{:S(2)}, u32[]{:S(2)}) collective-permute-start(bf16[336,128]{1,0:T(8,128)(2,1)} %after_y.1.left_ref), channel_id=1, source_target_pairs={{0,2},{1,3},{2,0},{3,1},{4,6},{5,7},{6,4},{7,5},{8,10},{9,11},{10,... | collective-permute-start | bytes 258056 | tf_op jit(solution)/shard_map/ppermute | solution.py:368
  53.3 9.1 %collective-permute-start.10 = (bf16[336,128]{1,0:T(8,128)(2,1)}, bf16[336,128]{1,0:T(8,128)(2,1)S(1)}, u32[]{:S(2)}, u32[]{:S(2)}) collective-permute-start(bf16[336,128]{1,0:T(8,128)(2,1)} %pair_sum.1.own_ref), channel_id=1, source_target_pairs={{0,8},{1,9},{2,10},{3,11},{4,12},{5,13},{6,14},{7,15},{8,0},{9,1},... | collective-permute-start | bytes 258056 | tf_op jit(solution)/shard_map/ppermute | solution.py:368
  60.0 7.4 %collective-permute-start.9 = (bf16[336,128]{1,0:T(8,128)(2,1)}, bf16[336,128]{1,0:T(8,128)(2,1)S(1)}, u32[]{:S(2)}, u32[]{:S(2)}) collective-permute-start(bf16[336,128]{1,0:T(8,128)(2,1)} %pair_sum.1.own_ref), channel_id=1, source_target_pairs={{0,12},{1,13},{2,14},{3,15},{4,0},{5,1},{6,2},{7,3},{8,4},{9,5},{1... | collective-permute-start | bytes 258056 | tf_op jit(solution)/shard_map/ppermute | solution.py:368
  60.0 7.4 %collective-permute-start.8 = (bf16[336,128]{1,0:T(8,128)(2,1)}, bf16[336,128]{1,0:T(8,128)(2,1)S(1)}, u32[]{:S(2)}, u32[]{:S(2)}) collective-permute-start(bf16[336,128]{1,0:T(8,128)(2,1)} %pair_sum.1.own_ref), channel_id=1, source_target_pairs={{0,4},{1,5},{2,6},{3,7},{4,8},{5,9},{6,10},{7,11},{8,12},{9,13},{1... | collective-permute-start | bytes 258056 | tf_op jit(solution)/shard_map/ppermute | solution.py:368
  62.4 5.1 %copy-start.13 = (bf16[336,128]{1,0:T(8,128)(2,1)}, bf16[336,128]{1,0:T(8,128)(2,1)S(1)}, u32[]{:S(2)}) copy-start(bf16[336,128]{1,0:T(8,128)(2,1)S(1)} %collective-permute-done.10.four_ref) | copy-start | bytes 258052
  70.4 5.1 %collective-permute-start.13 = (bf16[336,128]{1,0:T(8,128)(2,1)}, bf16[336,128]{1,0:T(8,128)(2,1)S(1)}, u32[]{:S(2)}, u32[]{:S(2)}) collective-permute-start(bf16[336,128]{1,0:T(8,128)(2,1)} %ring_sum.1.own_ref), channel_id=1, source_target_pairs={{0,128},{64,192},{128,0},{192,64},{1,129},{65,193},{129,1},{193,65... | collective-permute-start | bytes 258056 | tf_op jit(solution)/shard_map/ppermute | solution.py:360
  73.0 3.5 %collective-permute-start.12 = (bf16[336,128]{1,0:T(8,128)(2,1)}, bf16[336,128]{1,0:T(8,128)(2,1)S(1)}, u32[]{:S(2)}, u32[]{:S(2)}) collective-permute-start(bf16[336,128]{1,0:T(8,128)(2,1)} %ring_sum.1.own_ref), channel_id=1, source_target_pairs={{0,192},{64,0},{128,64},{192,128},{1,193},{65,1},{129,65},{193,129... | collective-permute-start | bytes 258056 | tf_op jit(solution)/shard_map/ppermute | solution.py:360
  73.9 5.7 %collective-permute-start.11 = (bf16[336,128]{1,0:T(8,128)(2,1)}, bf16[336,128]{1,0:T(8,128)(2,1)S(1)}, u32[]{:S(2)}, u32[]{:S(2)}) collective-permute-start(bf16[336,128]{1,0:T(8,128)(2,1)} %ring_sum.1.own_ref), channel_id=1, source_target_pairs={{0,64},{64,128},{128,192},{192,0},{1,65},{65,129},{129,193},{193,1... | collective-permute-start | bytes 258056 | tf_op jit(solution)/shard_map/ppermute | solution.py:360
  75.5 4.1 %copy-start.11 = (bf16[336,128]{1,0:T(8,128)(2,1)}, bf16[336,128]{1,0:T(8,128)(2,1)S(1)}, u32[]{:S(2)}) copy-start(bf16[336,128]{1,0:T(8,128)(2,1)S(1)} %collective-permute-done.13.two_ref) | copy-start | bytes 258052
  76.5 3.1 %copy-start.12 = (bf16[336,128]{1,0:T(8,128)(2,1)}, bf16[336,128]{1,0:T(8,128)(2,1)S(1)}, u32[]{:S(2)}) copy-start(bf16[336,128]{1,0:T(8,128)(2,1)S(1)} %collective-permute-done.12.three_ref) | copy-start | bytes 258052
  82.0 7.7 %collective-permute-start.16 = (bf16[1280,128]{1,0:T(8,128)(2,1)}, bf16[1280,128]{1,0:T(8,128)(2,1)S(1)}, u32[]{:S(2)}, u32[]{:S(2)}) collective-permute-start(bf16[1280,128]{1,0:T(8,128)(2,1)} %get-tuple-element.29.refs_0_), channel_id=1, source_target_pairs={{0,32},{1,33},{2,34},{3,35},{4,36},{5,37},{6,38},{7,39},{8,40},{9,... | collective-permute-start | bytes 983048 | tf_op jit(solution)/shard_map/ppermute | solution.py:368
  83.6 13.8 %collective-permute-start.15 = (bf16[1280,128]{1,0:T(8,128)(2,1)}, bf16[1280,128]{1,0:T(8,128)(2,1)S(1)}, u32[]{:S(2)}, u32[]{:S(2)}) collective-permute-start(bf16[1280,128]{1,0:T(8,128)(2,1)} %get-tuple-element.29.refs_0_), channel_id=1, source_target_pairs={{0,48},{1,49},{2,50},{3,51},{4,52},{5,53},{6,54},{7,55},{8,56},{9,... | collective-permute-start | bytes 983048 | tf_op jit(solution)/shard_map/ppermute | solution.py:368
  85.1 14.9 %collective-permute-start.14 = (bf16[1280,128]{1,0:T(8,128)(2,1)}, bf16[1280,128]{1,0:T(8,128)(2,1)S(1)}, u32[]{:S(2)}, u32[]{:S(2)}) collective-permute-start(bf16[1280,128]{1,0:T(8,128)(2,1)} %get-tuple-element.29.refs_0_), channel_id=1, source_target_pairs={{0,16},{1,17},{2,18},{3,19},{4,20},{5,21},{6,22},{7,23},{8,24},{9,... | collective-permute-start | bytes 983048 | tf_op jit(solution)/shard_map/ppermute | solution.py:368
  85.1 15.7 %collective-permute-start.17 = (bf16[1280,128]{1,0:T(8,128)(2,1)}, bf16[1280,128]{1,0:T(8,128)(2,1)S(1)}, u32[]{:S(2)}, u32[]{:S(2)}) collective-permute-start(bf16[1280,128]{1,0:T(8,128)(2,1)} %get-tuple-element.29.refs_0_), channel_id=1, source_target_pairs={{0,1},{1,0},{2,3},{3,2},{4,5},{5,4},{6,7},{7,6},{8,9},{9,8},{10,11... | collective-permute-start | bytes 983048 | tf_op jit(solution)/shard_map/ppermute | solution.py:368
  89.7 12.4 %copy-start.1 = (bf16[1280,128]{1,0:T(8,128)(2,1)}, bf16[1280,128]{1,0:T(8,128)(2,1)S(1)}, u32[]{:S(2)}) copy-start(bf16[1280,128]{1,0:T(8,128)(2,1)S(1)} %collective-permute-done.16.refs_3_) | copy-start | bytes 983044
  89.7 11.2 %collective-permute-start.20 = (bf16[1280,128]{1,0:T(8,128)(2,1)S(1)}, bf16[1280,128]{1,0:T(8,128)(2,1)S(1)}, u32[]{:S(2)}, u32[]{:S(2)}) collective-permute-start(bf16[1280,128]{1,0:T(8,128)(2,1)S(1)} %collective-permute-done.16.refs_3_), channel_id=1, source_target_pairs={{0,1},{1,0},{2,3},{3,2},{4,5},{5,4},{6,7},{7,6},{8,9},{9,8},{10,11... | collective-permute-start | bytes 983048 | tf_op jit(solution)/shard_map/ppermute | solution.py:368
  97.4 4.7 %copy-start.2 = (bf16[1280,128]{1,0:T(8,128)(2,1)}, bf16[1280,128]{1,0:T(8,128)(2,1)S(1)}, u32[]{:S(2)}) copy-start(bf16[1280,128]{1,0:T(8,128)(2,1)S(1)} %collective-permute-done.15.refs_2_) | copy-start | bytes 983044
  97.4 3.9 %collective-permute-start.19 = (bf16[1280,128]{1,0:T(8,128)(2,1)S(1)}, bf16[1280,128]{1,0:T(8,128)(2,1)S(1)}, u32[]{:S(2)}, u32[]{:S(2)}) collective-permute-start(bf16[1280,128]{1,0:T(8,128)(2,1)S(1)} %collective-permute-done.15.refs_2_), channel_id=1, source_target_pairs={{0,1},{1,0},{2,3},{3,2},{4,5},{5,4},{6,7},{7,6},{8,9},{9,8},{10,11... | collective-permute-start | bytes 983048 | tf_op jit(solution)/shard_map/ppermute | solution.py:368
  100.0 2.1 %copy-start.3 = (bf16[1280,128]{1,0:T(8,128)(2,1)}, bf16[1280,128]{1,0:T(8,128)(2,1)S(1)}, u32[]{:S(2)}) copy-start(bf16[1280,128]{1,0:T(8,128)(2,1)S(1)} %collective-permute-done.14.refs_1_) | copy-start | bytes 983044
  100.0 2.1 %collective-permute-start.18 = (bf16[1280,128]{1,0:T(8,128)(2,1)S(1)}, bf16[1280,128]{1,0:T(8,128)(2,1)S(1)}, u32[]{:S(2)}, u32[]{:S(2)}) collective-permute-start(bf16[1280,128]{1,0:T(8,128)(2,1)S(1)} %collective-permute-done.14.refs_1_), channel_id=1, source_target_pairs={{0,1},{1,0},{2,3},{3,2},{4,5},{5,4},{6,7},{7,6},{8,9},{9,8},{10,11... | collective-permute-start | bytes 983048 | tf_op jit(solution)/shard_map/ppermute | solution.py:368
  100.9 1.3 %copy-start.4 = (bf16[1280,128]{1,0:T(8,128)(2,1)}, bf16[1280,128]{1,0:T(8,128)(2,1)S(1)}, u32[]{:S(2)}) copy-start(bf16[1280,128]{1,0:T(8,128)(2,1)S(1)} %collective-permute-done.17.refs_4_) | copy-start | bytes 983044
  100.9 1.3 %copy-start.5 = (bf16[1280,128]{1,0:T(8,128)(2,1)}, bf16[1280,128]{1,0:T(8,128)(2,1)S(1)}, u32[]{:S(2)}) copy-start(bf16[1280,128]{1,0:T(8,128)(2,1)S(1)} %collective-permute-done.20.refs_7_) | copy-start | bytes 983044
  (10 other events, 6.9 us)

commit v2 on v1

v2 whole, which is shorter than its diff:
```python
import functools
import math

import jax
import jax.numpy as jnp
from jax import lax
from jax.experimental import pallas as pl
from jax.experimental.pallas import tpu as pltpu
from jax.sharding import PartitionSpec as P

NORM_EPS = 1e-05
BF = jnp.bfloat16
F32 = jnp.float32
LARGE = 30 * 1024 * 1024
SMALL = 12 * 1024 * 1024
STEPS = (0, 1, 3, 2)
UNPACK_FLOPS = 10**10
HIDDEN = -1e9


def normalize(values):
    centered = values - jnp.mean(values, axis=-1, keepdims=True)
    inv_scale = lax.rsqrt(jnp.mean(centered * centered, axis=-1, keepdims=True) + NORM_EPS)
    return (centered * inv_scale, inv_scale)


def norm_backward(grad_normed, normed, inv_scale):
    return inv_scale * (
        grad_normed
        - jnp.mean(grad_normed, axis=-1, keepdims=True)
        - normed * jnp.mean(grad_normed * normed, axis=-1, keepdims=True)
    )


def sigmoid(values):
    return 0.5 * jnp.tanh(0.5 * values) + 0.5


def dot_nn(left, right):
    return lax.dot_general(left, right, (((1,), (0,)), ((), ())), preferred_element_type=F32)


def dot_nt(left, right):
    return lax.dot_general(left, right, (((1,), (1,)), ((), ())), preferred_element_type=F32)


def dot_tn(left, right):
    return lax.dot_general(left, right, (((0,), (0,)), ((), ())), preferred_element_type=F32)


def three_parts(values):
    high = values.astype(BF)
    rest = values - high.astype(F32)
    middle = rest.astype(BF)
    low = (rest - middle.astype(F32)).astype(BF)
    return high, middle, low


def as_rows(row, parts):
    width = row.shape[1] // parts
    return jnp.concatenate([row[:, p * width : (p + 1) * width] for p in range(parts)], axis=0)


def prepare_kernel(
    bucket_hbm,
    bias_hbm,
    history_hbm,
    cotangent_hbm,
    in_gain_hbm,
    out_gain_hbm,
    uvqk_hbm,
    out_w_hbm,
    own_ref,
    own_cot_ref,
    in_gain_ref,
    out_gain_ref,
    uvqk_ref,
    out_w_ref,
    tile_ref,
    onehot_ref,
    bucket_ref,
    bias_ref,
    sems,
):
    copies = [
        pltpu.make_async_copy(source, target, sems.at[n])
        for n, (source, target) in enumerate(
            (
                (bucket_hbm, bucket_ref),
                (bias_hbm, bias_ref),
                (history_hbm, own_ref),
                (in_gain_hbm, in_gain_ref),
                (uvqk_hbm, uvqk_ref),
                (cotangent_hbm, own_cot_ref),
                (out_gain_hbm, out_gain_ref),
                (out_w_hbm, out_w_ref),
            )
        )
    ]
    for copy in copies:
        copy.start()
    heads, buckets = bias_ref.shape
    rows = own_ref.shape[0]
    total = bucket_ref.shape[1]
    copies[0].wait()
    copies[1].wait()

    span = total + rows
    offset = total - rows
    turned = offset - lax.broadcasted_iota(jnp.int32, (total, span), 1)
    turned = jnp.where(turned < 0, turned + span, turned)
    pick = (lax.broadcasted_iota(jnp.int32, (total, span), 0) == turned).astype(F32).astype(BF)
    bucket_rows = jnp.broadcast_to(bucket_ref[...].astype(F32), (8, total)).astype(BF)
    bucket_row = dot_nn(bucket_rows, pick)[:1, :]
    column = offset - lax.broadcasted_iota(jnp.int32, (1, span), 1)
    seen = jnp.where(column < 0, column + span, column) < total
    bucket_row = jnp.where(seen, bucket_row, -1.0)
    onehot = (
        lax.broadcasted_iota(jnp.int32, (buckets, span), 0).astype(F32)
        == jnp.broadcast_to(bucket_row, (buckets, span))
    ).astype(F32).astype(BF)
    onehot_ref[...] = onehot
    bias_rows = jnp.concatenate([bias_ref[...], jnp.zeros((8 - heads, buckets), F32)], axis=0)
    by_distance = sum(dot_nn(part, onehot) for part in three_parts(bias_rows))
    by_distance = jnp.where(seen, by_distance, HIDDEN)
    for h in range(heads):
        skewed = pltpu.roll(
            jnp.broadcast_to(by_distance[h : h + 1, :], (rows, span)), 0, 1, stride=1, stride_axis=0
        )
        tile_ref[h] = skewed[:, :total]
    for copy in copies[2:]:
        copy.wait()


def place_pieces(refs, target, size):
    me = lax.axis_index("seq")
    for step, ref in zip(STEPS, refs):
        source = lax.rem(me + size - step, size)
        rows = ref.shape[0]
        target[pl.ds(pl.multiple_of(source * rows, rows), rows), :] = ref[...]


def forward_kernel(size, *refs):
    pieces = refs[:size]
    (
        tile_ref,
        in_gain_ref,
        uvqk_ref,
        scaled_ref,
        gate_ref,
        slope_ref,
        vqk_ref,
        weights_ref,
        score_slope_ref,
        mixed_ref,
        hist_s,
    ) = refs[size:]
    rows, width = pieces[0].shape
    total = rows * size
    heads = tile_ref.shape[0]
    head_dim = width // heads
    scale = 1.0 / math.sqrt(head_dim)
    in_gain = in_gain_ref[...]
    place_pieces(pieces, hist_s, size)
    for i in range(size):
        here = slice(i * rows, (i + 1) * rows)
        ends = (i + 1) * rows
        first = total - ends
        normed, _ = normalize(hist_s[here, :].astype(F32))
        scaled = (normed * in_gain).astype(BF)
        scaled_ref[here, :] = scaled
        for part in range(4):
            projected = dot_nn(scaled, uvqk_ref[:, part * width : (part + 1) * width])
            sig = sigmoid(projected)
            activated = projected * sig
            slope_ref[part, here, :] = sig + activated * (1.0 - sig)
            if part == 0:
                gate_ref[here, :] = activated
            else:
                vqk_ref[part - 1, here, :] = activated.astype(BF)
        for h in range(heads):
            lanes = slice(h * head_dim, (h + 1) * head_dim)
            scores = dot_nt(vqk_ref[1, here, lanes], vqk_ref[2, :ends, lanes]) * scale
            scores = scores + tile_ref[h, :, first:]
            sig = sigmoid(scores)
            weights = scores * sig
            score_slope_ref[h, here, :ends] = sig + weights * (1.0 - sig)
            weights_low = weights.astype(BF)
            weights_ref[h, here, :ends] = weights_low
            mixed_ref[here, lanes] = dot_nn(weights_low, vqk_ref[0, :ends, lanes])


def backward_kernel(size, length_ref, *refs):
    pieces = refs[:size]
    (
        out_gain_ref,
        out_w_ref,
        scaled_ref,
        gate_ref,
        slope_ref,
        vqk_ref,
        weights_ref,
        score_slope_ref,
        mixed_ref,
        send_ref,
        keep_ref,
        own_gated_ref,
        own_grad_ref,
        diag_ref,
        gain_ref,
        cot_s,
        gated_s,
        grads_s,
        grad_mixed_s,
        proj_grad_s,
    ) = refs[size:]
    rows, width = pieces[0].shape
    total = rows * size
    heads = weights_ref.shape[0]
    head_dim = width // heads
    scale = 1.0 / math.sqrt(head_dim)
    me = lax.axis_index("seq")
    core = lax.rem(lax.axis_index("batch"), 2)
    length = length_ref[0]
    out_gain = out_gain_ref[...]
    place_pieces(pieces, cot_s, size)
    grad_out_gain = jnp.zeros((1, width), F32)
    for h in range(heads):
        diag_ref[h] = jnp.zeros((rows, total), F32)
    for i in range(size):
        here = slice(i * rows, (i + 1) * rows)
        ends = (i + 1) * rows
        first = total - ends
        valid = (lax.broadcasted_iota(jnp.int32, (rows, 1), 0) + i * rows) < length
        mixed = jnp.where(valid, mixed_ref[here, :], 0.0)
        mixed_normed, inv_mixed = normalize(mixed)
        gating = gate_ref[here, :]
        gated_s[here, :] = (mixed_normed * out_gain * gating).astype(BF)
        grad_gated = dot_nt(cot_s[here, :], out_w_ref[...])
        times_normed = grad_gated * mixed_normed
        grad_out_gain = grad_out_gain + jnp.sum(times_normed * gating, axis=0, keepdims=True)
        proj_grad_s[0, here, :] = (times_normed * out_gain * slope_ref[0, here, :]).astype(BF)
        grad_mixed = norm_backward(grad_gated * out_gain * gating, mixed_normed, inv_mixed)
        grad_mixed_low = jnp.where(valid, grad_mixed, 0.0).astype(BF)
        grad_mixed_s[here, :] = grad_mixed_low
        for h in range(heads):
            lanes = slice(h * head_dim, (h + 1) * head_dim)
            grad_weights = dot_nt(grad_mixed_low[:, lanes], vqk_ref[0, :ends, lanes])
            grad_scores = grad_weights * score_slope_ref[h, here, :ends]
            diag_ref[h, :, first:] += grad_scores
            grad_scores_low = grad_scores.astype(BF)
            grads_s[h, here, :ends] = grad_scores_low
            grad_query = dot_nn(grad_scores_low, vqk_ref[2, :ends, lanes]) * scale
            proj_grad_s[2, here, lanes] = (grad_query * slope_ref[2, here, lanes]).astype(BF)
    gain_ref[...] = grad_out_gain

    for j in range(size):
        here = slice(j * rows, (j + 1) * rows)
        later = slice(j * rows, total)
        for h in range(heads):
            lanes = slice(h * head_dim, (h + 1) * head_dim)
            grad_key = dot_tn(grads_s[h, later, here], vqk_ref[1, later, lanes]) * scale
            proj_grad_s[3, here, lanes] = (grad_key * slope_ref[3, here, lanes]).astype(BF)
            grad_value = dot_tn(weights_ref[h, later, here], grad_mixed_s[later, lanes])
            proj_grad_s[1, here, lanes] = (grad_value * slope_ref[1, here, lanes]).astype(BF)

    half = total // 2
    block = width // 4
    own_block = proj_grad_s[me]
    cot_block = cot_s[:, pl.ds(pl.multiple_of(me * block, block), block)]
    for ref, side in ((send_ref, 1 - core), (keep_ref, core)):
        lanes = pl.ds(pl.multiple_of(side * half, half), half)
        uvqk_term = dot_tn(scaled_ref[:, lanes], own_block)
        for b in range(4):
            ref[b * half : (b + 1) * half, :] = uvqk_term[:, b * block : (b + 1) * block].astype(
                ref.dtype
            )
        out_term = dot_tn(gated_s[:, lanes], cot_block)
        ref[4 * half : 5 * half, :] = out_term.astype(ref.dtype)
    own_rows = pl.ds(pl.multiple_of(me * rows, rows), rows)
    own_gated_ref[...] = gated_s[own_rows, :]
    for part in range(4):
        own_grad_ref[part] = proj_grad_s[part, own_rows, :]


def rows_kernel(
    own_ref,
    own_cot_ref,
    in_gain_ref,
    uvqk_ref,
    out_w_ref,
    own_gated_ref,
    own_grad_ref,
    diag_ref,
    gain_ref,
    onehot_ref,
    output_ref,
    grad_input_ref,
    small_ref,
):
    rows, width = own_ref.shape
    heads, _, total = diag_ref.shape
    buckets, span = onehot_ref.shape
    me = lax.axis_index("seq")
    in_gain = in_gain_ref[...]
    wide = own_ref[...].astype(F32)
    normed, inv_in = normalize(wide)
    grad_scaled = jnp.zeros((rows, width), F32)
    for part in range(4):
        grad_scaled = grad_scaled + dot_nt(
            own_grad_ref[part], uvqk_ref[:, part * width : (part + 1) * width]
        )
    grad_in_gain = jnp.sum(grad_scaled * normed, axis=0, keepdims=True)
    grad_input = own_cot_ref[...].astype(F32) + norm_backward(grad_scaled * in_gain, normed, inv_in)
    grad_input_ref[...] = grad_input.astype(BF)
    output_ref[...] = (wide + dot_nn(own_gated_ref[...], out_w_ref[...])).astype(BF)

    onehot = onehot_ref[...]
    bias_sums = []
    for h in range(heads):
        folded = jnp.concatenate([diag_ref[h], jnp.zeros((rows, span - total), F32)], axis=1)
        count = rows // 2
        while count >= 8:
            folded = folded[:count, :] + pltpu.roll(folded[count:, :], span - count, 1)
            count //= 2
        while count >= 1:
            folded = folded + pltpu.roll(pltpu.roll(folded, 8 - count, 0), span - count, 1)
            count //= 2
        bias_sums.append(folded[:1, :])
    bias_sums = jnp.concatenate(bias_sums + [jnp.zeros((8 - heads, span), F32)], axis=0)
    grad_bias = sum(dot_nt(part, onehot) for part in three_parts(bias_sums))[:heads, :]
    small = jnp.concatenate(
        [
            grad_bias,
            as_rows(grad_in_gain, 4),
            as_rows(gain_ref[...], 4),
            jnp.zeros((4, buckets), F32),
        ],
        axis=0,
    )
    row = lax.broadcasted_iota(jnp.int32, small.shape, 0)
    mine = (row == me) | ((row >= 4) & (row < 8)) | (row == 8 + me)
    small_ref[...] = jnp.where(mine, small, 0.0)


def after_core_kernel(keep_ref, got_ref, small_ref, own_ref, *others):
    half = keep_ref.shape[0] // 5
    part = half // 4
    y = lax.axis_index("batch") // (lax.axis_size("batch") // 4)
    for ref, step in zip((own_ref,) + others, STEPS):
        there = lax.rem(y + step, 4)
        for b in range(5):
            place = pl.ds(pl.multiple_of(b * half + there * part, part), part)
            ref[b * part : (b + 1) * part, :] = (
                keep_ref[place, :] + got_ref[place, :].astype(F32)
            ).astype(ref.dtype)
        ref[5 * part :, :] = small_ref[...].astype(ref.dtype)


def after_y_kernel(own_ref, one_ref, three_ref, two_ref, sum_ref):
    body = own_ref.shape[0] - 16
    got = lambda ref, place: ref[place, :].astype(F32)
    for place, own in (
        (slice(0, body), own_ref[:body, :]),
        (slice(body, None), own_ref[body:, :].astype(BF).astype(F32)),
    ):
        sum_ref[place, :] = (
            (own + got(two_ref, place)) + (got(one_ref, place) + got(three_ref, place))
        ).astype(BF)


def pair_sum_kernel(left_ref, right_ref, sum_ref):
    sum_ref[...] = (left_ref[...].astype(F32) + right_ref[...].astype(F32)).astype(BF)


def ring_sum_kernel(own_ref, two_ref, six_ref, four_ref, sum_ref):
    sum_ref[...] = (
        (own_ref[...].astype(F32) + four_ref[...].astype(F32))
        + (two_ref[...].astype(F32) + six_ref[...].astype(F32))
    ).astype(BF)


def join_kernel(*refs):
    joined = refs[-1]
    size = refs[0].shape[0]
    for n, ref in enumerate(refs[:-1]):
        joined[n * size : (n + 1) * size, :] = ref[...]


def unpack(factor, sources, kept, *refs):
    blocks = refs[: len(sources)]
    uvqk_hbm, out_hbm, wide_s, narrow_s, sems = refs[len(sources) + kept :]
    size = blocks[0].shape[0] // 4
    part = (size - 16) // 5
    width = uvqk_hbm.shape[1] // 4
    block = width // 4
    batch = lax.axis_index("batch")
    core = lax.rem(batch, 2)
    x = lax.axis_index("seq")
    y = batch // (lax.axis_size("batch") // 4)
    copies = []
    for n, (ref, (other, second)) in enumerate(zip(blocks, sources)):
        from_core = 1 - core if other else core
        x_first = from_core == 0
        for m, first in enumerate(STEPS):
            slot = n * 4 + m
            from_x = lax.rem(x + 4 - jnp.where(x_first, first, second), 4)
            from_y = lax.rem(y + 4 - jnp.where(x_first, second, first), 4)
            start = m * size
            for b in range(4):
                wide_s[slot, :, b * block : (b + 1) * block] = (
                    ref[start + b * part : start + (b + 1) * part, :].astype(F32) * factor
                )
            narrow_s[slot] = ref[start + 4 * part : start + 5 * part, :].astype(F32) * factor
            place = pl.ds(pl.multiple_of((from_core * 4 + from_y) * part, part), part)
            for copy in (
                pltpu.make_async_copy(
                    wide_s.at[slot],
                    uvqk_hbm.at[place, pl.ds(pl.multiple_of(from_x * width, width), width)],
                    sems.at[slot, 0],
                ),
                pltpu.make_async_copy(
                    narrow_s.at[slot],
                    out_hbm.at[place, pl.ds(pl.multiple_of(from_x * block, block), block)],
                    sems.at[slot, 1],
                ),
            ):
                copy.start()
                copies.append(copy)
    return copies


def unpack_kernel(factor, sources, kept, *refs):
    for copy in unpack(factor, sources, kept, *refs):
        copy.wait()


def last_kernel(factor, sources, kept, *refs):
    blocks = refs[:8]
    unpacked = refs[8 - len(sources) : 8 + kept]
    uvqk_hbm, out_hbm, bias_ref, in_gain_ref, out_gain_ref = refs[8 + kept : 13 + kept]
    copies = unpack(factor, sources, kept, *unpacked, uvqk_hbm, out_hbm, *refs[13 + kept :])
    size = blocks[0].shape[0] // 4
    core = lax.rem(lax.axis_index("batch"), 2)

    def piece(ref, first):
        place = (first + 1) * size
        return ref[place - 16 : place, :].astype(F32)

    def over_x(own, x_first):
        by_first = [piece(own[0], n) for n in range(4)]
        by_second = [piece(own[n], 0) for n in range(4)]
        zero, one, three, two = [
            jnp.where(x_first, left, right) for left, right in zip(by_first, by_second)
        ]
        return (zero + two) + (one + three)

    summed = (over_x(blocks[:4], core == 0) + over_x(blocks[4:], core == 1)) * factor
    bias_ref[...] = summed[:4, :]
    in_gain_ref[...] = summed[4:8, :]
    out_gain_ref[...] = summed[8:12, :]
    for copy in copies:
        copy.wait()


def params(limit):
    return pltpu.CompilerParams(vmem_limit_bytes=limit)


def cost(flops, bytes_accessed):
    return pl.CostEstimate(flops=flops, bytes_accessed=bytes_accessed, transcendentals=0)


def shards(
    history,
    out_cotangent,
    lengths,
    bucket_of,
    position_bias,
    norm_gain,
    uvqk_weight,
    out_gain,
    out_weight,
):
    rows, width = history.shape[1:]
    heads, buckets = position_bias.shape
    seq_size = lax.axis_size("seq")
    batch_size = lax.axis_size("batch")
    total = rows * seq_size
    span = total + rows
    z_size = batch_size // 8
    factor = 1.0 / math.sqrt(batch_size * total)

    def along_x(values, step):
        return lax.ppermute(values, "seq", [(i, (i + step) % seq_size) for i in range(seq_size)])

    def place_of(b):
        return b // (2 * z_size), (b // 2) % z_size, b % 2

    def along_batch(values, move):
        pairs = []
        for b in range(batch_size):
            y, z, c = move(*place_of(b))
            pairs.append((b, (y * z_size + z) * 2 + c))
        return lax.ppermute(values, "batch", pairs)

    def along_y(values, step):
        return along_batch(values, lambda y, z, c: ((y + step) % 4, z, c))

    def along_z(values, step):
        return along_batch(values, lambda y, z, c: (y, (z + step) % z_size, c))

    def across(values):
        return along_batch(values, lambda y, z, c: (y, z, 1 - c))

    def along_either(values, step, x_core):
        pairs = []
        for x in range(seq_size):
            for b in range(batch_size):
                y, z, c = place_of(b)
                to_x = (x + step) % 4 if c == x_core else x
                to_y = y if c == x_core else (y + step) % 4
                pairs.append(
                    (x * batch_size + b, to_x * batch_size + (to_y * z_size + z) * 2 + c)
                )
        return lax.ppermute(values, ("seq", "batch"), pairs)

    shape = jax.ShapeDtypeStruct
    vmem = pl.BlockSpec(memory_space=pltpu.VMEM)
    smem = pl.BlockSpec(memory_space=pltpu.SMEM)
    hbm = pl.BlockSpec(memory_space=pltpu.HBM)
    own_history = history[0]
    own_cotangent = out_cotangent[0]
    pieces = [along_x(own_history, step) for step in STEPS[1:]]
    cot_pieces = [along_x(own_cotangent, step) for step in STEPS[1:]]
    own, own_cot, in_gain, gain, uvqk, out_w, tile, onehot = pl.pallas_call(
        prepare_kernel,
        out_shape=[
            shape((rows, width), BF),
            shape((rows, width), BF),
            shape((1, width), F32),
            shape((1, width), F32),
            shape(uvqk_weight.shape, BF),
            shape(out_weight.shape, BF),
            shape((heads, rows, total), F32),
            shape((buckets, span), BF),
        ],
        in_specs=[hbm] * 8,
        out_specs=[vmem] * 8,
        scratch_shapes=[
            pltpu.VMEM((1, total), jnp.int32),
            pltpu.VMEM((heads, buckets), F32),
            pltpu.SemaphoreType.DMA((8,)),
        ],
        compiler_params=params(SMALL),
        cost_estimate=cost(10**9, 3 * 10**6),
        name="prepare",
    )(
        *[
            pltpu.with_memory_space_constraint(values, pltpu.HBM)
            for values in (
                bucket_of.reshape(1, total),
                position_bias,
                own_history,
                own_cotangent,
                norm_gain.reshape(1, width),
                out_gain.reshape(1, width),
                uvqk_weight,
                out_weight,
            )
        ]
    )
    scaled, gate, slope, vqk, weights, score_slope, mixed = pl.pallas_call(
        functools.partial(forward_kernel, seq_size),
        out_shape=[
            shape((total, width), BF),
            shape((total, width), F32),
            shape((4, total, width), F32),
            shape((3, total, width), BF),
            shape((heads, total, total), BF),
            shape((heads, total, total), F32),
            shape((total, width), F32),
        ],
        scratch_shapes=[pltpu.VMEM((total, width), BF)],
        compiler_params=params(LARGE),
        cost_estimate=cost(4 * 10**9, 10**7),
        name="forward",
    )(own, *pieces, tile, in_gain, uvqk)
    half = total // 2
    body = 5 * half
    send, keep, own_gated, own_grad, diag, gain_term = pl.pallas_call(
        functools.partial(backward_kernel, seq_size),
        out_shape=[
            shape((body, buckets), BF),
            shape((body, buckets), F32),
            shape((rows, width), BF),
            shape((4, rows, width), BF),
            shape((heads, rows, total), F32),
            shape((1, width), F32),
        ],
        in_specs=[smem] + [vmem] * 13,
        out_specs=[vmem] * 6,
        scratch_shapes=[
            pltpu.VMEM((total, width), BF),
            pltpu.VMEM((total, width), BF),
            pltpu.VMEM((heads, total, total), BF),
            pltpu.VMEM((total, width), BF),
            pltpu.VMEM((4, total, width), BF),
        ],
        compiler_params=params(LARGE),
        cost_estimate=cost(4 * 10**9, 10**7),
        name="backward",
    )(
        lengths,
        own_cot,
        *cot_pieces,
        gain,
        out_w,
        scaled,
        gate,
        slope,
        vqk,
        weights,
        score_slope,
        mixed,
    )

    got = across(send)
    output, grad_input, small = pl.pallas_call(
        rows_kernel,
        out_shape=[
            shape((rows, width), BF),
            shape((rows, width), BF),
            shape((16, buckets), F32),
        ],
        compiler_params=params(SMALL),
        cost_estimate=cost(10**9, 3 * 10**6),
        name="rows",
    )(own, own_cot, in_gain, uvqk, out_w, own_gated, own_grad, diag, gain_term, onehot)

    part = half // 4
    size = 5 * part + 16
    chunk = (size, buckets)
    mine, *parts = pl.pallas_call(
        after_core_kernel,
        out_shape=[shape(chunk, F32)] + [shape(chunk, BF)] * 3,
        compiler_params=params(SMALL),
        name="after_core",
    )(keep, got, small)
    parts = [along_y(values, step) for values, step in zip(parts, STEPS[1:])]
    summed = pl.pallas_call(
        after_y_kernel, out_shape=shape(chunk, BF), compiler_params=params(SMALL), name="after_y"
    )(mine, *parts)
    other = along_batch(summed, lambda y, z, c: (y, z ^ 1, c))
    summed = pl.pallas_call(
        pair_sum_kernel, out_shape=shape(chunk, BF), compiler_params=params(SMALL), name="pair_sum"
    )(summed, other)
    ring = [along_z(summed, step) for step in (2, 6, 4)]
    summed = pl.pallas_call(
        ring_sum_kernel, out_shape=shape(chunk, BF), compiler_params=params(SMALL), name="ring_sum"
    )(summed, *ring)

    blocks = [along_either(summed, step, 0) for step in STEPS[1:]]
    joined = pl.pallas_call(
        join_kernel,
        out_shape=shape((4 * size, buckets), BF),
        compiler_params=params(SMALL),
        name="join",
    )(summed, *blocks)
    columns, others = {0: joined}, {}
    def unpack_call(sources, kept, last=False):
        blocks = [(others if other else columns)[step] for other, step in sources]
        slots = 4 * len(blocks)
        outs = [shape((width, 4 * width), F32), shape((width, width), F32)]
        if last:
            blocks = [columns[step] for step in STEPS] + [others[step] for step in STEPS]
        count = len(blocks)
        return pl.pallas_call(
            functools.partial(last_kernel if last else unpack_kernel, factor, sources, len(kept)),
            out_shape=outs + [shape((4, buckets), F32)] * (3 if last else 0),
            in_specs=[vmem] * count + [hbm] * len(kept),
            out_specs=[hbm] * 2 + [vmem] * (3 if last else 0),
            input_output_aliases={count + n: n for n in range(len(kept))},
            scratch_shapes=[
                pltpu.VMEM((slots, part, width), F32),
                pltpu.VMEM((slots, part, buckets), F32),
                pltpu.SemaphoreType.DMA((slots, 2)),
            ],
            compiler_params=params(SMALL),
            cost_estimate=cost(UNPACK_FLOPS, 10**6 * slots // 4),
            name="unpack",
        )(*blocks, *kept)

    moved = {step: along_either(joined, step, 1) for step in STEPS[1:]}
    kept = unpack_call(((False, 0),), ())
    again, kept = lax.optimization_barrier((joined, kept))
    others[0] = across(again)
    for step in STEPS[1:]:
        columns[step], kept = lax.optimization_barrier((moved[step], kept))
        others[step] = across(columns[step])
    kept = unpack_call(((True, 0), (False, 1), (False, 3), (False, 2)), kept)
    grad_uvqk, grad_out_weight, grad_bias, grad_in_gain, grad_out_gain = unpack_call(
        ((True, 1), (True, 3), (True, 2)), kept, last=True
    )
    return (
        output[None],
        grad_input[None],
        grad_uvqk,
        grad_out_weight,
        grad_bias,
        grad_in_gain.reshape(width),
        grad_out_gain.reshape(width),
    )


def solution(mesh):
    return jax.shard_map(
        shards,
        mesh=mesh,
        in_specs=(
            P("batch", "seq", None),
            P("batch", "seq", None),
            P("batch"),
            P(),
            P(),
            P(),
            P(),
            P(),
            P(),
        ),
        out_specs=(P("batch", "seq", None), P("batch", "seq", None), P(), P(), P(), P(), P()),
        check_vma=False,
    )
```

time: 108 us -> 85.7 us (0.79)
  waiting for transfers between devices: 28.7 us -> 20 us
  Pallas kernels: 26.9 us -> 18.9 us
  local copies, waits for them, and re-layouts: 5.35 us -> 0 us
    ppermute x6, waiting for transfers between devices: 15.1 us -> 4.44 us  [along_x(): lax.ppermute(values, 'seq', [(i, (i + step) % seq_size) for i in range(se...]
    ppermute x0 -> x6, starting transfers between devices: none -> 5.57 us  [along_either(): return lax.ppermute(values, ('seq', 'batch'), pairs)]
    unnamed x42 -> x0, local copies, waits for them, and re-layouts: 5.35 us -> none
    ppermute x0 -> x6, waiting for transfers between devices: none -> 4.57 us  [along_either(): return lax.ppermute(values, ('seq', 'batch'), pairs)]
    ppermute x15 -> x12, starting transfers between devices: 35 us -> 31.4 us  [along_batch(): return lax.ppermute(values, 'batch', pairs)]
    ppermute x15 -> x12, waiting for transfers between devices: 13.5 us -> 11 us  [along_batch(): return lax.ppermute(values, 'batch', pairs)]
    pallas_call x1, Pallas kernels: 1.99 us -> 0.06 us  [shards(): pl.pallas_call(after_core_kernel, out_shape=[shape(chunk, F32)] + [shape(...]
    pallas_call x1, Pallas kernels: 1.72 us -> 0.06 us  [shards(): pl.pallas_call(after_y_kernel, out_shape=shape(chunk, BF), compiler_param...]
  transfers between devices with their start and end apart: 21 -> 24, of which waited for: 14 -> 9; matrix products, arithmetic and copies ran while one was open for 0% -> 0% of each run, Pallas kernels for 0% -> 13%
where the time goes in v2:
time: 85.7 us; the launch traced here: 85.6 us
  starting transfers between devices  45 us (53%)
  waiting for transfers between devices  20 us (23%)
  Pallas kernels  18.9 us (22%)
  between operations  1.62 us (2%)
    ppermute x12, starting transfers between devices, along_batch(): return lax.ppermute(values, 'batch', pairs)  31.4 us
    ppermute x12, waiting for transfers between devices, along_batch(): return lax.ppermute(values, 'batch', pairs)  11 us
    ppermute x6, starting transfers between devices, along_x(): lax.ppermute(values, 'seq', [(i, (i + step) % seq_size) for i in range(se...  8.1 us
    ppermute x6, starting transfers between devices, along_either(): return lax.ppermute(values, ('seq', 'batch'), pairs)  5.57 us
    pallas_call x1, Pallas kernels, shards(): pl.pallas_call(functools.partial(backward_kernel, seq_size), out_shape=[s...  5.5 us
    pallas_call x3, Pallas kernels, unpack_call(): pl.pallas_call(functools.partial(last_kernel if last else unpack_kernel,...  4.89 us
    pallas_call x1, Pallas kernels, shards(): pl.pallas_call(functools.partial(forward_kernel, seq_size), out_shape=[sh...  4.58 us
    ppermute x6, waiting for transfers between devices, along_either(): return lax.ppermute(values, ('seq', 'batch'), pairs)  4.57 us
  transfers between devices with their start and end apart: 24, of which 9 were waited for; matrix products, arithmetic and copies ran while one was open for 0% of the time, Pallas kernels for 13%

profile of v2, /device:TPU:1, one launch (start us, length us, event | category | flops | bytes accessed | tf_op | source)
XLA Modules:
  0.0 85.6 jit_solution(2697027450480876692)
XLA Ops:
  0.6 3.7 %collective-permute-start.5 = (bf16[128,512]{1,0:T(8,128)(2,1)}, bf16[128,512]{1,0:T(8,128)(2,1)S(1)}, u32[]{:S(2)}, u32[]{:S(2)}) collective-permute-start(bf16[128,512]{1,0:T(8,128)(2,1)} %bitcast.9), channel_id=1, source_target_pairs={{0,128},{64,192},{128,0},{192,64},{1,129},{65,193},{129,1},{193,65... | collective-permute-start | bytes 393224 | tf_op jit(solution)/shard_map/ppermute | solution.py:495
  4.3 0.9 %collective-permute-start.4 = (bf16[128,512]{1,0:T(8,128)(2,1)}, bf16[128,512]{1,0:T(8,128)(2,1)S(1)}, u32[]{:S(2)}, u32[]{:S(2)}) collective-permute-start(bf16[128,512]{1,0:T(8,128)(2,1)} %bitcast.10), channel_id=1, source_target_pairs={{0,192},{64,0},{128,64},{192,128},{1,193},{65,1},{129,65},{193,129... | collective-permute-start | bytes 393224 | tf_op jit(solution)/shard_map/ppermute | solution.py:495
  5.2 0.6 collective-permute-start.3
  5.8 0.6 collective-permute-start.2
  6.4 2.1 %collective-permute-start.1 = (bf16[128,512]{1,0:T(8,128)(2,1)}, bf16[128,512]{1,0:T(8,128)(2,1)S(1)}, u32[]{:S(2)}, u32[]{:S(2)}) collective-permute-start(bf16[128,512]{1,0:T(8,128)(2,1)} %bitcast.14), channel_id=1, source_target_pairs={{0,192},{64,0},{128,64},{192,128},{1,193},{65,1},{129,65},{193,129... | collective-permute-start | bytes 393224 | tf_op jit(solution)/shard_map/ppermute | solution.py:495
  9.1 1.9 %prepare.1 = (bf16[128,512]{1,0:T(8,128)(2,1)S(1)}, bf16[128,512]{1,0:T(8,128)(2,1)S(1)}, f32[1,512]{1,0:T(1,128)S(1)}, f32[1,512]{1,0:T(1,128)S(1)}, bf16[512,2...) custom-call(s32[1,512]{1,0:T(1,128)} %bitcast.19, ...), custom_call_target="tpu_custom_call" | custom-call | flops 1000000000 | bytes 3000000 | tf_op jit(solution)/shard_map/prepare/pallas_call | solution.py:536
  11.3 4.4 %collective-permute-done.3.refs_1_ = bf16[128,512]{1,0:T(8,128)(2,1)S(1)} collective-permute-done((bf16[128,512]{1,0:T(8,128)(2,1)}, bf16[128,512]{1,0:T(8,128)(2,1)S(1)}, u32[]{:S(2)}, u32[]{:S(2)}) %collective-permute-start.3) | collective-permute-done | bytes 131104 | tf_op jit(solution)/shard_map/ppermute | solution.py:495
  15.8 4.6 %forward.1 = (bf16[512,512]{1,0:T(8,128)(2,1)S(1)}, f32[512,512]{1,0:T(8,128)S(1)}, f32[4,512,512]{2,1,0:T(8,128)S(1)}, bf16[3,512,512]{2,1,0:T(8,128)(2,1)S(1)}...) custom-call(bf16[128,512]{1,0:T(8,128)(2,1)S(1)} %get-tuple-element.56.refs_0_.own_ref, ...), custom_call_target="tpu_custom_call" | custom-call | flops 4000000000 | bytes 10000000 | tf_op jit(solution)/shard_map/forward/pallas_call | solution.py:573
  20.4 5.5 %backward.1 = (bf16[1280,128]{1,0:T(8,128)(2,1)S(1)}, f32[1280,128]{1,0:T(8,128)S(1)}, bf16[128,512]{1,0:T(8,128)(2,1)S(1)}, bf16[4,128,512]{2,1,0:T(8,128)(2,1)...) custom-call(s32[1]{0:T(128)S(6)} %copy.24.length_ref, ...), custom_call_target="tpu_custom_call" | custom-call | flops 4000000000 | bytes 10000000 | tf_op jit(solution)/shard_map/backward/pallas_call | solution.py:591
  25.9 1.1 %collective-permute-start.6 = (bf16[1280,128]{1,0:T(8,128)(2,1)S(1)}, bf16[1280,128]{1,0:T(8,128)(2,1)S(1)}, u32[]{:S(2)}, u32[]{:S(2)}) collective-permute-start(bf16[1280,128]{1,0:T(8,128)(2,1)S(1)} %get-tuple-element.78), channel_id=1, source_target_pairs={{0,1},{1,0},{2,3},{3,2},{4,5},{5,4},{6,7},{7,6},{8,9},{9,8},{10,11... | collective-permute-start | bytes 983048 | tf_op jit(solution)/shard_map/ppermute | solution.py:505
  27.0 1.8 %rows.1 = (bf16[128,512]{1,0:T(8,128)(2,1)}, bf16[128,512]{1,0:T(8,128)(2,1)}, f32[16,128]{1,0:T(8,128)S(1)}) custom-call(bf16[128,512]{1,0:T(8,128)(2,1)S(1)} %get-tuple-element.56.refs_0_.own_ref, bf16[128,512]{1,0:T(8,128)(2,1)S(1)} %get-tuple-element.57.refs_0_.own_cot_ref, f32[1,512]{1,0:T(1,128)S(1)} %get-tuple-element.58.refs_5_.in_gain_ref, ...), custom_call_target="tpu_custom_call" | custom-call | flops 1000000000 | bytes 3000000 | tf_op jit(solution)/shard_map/rows/pallas_call | solution.py:629
  29.0 2.7 %collective-permute-start.8 = (bf16[336,128]{1,0:T(8,128)(2,1)S(1)}, bf16[336,128]{1,0:T(8,128)(2,1)S(1)}, u32[]{:S(2)}, u32[]{:S(2)}) collective-permute-start(bf16[336,128]{1,0:T(8,128)(2,1)S(1)} %get-tuple-element.82), channel_id=1, source_target_pairs={{0,48},{1,49},{2,50},{3,51},{4,52},{5,53},{6,54},{7,55},{8,56},{9,... | collective-permute-start | bytes 258056 | tf_op jit(solution)/shard_map/ppermute | solution.py:505
  31.7 0.4 collective-permute-start.9
  32.1 2.3 %collective-permute-done.7.one_ref = bf16[336,128]{1,0:T(8,128)(2,1)S(1)} collective-permute-done((bf16[336,128]{1,0:T(8,128)(2,1)S(1)}, bf16[336,128]{1,0:T(8,128)(2,1)S(1)}, u32[]{:S(2)}, u32[]{:S(2)}) %collective-permute-start.7) | collective-permute-done | bytes 86048 | tf_op jit(solution)/shard_map/ppermute | solution.py:505
  34.4 0.8 collective-permute-done.8.three_ref
  35.2 1.4 %collective-permute-done.9.two_ref = bf16[336,128]{1,0:T(8,128)(2,1)S(1)} collective-permute-done((bf16[336,128]{1,0:T(8,128)(2,1)S(1)}, bf16[336,128]{1,0:T(8,128)(2,1)S(1)}, u32[]{:S(2)}, u32[]{:S(2)}) %collective-permute-start.9) | collective-permute-done | bytes 86048 | tf_op jit(solution)/shard_map/ppermute | solution.py:505
  36.6 1.1 %collective-permute-start.10 = (bf16[336,128]{1,0:T(8,128)(2,1)S(1)}, bf16[336,128]{1,0:T(8,128)(2,1)S(1)}, u32[]{:S(2)}, u32[]{:S(2)}) collective-permute-start(bf16[336,128]{1,0:T(8,128)(2,1)S(1)} %after_y.1.left_ref), channel_id=1, source_target_pairs={{0,2},{1,3},{2,0},{3,1},{4,6},{5,7},{6,4},{7,5},{8,10},{9,11},{10,... | collective-permute-start | bytes 258056 | tf_op jit(solution)/shard_map/ppermute | solution.py:505
  37.7 2.5 %collective-permute-done.10.right_ref = bf16[336,128]{1,0:T(8,128)(2,1)S(1)} collective-permute-done((bf16[336,128]{1,0:T(8,128)(2,1)S(1)}, bf16[336,128]{1,0:T(8,128)(2,1)S(1)}, u32[]{:S(2)}, u32[]{:S(2)}) %collective-permute-start.10) | collective-permute-done | bytes 86048 | tf_op jit(solution)/shard_map/ppermute | solution.py:505
  40.3 6.2 %collective-permute-start.13 = (bf16[336,128]{1,0:T(8,128)(2,1)S(1)}, bf16[336,128]{1,0:T(8,128)(2,1)S(1)}, u32[]{:S(2)}, u32[]{:S(2)}) collective-permute-start(bf16[336,128]{1,0:T(8,128)(2,1)S(1)} %pair_sum.1.own_ref), channel_id=1, source_target_pairs={{0,8},{1,9},{2,10},{3,11},{4,12},{5,13},{6,14},{7,15},{8,0},{9,1},... | collective-permute-start | bytes 258056 | tf_op jit(solution)/shard_map/ppermute | solution.py:505
  46.4 2.4 %collective-permute-start.11 = (bf16[336,128]{1,0:T(8,128)(2,1)S(1)}, bf16[336,128]{1,0:T(8,128)(2,1)S(1)}, u32[]{:S(2)}, u32[]{:S(2)}) collective-permute-start(bf16[336,128]{1,0:T(8,128)(2,1)S(1)} %pair_sum.1.own_ref), channel_id=1, source_target_pairs={{0,4},{1,5},{2,6},{3,7},{4,8},{5,9},{6,10},{7,11},{8,12},{9,13},{1... | collective-permute-start | bytes 258056 | tf_op jit(solution)/shard_map/ppermute | solution.py:505
  48.8 4.1 %collective-permute-done.12.six_ref = bf16[336,128]{1,0:T(8,128)(2,1)S(1)} collective-permute-done((bf16[336,128]{1,0:T(8,128)(2,1)S(1)}, bf16[336,128]{1,0:T(8,128)(2,1)S(1)}, u32[]{:S(2)}, u32[]{:S(2)}) %collective-permute-start.12) | collective-permute-done | bytes 86048 | tf_op jit(solution)/shard_map/ppermute | solution.py:505
  52.9 2.3 %collective-permute-start.16 = (bf16[336,128]{1,0:T(8,128)(2,1)S(1)}, bf16[336,128]{1,0:T(8,128)(2,1)S(1)}, u32[]{:S(2)}, u32[]{:S(2)}) collective-permute-start(bf16[336,128]{1,0:T(8,128)(2,1)S(1)} %ring_sum.1.refs_0_), channel_id=1, source_target_pairs={{0,128},{1,33},{2,130},{3,35},{4,132},{5,37},{6,134},{7,39},{8,136... | collective-permute-start | bytes 258056 | tf_op jit(solution)/shard_map/ppermute | solution.py:526
  55.2 1.2 %collective-permute-start.15 = (bf16[336,128]{1,0:T(8,128)(2,1)S(1)}, bf16[336,128]{1,0:T(8,128)(2,1)S(1)}, u32[]{:S(2)}, u32[]{:S(2)}) collective-permute-start(bf16[336,128]{1,0:T(8,128)(2,1)S(1)} %ring_sum.1.refs_0_), channel_id=1, source_target_pairs={{0,192},{1,49},{2,194},{3,51},{4,196},{5,53},{6,198},{7,55},{8,200... | collective-permute-start | bytes 258056 | tf_op jit(solution)/shard_map/ppermute | solution.py:526
  56.6 1.2 %collective-permute-done.16.refs_3_ = bf16[336,128]{1,0:T(8,128)(2,1)S(1)} collective-permute-done((bf16[336,128]{1,0:T(8,128)(2,1)S(1)}, bf16[336,128]{1,0:T(8,128)(2,1)S(1)}, u32[]{:S(2)}, u32[]{:S(2)}) %collective-permute-start.16) | collective-permute-done | bytes 86048 | tf_op jit(solution)/shard_map/ppermute | solution.py:526
  57.8 0.7 collective-permute-done.15.refs_2_
  58.5 2.7 %collective-permute-done.14.refs_1_ = bf16[336,128]{1,0:T(8,128)(2,1)S(1)} collective-permute-done((bf16[336,128]{1,0:T(8,128)(2,1)S(1)}, bf16[336,128]{1,0:T(8,128)(2,1)S(1)}, u32[]{:S(2)}, u32[]{:S(2)}) %collective-permute-start.14) | collective-permute-done | bytes 86048 | tf_op jit(solution)/shard_map/ppermute | solution.py:526
  61.4 1.6 %collective-permute-start.18 = (bf16[1344,128]{1,0:T(8,128)(2,1)S(1)}, bf16[1344,128]{1,0:T(8,128)(2,1)S(1)}, u32[]{:S(2)}, u32[]{:S(2)}) collective-permute-start(bf16[1344,128]{1,0:T(8,128)(2,1)S(1)} %join.1.refs_0_), channel_id=1, source_target_pairs={{0,48},{1,193},{2,50},{3,195},{4,52},{5,197},{6,54},{7,199},{8,56}... | collective-permute-start | bytes 1032200 | tf_op jit(solution)/shard_map/ppermute | solution.py:526
  63.1 0.9 %unpack.3 = (f32[512,2048]{1,0:T(8,128)}, f32[512,512]{1,0:T(8,128)}) custom-call(bf16[1344,128]{1,0:T(8,128)(2,1)S(1)} %join.1.refs_0_), custom_call_target="tpu_custom_call" | custom-call | flops 10000000000 | bytes 1000000 | tf_op jit(solution)/shard_map/unpack/pallas_call | solution.py:678
  64.0 9.6 %collective-permute-start.20 = (bf16[1344,128]{1,0:T(8,128)(2,1)S(1)}, bf16[1344,128]{1,0:T(8,128)(2,1)S(1)}, u32[]{:S(2)}, u32[]{:S(2)}) collective-permute-start(bf16[1344,128]{1,0:T(8,128)(2,1)S(1)} %join.1.refs_0_), channel_id=1, source_target_pairs={{0,1},{1,0},{2,3},{3,2},{4,5},{5,4},{6,7},{7,6},{8,9},{9,8},{10,11... | collective-permute-start | bytes 1032200 | tf_op jit(solution)/shard_map/ppermute | solution.py:505
  73.6 7.3 %collective-permute-start.23 = (bf16[1344,128]{1,0:T(8,128)(2,1)S(1)}, bf16[1344,128]{1,0:T(8,128)(2,1)S(1)}, u32[]{:S(2)}, u32[]{:S(2)}) collective-permute-start(bf16[1344,128]{1,0:T(8,128)(2,1)S(1)} %collective-permute-done.19.refs_3_), channel_id=1, source_target_pairs={{0,1},{1,0},{2,3},{3,2},{4,5},{5,4},{6,7},{7,6},{8,9},{9,8},{10,11... | collective-permute-start | bytes 1032200 | tf_op jit(solution)/shard_map/ppermute | solution.py:505
  81.4 1.8 %unpack.4 = (f32[512,2048]{1,0:T(8,128)}, f32[512,512]{1,0:T(8,128)}) custom-call(bf16[1344,128]{1,0:T(8,128)(2,1)S(1)} %collective-permute-done.20.refs_0_.refs_4_, bf16[1344,128]{1,0:T(8,128)(2,1)S(1)} %collective-permute-done.17.refs_1_, bf16[1344,128]{1,0:T(8,128)(2,1)S(1)} %collective-permute-done.18.refs_2_, ...), custom_call_target="tpu_custom_call", output_to_operand_aliasing={{0}: (4, {}), {1}: (5, {})} | custom-call | flops 10000000000 | bytes 4000000 | tf_op jit(solution)/shard_map/unpack/pallas_call | solution.py:678
  83.3 2.1 %unpack.5 = (f32[512,2048]{1,0:T(8,128)}, f32[512,512]{1,0:T(8,128)}, f32[4,128]{1,0:T(4,128)}, f32[4,128]{1,0:T(4,128)}, f32[4,128]{1,0:T(4,128)}) custom-call(bf16[1344,128]{1,0:T(8,128)(2,1)S(1)} %join.1.refs_0_, bf16[1344,128]{1,0:T(8,128)(2,1)S(1)} %collective-permute-done.17.refs_1_, ...), custom_call_target="tpu_custom_call", output_to_operand_aliasing={{0}: (8, {}), {1}: (9, {})} | custom-call | flops 10000000000 | bytes 3000000 | tf_op jit(solution)/shard_map/unpack/pallas_call | solution.py:678
  (28 shorter events, 1.6 us)
Async XLA Ops:
  0.6 10.4 %collective-permute-start.5 = (bf16[128,512]{1,0:T(8,128)(2,1)}, bf16[128,512]{1,0:T(8,128)(2,1)S(1)}, u32[]{:S(2)}, u32[]{:S(2)}) collective-permute-start(bf16[128,512]{1,0:T(8,128)(2,1)} %bitcast.9), channel_id=1, source_target_pairs={{0,128},{64,192},{128,0},{192,64},{1,129},{65,193},{129,1},{193,65... | collective-permute-start | bytes 393224 | tf_op jit(solution)/shard_map/ppermute | solution.py:495
  4.3 7.0 %collective-permute-start.4 = (bf16[128,512]{1,0:T(8,128)(2,1)}, bf16[128,512]{1,0:T(8,128)(2,1)S(1)}, u32[]{:S(2)}, u32[]{:S(2)}) collective-permute-start(bf16[128,512]{1,0:T(8,128)(2,1)} %bitcast.10), channel_id=1, source_target_pairs={{0,192},{64,0},{128,64},{192,128},{1,193},{65,1},{129,65},{193,129... | collective-permute-start | bytes 393224 | tf_op jit(solution)/shard_map/ppermute | solution.py:495
  5.2 10.6 %collective-permute-start.3 = (bf16[128,512]{1,0:T(8,128)(2,1)}, bf16[128,512]{1,0:T(8,128)(2,1)S(1)}, u32[]{:S(2)}, u32[]{:S(2)}) collective-permute-start(bf16[128,512]{1,0:T(8,128)(2,1)} %bitcast.11), channel_id=1, source_target_pairs={{0,64},{64,128},{128,192},{192,0},{1,65},{65,129},{129,193},{193,1... | collective-permute-start | bytes 393224 | tf_op jit(solution)/shard_map/ppermute | solution.py:495
  5.8 14.6 %collective-permute-start.2 = (bf16[128,512]{1,0:T(8,128)(2,1)}, bf16[128,512]{1,0:T(8,128)(2,1)S(1)}, u32[]{:S(2)}, u32[]{:S(2)}) collective-permute-start(bf16[128,512]{1,0:T(8,128)(2,1)} %bitcast.13), channel_id=1, source_target_pairs={{0,128},{64,192},{128,0},{192,64},{1,129},{65,193},{129,1},{193,65... | collective-permute-start | bytes 393224 | tf_op jit(solution)/shard_map/ppermute | solution.py:495
  6.4 14.0 %collective-permute-start.1 = (bf16[128,512]{1,0:T(8,128)(2,1)}, bf16[128,512]{1,0:T(8,128)(2,1)S(1)}, u32[]{:S(2)}, u32[]{:S(2)}) collective-permute-start(bf16[128,512]{1,0:T(8,128)(2,1)} %bitcast.14), channel_id=1, source_target_pairs={{0,192},{64,0},{128,64},{192,128},{1,193},{65,1},{129,65},{193,129... | collective-permute-start | bytes 393224 | tf_op jit(solution)/shard_map/ppermute | solution.py:495
  11.1 9.3 %collective-permute-start = (bf16[128,512]{1,0:T(8,128)(2,1)}, bf16[128,512]{1,0:T(8,128)(2,1)S(1)}, u32[]{:S(2)}, u32[]{:S(2)}) collective-permute-start(bf16[128,512]{1,0:T(8,128)(2,1)} %bitcast.16), channel_id=1, source_target_pairs={{0,64},{64,128},{128,192},{192,0},{1,65},{65,129},{129,193},{193,1... | collective-permute-start | bytes 393224 | tf_op jit(solution)/shard_map/ppermute | solution.py:495
  25.9 3.0 %collective-permute-start.6 = (bf16[1280,128]{1,0:T(8,128)(2,1)S(1)}, bf16[1280,128]{1,0:T(8,128)(2,1)S(1)}, u32[]{:S(2)}, u32[]{:S(2)}) collective-permute-start(bf16[1280,128]{1,0:T(8,128)(2,1)S(1)} %get-tuple-element.78), channel_id=1, source_target_pairs={{0,1},{1,0},{2,3},{3,2},{4,5},{5,4},{6,7},{7,6},{8,9},{9,8},{10,11... | collective-permute-start | bytes 983048 | tf_op jit(solution)/shard_map/ppermute | solution.py:505
  28.9 5.4 %collective-permute-start.7 = (bf16[336,128]{1,0:T(8,128)(2,1)S(1)}, bf16[336,128]{1,0:T(8,128)(2,1)S(1)}, u32[]{:S(2)}, u32[]{:S(2)}) collective-permute-start(bf16[336,128]{1,0:T(8,128)(2,1)S(1)} %get-tuple-element.81), channel_id=1, source_target_pairs={{0,16},{1,17},{2,18},{3,19},{4,20},{5,21},{6,22},{7,23},{8,24},{9,... | collective-permute-start | bytes 258056 | tf_op jit(solution)/shard_map/ppermute | solution.py:505
  29.0 6.1 %collective-permute-start.8 = (bf16[336,128]{1,0:T(8,128)(2,1)S(1)}, bf16[336,128]{1,0:T(8,128)(2,1)S(1)}, u32[]{:S(2)}, u32[]{:S(2)}) collective-permute-start(bf16[336,128]{1,0:T(8,128)(2,1)S(1)} %get-tuple-element.82), channel_id=1, source_target_pairs={{0,48},{1,49},{2,50},{3,51},{4,52},{5,53},{6,54},{7,55},{8,56},{9,... | collective-permute-start | bytes 258056 | tf_op jit(solution)/shard_map/ppermute | solution.py:505
  31.7 4.8 %collective-permute-start.9 = (bf16[336,128]{1,0:T(8,128)(2,1)S(1)}, bf16[336,128]{1,0:T(8,128)(2,1)S(1)}, u32[]{:S(2)}, u32[]{:S(2)}) collective-permute-start(bf16[336,128]{1,0:T(8,128)(2,1)S(1)} %get-tuple-element.83), channel_id=1, source_target_pairs={{0,32},{1,33},{2,34},{3,35},{4,36},{5,37},{6,38},{7,39},{8,40},{9,... | collective-permute-start | bytes 258056 | tf_op jit(solution)/shard_map/ppermute | solution.py:505
  36.6 3.6 %collective-permute-start.10 = (bf16[336,128]{1,0:T(8,128)(2,1)S(1)}, bf16[336,128]{1,0:T(8,128)(2,1)S(1)}, u32[]{:S(2)}, u32[]{:S(2)}) collective-permute-start(bf16[336,128]{1,0:T(8,128)(2,1)S(1)} %after_y.1.left_ref), channel_id=1, source_target_pairs={{0,2},{1,3},{2,0},{3,1},{4,6},{5,7},{6,4},{7,5},{8,10},{9,11},{10,... | collective-permute-start | bytes 258056 | tf_op jit(solution)/shard_map/ppermute | solution.py:505
  40.3 8.5 %collective-permute-start.13 = (bf16[336,128]{1,0:T(8,128)(2,1)S(1)}, bf16[336,128]{1,0:T(8,128)(2,1)S(1)}, u32[]{:S(2)}, u32[]{:S(2)}) collective-permute-start(bf16[336,128]{1,0:T(8,128)(2,1)S(1)} %pair_sum.1.own_ref), channel_id=1, source_target_pairs={{0,8},{1,9},{2,10},{3,11},{4,12},{5,13},{6,14},{7,15},{8,0},{9,1},... | collective-permute-start | bytes 258056 | tf_op jit(solution)/shard_map/ppermute | solution.py:505
  46.4 6.4 %collective-permute-start.12 = (bf16[336,128]{1,0:T(8,128)(2,1)S(1)}, bf16[336,128]{1,0:T(8,128)(2,1)S(1)}, u32[]{:S(2)}, u32[]{:S(2)}) collective-permute-start(bf16[336,128]{1,0:T(8,128)(2,1)S(1)} %pair_sum.1.own_ref), channel_id=1, source_target_pairs={{0,12},{1,13},{2,14},{3,15},{4,0},{5,1},{6,2},{7,3},{8,4},{9,5},{1... | collective-permute-start | bytes 258056 | tf_op jit(solution)/shard_map/ppermute | solution.py:505
  46.4 6.4 %collective-permute-start.11 = (bf16[336,128]{1,0:T(8,128)(2,1)S(1)}, bf16[336,128]{1,0:T(8,128)(2,1)S(1)}, u32[]{:S(2)}, u32[]{:S(2)}) collective-permute-start(bf16[336,128]{1,0:T(8,128)(2,1)S(1)} %pair_sum.1.own_ref), channel_id=1, source_target_pairs={{0,4},{1,5},{2,6},{3,7},{4,8},{5,9},{6,10},{7,11},{8,12},{9,13},{1... | collective-permute-start | bytes 258056 | tf_op jit(solution)/shard_map/ppermute | solution.py:505
  52.9 4.9 %collective-permute-start.16 = (bf16[336,128]{1,0:T(8,128)(2,1)S(1)}, bf16[336,128]{1,0:T(8,128)(2,1)S(1)}, u32[]{:S(2)}, u32[]{:S(2)}) collective-permute-start(bf16[336,128]{1,0:T(8,128)(2,1)S(1)} %ring_sum.1.refs_0_), channel_id=1, source_target_pairs={{0,128},{1,33},{2,130},{3,35},{4,132},{5,37},{6,134},{7,39},{8,136... | collective-permute-start | bytes 258056 | tf_op jit(solution)/shard_map/ppermute | solution.py:526
  55.2 3.3 %collective-permute-start.15 = (bf16[336,128]{1,0:T(8,128)(2,1)S(1)}, bf16[336,128]{1,0:T(8,128)(2,1)S(1)}, u32[]{:S(2)}, u32[]{:S(2)}) collective-permute-start(bf16[336,128]{1,0:T(8,128)(2,1)S(1)} %ring_sum.1.refs_0_), channel_id=1, source_target_pairs={{0,192},{1,49},{2,194},{3,51},{4,196},{5,53},{6,198},{7,55},{8,200... | collective-permute-start | bytes 258056 | tf_op jit(solution)/shard_map/ppermute | solution.py:526
  56.4 4.8 %collective-permute-start.14 = (bf16[336,128]{1,0:T(8,128)(2,1)S(1)}, bf16[336,128]{1,0:T(8,128)(2,1)S(1)}, u32[]{:S(2)}, u32[]{:S(2)}) collective-permute-start(bf16[336,128]{1,0:T(8,128)(2,1)S(1)} %ring_sum.1.refs_0_), channel_id=1, source_target_pairs={{0,64},{1,17},{2,66},{3,19},{4,68},{5,21},{6,70},{7,23},{8,72},{9,... | collective-permute-start | bytes 258056 | tf_op jit(solution)/shard_map/ppermute | solution.py:526
  61.2 12.4 %collective-permute-start.19 = (bf16[1344,128]{1,0:T(8,128)(2,1)S(1)}, bf16[1344,128]{1,0:T(8,128)(2,1)S(1)}, u32[]{:S(2)}, u32[]{:S(2)}) collective-permute-start(bf16[1344,128]{1,0:T(8,128)(2,1)S(1)} %join.1.refs_0_), channel_id=1, source_target_pairs={{0,32},{1,129},{2,34},{3,131},{4,36},{5,133},{6,38},{7,135},{8,40}... | collective-permute-start | bytes 1032200 | tf_op jit(solution)/shard_map/ppermute | solution.py:526
  61.4 12.2 %collective-permute-start.18 = (bf16[1344,128]{1,0:T(8,128)(2,1)S(1)}, bf16[1344,128]{1,0:T(8,128)(2,1)S(1)}, u32[]{:S(2)}, u32[]{:S(2)}) collective-permute-start(bf16[1344,128]{1,0:T(8,128)(2,1)S(1)} %join.1.refs_0_), channel_id=1, source_target_pairs={{0,48},{1,193},{2,50},{3,195},{4,52},{5,197},{6,54},{7,199},{8,56}... | collective-permute-start | bytes 1032200 | tf_op jit(solution)/shard_map/ppermute | solution.py:526
  63.0 10.6 %collective-permute-start.17 = (bf16[1344,128]{1,0:T(8,128)(2,1)S(1)}, bf16[1344,128]{1,0:T(8,128)(2,1)S(1)}, u32[]{:S(2)}, u32[]{:S(2)}) collective-permute-start(bf16[1344,128]{1,0:T(8,128)(2,1)S(1)} %join.1.refs_0_), channel_id=1, source_target_pairs={{0,16},{1,65},{2,18},{3,67},{4,20},{5,69},{6,22},{7,71},{8,24},{9,... | collective-permute-start | bytes 1032200 | tf_op jit(solution)/shard_map/ppermute | solution.py:526
  64.0 17.4 %collective-permute-start.20 = (bf16[1344,128]{1,0:T(8,128)(2,1)S(1)}, bf16[1344,128]{1,0:T(8,128)(2,1)S(1)}, u32[]{:S(2)}, u32[]{:S(2)}) collective-permute-start(bf16[1344,128]{1,0:T(8,128)(2,1)S(1)} %join.1.refs_0_), channel_id=1, source_target_pairs={{0,1},{1,0},{2,3},{3,2},{4,5},{5,4},{6,7},{7,6},{8,9},{9,8},{10,11... | collective-permute-start | bytes 1032200 | tf_op jit(solution)/shard_map/ppermute | solution.py:505
  73.6 9.6 %collective-permute-start.23 = (bf16[1344,128]{1,0:T(8,128)(2,1)S(1)}, bf16[1344,128]{1,0:T(8,128)(2,1)S(1)}, u32[]{:S(2)}, u32[]{:S(2)}) collective-permute-start(bf16[1344,128]{1,0:T(8,128)(2,1)S(1)} %collective-permute-done.19.refs_3_), channel_id=1, source_target_pairs={{0,1},{1,0},{2,3},{3,2},{4,5},{5,4},{6,7},{7,6},{8,9},{9,8},{10,11... | collective-permute-start | bytes 1032200 | tf_op jit(solution)/shard_map/ppermute | solution.py:505
  80.9 2.4 %collective-permute-start.22 = (bf16[1344,128]{1,0:T(8,128)(2,1)S(1)}, bf16[1344,128]{1,0:T(8,128)(2,1)S(1)}, u32[]{:S(2)}, u32[]{:S(2)}) collective-permute-start(bf16[1344,128]{1,0:T(8,128)(2,1)S(1)} %collective-permute-done.18.refs_2_), channel_id=1, source_target_pairs={{0,1},{1,0},{2,3},{3,2},{4,5},{5,4},{6,7},{7,6},{8,9},{9,8},{10,11... | collective-permute-start | bytes 1032200 | tf_op jit(solution)/shard_map/ppermute | solution.py:505
  81.0 2.3 %collective-permute-start.21 = (bf16[1344,128]{1,0:T(8,128)(2,1)S(1)}, bf16[1344,128]{1,0:T(8,128)(2,1)S(1)}, u32[]{:S(2)}, u32[]{:S(2)}) collective-permute-start(bf16[1344,128]{1,0:T(8,128)(2,1)S(1)} %collective-permute-done.17.refs_1_), channel_id=1, source_target_pairs={{0,1},{1,0},{2,3},{3,2},{4,5},{5,4},{6,7},{7,6},{8,9},{9,8},{10,11... | collective-permute-start | bytes 1032200 | tf_op jit(solution)/shard_map/ppermute | solution.py:505

commit v3 on v2

--- a/solution.py
+++ b/solution.py
@@ -130,6 +130,15 @@
         tile_ref[h] = skewed[:, :total]
     for copy in copies[2:]:
         copy.wait()
+
+
+def square_index():
+    batch = lax.axis_index("batch")
+    z_size = lax.axis_size("batch") // 8
+    y = batch // (2 * z_size)
+    z = lax.rem(batch // 2, z_size)
+    bit = lambda place: lax.rem((place + 1) // 2, 2)
+    return 2 * bit(y) + bit(z)
 
 
 def place_pieces(refs, target, size):
@@ -346,18 +355,19 @@
 def after_core_kernel(keep_ref, got_ref, small_ref, own_ref, *others):
     half = keep_ref.shape[0] // 5
     part = half // 4
-    y = lax.axis_index("batch") // (lax.axis_size("batch") // 4)
+    index = square_index()
     for ref, step in zip((own_ref,) + others, STEPS):
-        there = lax.rem(y + step, 4)
+        there = jnp.bitwise_xor(index, step)
         for b in range(5):
             place = pl.ds(pl.multiple_of(b * half + there * part, part), part)
             ref[b * part : (b + 1) * part, :] = (
                 keep_ref[place, :] + got_ref[place, :].astype(F32)
             ).astype(ref.dtype)
-        ref[5 * part :, :] = small_ref[...].astype(ref.dtype)
-
-
-def after_y_kernel(own_ref, one_ref, three_ref, two_ref, sum_ref):
+        small = jnp.where(there == 0, small_ref[...], 0.0)
+        ref[5 * part :, :] = small.astype(ref.dtype)
+
+
+def square_sum_kernel(own_ref, one_ref, three_ref, two_ref, sum_ref):
     body = own_ref.shape[0] - 16
     got = lambda ref, place: ref[place, :].astype(F32)
     for place, own in (
@@ -373,10 +383,10 @@
     sum_ref[...] = (left_ref[...].astype(F32) + right_ref[...].astype(F32)).astype(BF)
 
 
-def ring_sum_kernel(own_ref, two_ref, six_ref, four_ref, sum_ref):
+def four_sum_kernel(own_ref, one_ref, three_ref, two_ref, sum_ref):
     sum_ref[...] = (
-        (own_ref[...].astype(F32) + four_ref[...].astype(F32))
-        + (two_ref[...].astype(F32) + six_ref[...].astype(F32))
+        (own_ref[...].astype(F32) + two_ref[...].astype(F32))
+        + (one_ref[...].astype(F32) + three_ref[...].astype(F32))
     ).astype(BF)
 
 
@@ -397,22 +407,22 @@
     batch = lax.axis_index("batch")
     core = lax.rem(batch, 2)
     x = lax.axis_index("seq")
-    y = batch // (lax.axis_size("batch") // 4)
+    index = square_index()
     copies = []
     for n, (ref, (other, second)) in enumerate(zip(blocks, sources)):
         from_core = 1 - core if other else core
-        x_first = from_core == 0
+        x_first = from_core == 1
         for m, first in enumerate(STEPS):
             slot = n * 4 + m
             from_x = lax.rem(x + 4 - jnp.where(x_first, first, second), 4)
-            from_y = lax.rem(y + 4 - jnp.where(x_first, second, first), 4)
+            from_index = jnp.bitwise_xor(index, jnp.where(x_first, second, first))
             start = m * size
             for b in range(4):
                 wide_s[slot, :, b * block : (b + 1) * block] = (
                     ref[start + b * part : start + (b + 1) * part, :].astype(F32) * factor
                 )
             narrow_s[slot] = ref[start + 4 * part : start + 5 * part, :].astype(F32) * factor
-            place = pl.ds(pl.multiple_of((from_core * 4 + from_y) * part, part), part)
+            place = pl.ds(pl.multiple_of((from_core * 4 + from_index) * part, part), part)
             for copy in (
                 pltpu.make_async_copy(
                     wide_s.at[slot],
@@ -444,18 +454,17 @@
     core = lax.rem(lax.axis_index("batch"), 2)
 
     def piece(ref, first):
-        place = (first + 1) * size
-        return ref[place - 16 : place, :].astype(F32)
+        return ref[(first + 1) * size - 16 : (first + 1) * size, :].astype(F32)
 
     def over_x(own, x_first):
-        by_first = [piece(own[0], n) for n in range(4)]
-        by_second = [piece(own[n], 0) for n in range(4)]
+        by_first = [sum(piece(ref, n) for ref in own) for n in range(4)]
+        by_second = [sum(piece(ref, n) for n in range(4)) for ref in own]
         zero, one, three, two = [
             jnp.where(x_first, left, right) for left, right in zip(by_first, by_second)
         ]
         return (zero + two) + (one + three)
 
-    summed = (over_x(blocks[:4], core == 0) + over_x(blocks[4:], core == 1)) * factor
+    summed = (over_x(blocks[:4], core == 1) + over_x(blocks[4:], core == 0)) * factor
     bias_ref[...] = summed[:4, :]
     in_gain_ref[...] = summed[4:8, :]
     out_gain_ref[...] = summed[8:12, :]
@@ -504,11 +513,15 @@
             pairs.append((b, (y * z_size + z) * 2 + c))
         return lax.ppermute(values, "batch", pairs)
 
-    def along_y(values, step):
-        return along_batch(values, lambda y, z, c: ((y + step) % 4, z, c))
-
-    def along_z(values, step):
-        return along_batch(values, lambda y, z, c: (y, (z + step) % z_size, c))
+    def in_square(y, z, step):
+        return y ^ (step // 2), z ^ (step % 2)
+
+    def in_shifted_square(y, z, step):
+        y, z = in_square(y + 1, z + 1, step)
+        return (y - 1) % 4, (z - 1) % z_size
+
+    def far(z):
+        return (z + (5 if z % 2 else 3)) % z_size
 
     def across(values):
         return along_batch(values, lambda y, z, c: (y, z, 1 - c))
@@ -518,10 +531,13 @@
         for x in range(seq_size):
             for b in range(batch_size):
                 y, z, c = place_of(b)
-                to_x = (x + step) % 4 if c == x_core else x
-                to_y = y if c == x_core else (y + step) % 4
+                to_x, to_y, to_z = x, y, z
+                if c == x_core:
+                    to_x = (x + step) % 4
+                else:
+                    to_y, to_z = in_square(y, z, step)
                 pairs.append(
-                    (x * batch_size + b, to_x * batch_size + (to_y * z_size + z) * 2 + c)
+                    (x * batch_size + b, to_x * batch_size + (to_y * z_size + to_z) * 2 + c)
                 )
         return lax.ppermute(values, ("seq", "batch"), pairs)
 
@@ -532,7 +548,6 @@
     own_history = history[0]
     own_cotangent = out_cotangent[0]
     pieces = [along_x(own_history, step) for step in STEPS[1:]]
-    cot_pieces = [along_x(own_cotangent, step) for step in STEPS[1:]]
     own, own_cot, in_gain, gain, uvqk, out_w, tile, onehot = pl.pallas_call(
         prepare_kernel,
         out_shape=[
@@ -570,6 +585,7 @@
             )
         ]
     )
+    cot_pieces = [along_x(own_cot, step) for step in STEPS[1:]]
     scaled, gate, slope, vqk, weights, score_slope, mixed = pl.pallas_call(
         functools.partial(forward_kernel, seq_size),
         out_shape=[
@@ -647,20 +663,29 @@
         compiler_params=params(SMALL),
         name="after_core",
     )(keep, got, small)
-    parts = [along_y(values, step) for values, step in zip(parts, STEPS[1:])]
+    parts = [
+        along_batch(values, lambda y, z, c: (*in_square(y, z, step), c))
+        for values, step in zip(parts, STEPS[1:])
+    ]
     summed = pl.pallas_call(
-        after_y_kernel, out_shape=shape(chunk, BF), compiler_params=params(SMALL), name="after_y"
+        square_sum_kernel,
+        out_shape=shape(chunk, BF),
+        compiler_params=params(SMALL),
+        name="square_sum",
     )(mine, *parts)
-    other = along_batch(summed, lambda y, z, c: (y, z ^ 1, c))
+    parts = [
+        along_batch(summed, lambda y, z, c: (*in_shifted_square(y, z, step), c))
+        for step in STEPS[1:]
+    ]
+    summed = pl.pallas_call(
+        four_sum_kernel, out_shape=shape(chunk, BF), compiler_params=params(SMALL), name="four_sum"
+    )(summed, *parts)
+    other = along_batch(summed, lambda y, z, c: (y, far(z), c))
     summed = pl.pallas_call(
         pair_sum_kernel, out_shape=shape(chunk, BF), compiler_params=params(SMALL), name="pair_sum"
     )(summed, other)
-    ring = [along_z(summed, step) for step in (2, 6, 4)]
-    summed = pl.pallas_call(
-        ring_sum_kernel, out_shape=shape(chunk, BF), compiler_params=params(SMALL), name="ring_sum"
-    )(summed, *ring)
-
-    blocks = [along_either(summed, step, 0) for step in STEPS[1:]]
+
+    blocks = [along_either(summed, step, 1) for step in STEPS[1:]]
     joined = pl.pallas_call(
         join_kernel,
         out_shape=shape((4 * size, buckets), BF),
@@ -691,7 +716,7 @@
             name="unpack",
         )(*blocks, *kept)
 
-    moved = {step: along_either(joined, step, 1) for step in STEPS[1:]}
+    moved = {step: along_either(joined, step, 0) for step in STEPS[1:]}
     kept = unpack_call(((False, 0),), ())
     again, kept = lax.optimization_barrier((joined, kept))
     others[0] = across(again)

time: 85.7 us -> 81.6 us (0.952)
  starting transfers between devices: 45 us -> 37.5 us
  waiting for transfers between devices: 20 us -> 23.5 us
    ppermute x12, starting transfers between devices: 31.4 us -> 24 us  [along_batch(): return lax.ppermute(values, 'batch', pairs)]
    ppermute x6, waiting for transfers between devices: 4.57 us -> 7.8 us  [along_either(): return lax.ppermute(values, ('seq', 'batch'), pairs)]
    ppermute x12, waiting for transfers between devices: 11 us -> 12.5 us  [along_batch(): return lax.ppermute(values, 'batch', pairs)]
    ppermute x6, waiting for transfers between devices: 4.44 us -> 3.17 us  [along_x(): lax.ppermute(values, 'seq', [(i, (i + step) % seq_size) for i in range(se...]
  transfers between devices with their start and end apart: 24 -> 24, of which waited for: 9 -> 10; matrix products, arithmetic and copies ran while one was open for 0% -> 0% of each run, Pallas kernels for 13% -> 14%
where the time goes in v3:
time: 81.6 us; the launch traced here: 81.5 us
  starting transfers between devices  37.5 us (46%)
  waiting for transfers between devices  23.5 us (29%)
  Pallas kernels  18.9 us (23%)
  between operations  1.61 us (2%)
    ppermute x12, starting transfers between devices, along_batch(): return lax.ppermute(values, 'batch', pairs)  24 us
    ppermute x12, waiting for transfers between devices, along_batch(): return lax.ppermute(values, 'batch', pairs)  12.5 us
    ppermute x6, starting transfers between devices, along_x(): lax.ppermute(values, 'seq', [(i, (i + step) % seq_size) for i in range(se...  8.18 us
    ppermute x6, waiting for transfers between devices, along_either(): return lax.ppermute(values, ('seq', 'batch'), pairs)  7.8 us
    pallas_call x1, Pallas kernels, shards(): pl.pallas_call(functools.partial(backward_kernel, seq_size), out_shape=[s...  5.5 us
    ppermute x6, starting transfers between devices, along_either(): return lax.ppermute(values, ('seq', 'batch'), pairs)  5.37 us
    pallas_call x3, Pallas kernels, unpack_call(): pl.pallas_call(functools.partial(last_kernel if last else unpack_kernel,...  4.89 us
    pallas_call x1, Pallas kernels, shards(): pl.pallas_call(functools.partial(forward_kernel, seq_size), out_shape=[sh...  4.58 us
  transfers between devices with their start and end apart: 24, of which 10 were waited for; matrix products, arithmetic and copies ran while one was open for 0% of the time, Pallas kernels for 14%

profile of v3, /device:TPU:1, one launch (start us, length us, event | category | flops | bytes accessed | tf_op | source)
XLA Modules:
  0.0 81.5 jit_solution(16038617778687965175)
XLA Ops:
  0.6 3.7 %collective-permute-start.5 = (bf16[128,512]{1,0:T(8,128)(2,1)}, bf16[128,512]{1,0:T(8,128)(2,1)S(1)}, u32[]{:S(2)}, u32[]{:S(2)}) collective-permute-start(bf16[128,512]{1,0:T(8,128)(2,1)} %bitcast.10), channel_id=1, source_target_pairs={{0,128},{64,192},{128,0},{192,64},{1,129},{65,193},{129,1},{193,65... | collective-permute-start | bytes 393224 | tf_op jit(solution)/shard_map/ppermute | solution.py:504
  4.3 0.9 %collective-permute-start.4 = (bf16[128,512]{1,0:T(8,128)(2,1)}, bf16[128,512]{1,0:T(8,128)(2,1)S(1)}, u32[]{:S(2)}, u32[]{:S(2)}) collective-permute-start(bf16[128,512]{1,0:T(8,128)(2,1)} %bitcast.11), channel_id=1, source_target_pairs={{0,192},{64,0},{128,64},{192,128},{1,193},{65,1},{129,65},{193,129... | collective-permute-start | bytes 393224 | tf_op jit(solution)/shard_map/ppermute | solution.py:504
  5.8 1.9 %prepare.1 = (bf16[128,512]{1,0:T(8,128)(2,1)S(1)}, bf16[128,512]{1,0:T(8,128)(2,1)S(1)}, f32[1,512]{1,0:T(1,128)S(1)}, f32[1,512]{1,0:T(1,128)S(1)}, bf16[512,2...) custom-call(s32[1,512]{1,0:T(1,128)} %bitcast.16, ...), custom_call_target="tpu_custom_call" | custom-call | flops 1000000000 | bytes 3000000 | tf_op jit(solution)/shard_map/prepare/pallas_call | solution.py:551
  7.7 0.7 collective-permute-start.2
  8.4 2.1 %collective-permute-start.1 = (bf16[128,512]{1,0:T(8,128)(2,1)S(1)}, bf16[128,512]{1,0:T(8,128)(2,1)S(1)}, u32[]{:S(2)}, u32[]{:S(2)}) collective-permute-start(bf16[128,512]{1,0:T(8,128)(2,1)S(1)} %get-tuple-element.57.refs_0_.own_cot_ref), channel_id=1, source_target_pairs={{0,192},{64,0},{128,64},{192,128},{1,193},{65,1},{129,65},{193,129... | collective-permute-start | bytes 393224 | tf_op jit(solution)/shard_map/ppermute | solution.py:504
  11.4 3.2 %collective-permute-done.3.refs_1_ = bf16[128,512]{1,0:T(8,128)(2,1)S(1)} collective-permute-done((bf16[128,512]{1,0:T(8,128)(2,1)}, bf16[128,512]{1,0:T(8,128)(2,1)S(1)}, u32[]{:S(2)}, u32[]{:S(2)}) %collective-permute-start.3) | collective-permute-done | bytes 131104 | tf_op jit(solution)/shard_map/ppermute | solution.py:504
  14.6 4.6 %forward.1 = (bf16[512,512]{1,0:T(8,128)(2,1)S(1)}, f32[512,512]{1,0:T(8,128)S(1)}, f32[4,512,512]{2,1,0:T(8,128)S(1)}, bf16[3,512,512]{2,1,0:T(8,128)(2,1)S(1)}...) custom-call(bf16[128,512]{1,0:T(8,128)(2,1)S(1)} %get-tuple-element.56.refs_0_.own_ref, ...), custom_call_target="tpu_custom_call" | custom-call | flops 4000000000 | bytes 10000000 | tf_op jit(solution)/shard_map/forward/pallas_call | solution.py:589
  19.2 5.5 %backward.1 = (bf16[1280,128]{1,0:T(8,128)(2,1)S(1)}, f32[1280,128]{1,0:T(8,128)S(1)}, bf16[128,512]{1,0:T(8,128)(2,1)S(1)}, bf16[4,128,512]{2,1,0:T(8,128)(2,1)...) custom-call(s32[1]{0:T(128)S(6)} %copy.24.length_ref, ...), custom_call_target="tpu_custom_call" | custom-call | flops 4000000000 | bytes 10000000 | tf_op jit(solution)/shard_map/backward/pallas_call | solution.py:607
  24.7 1.9 %collective-permute-start.6 = (bf16[1280,128]{1,0:T(8,128)(2,1)S(1)}, bf16[1280,128]{1,0:T(8,128)(2,1)S(1)}, u32[]{:S(2)}, u32[]{:S(2)}) collective-permute-start(bf16[1280,128]{1,0:T(8,128)(2,1)S(1)} %get-tuple-element.78), channel_id=1, source_target_pairs={{0,1},{1,0},{2,3},{3,2},{4,5},{5,4},{6,7},{7,6},{8,9},{9,8},{10,11... | collective-permute-start | bytes 983048 | tf_op jit(solution)/shard_map/ppermute | solution.py:514
  26.6 1.8 %rows.1 = (bf16[128,512]{1,0:T(8,128)(2,1)}, bf16[128,512]{1,0:T(8,128)(2,1)}, f32[16,128]{1,0:T(8,128)S(1)}) custom-call(bf16[128,512]{1,0:T(8,128)(2,1)S(1)} %get-tuple-element.56.refs_0_.own_ref, bf16[128,512]{1,0:T(8,128)(2,1)S(1)} %get-tuple-element.57.refs_0_.own_cot_ref, f32[1,512]{1,0:T(1,128)S(1)} %get-tuple-element.58.refs_5_.in_gain_ref, ...), custom_call_target="tpu_custom_call" | custom-call | flops 1000000000 | bytes 3000000 | tf_op jit(solution)/shard_map/rows/pallas_call | solution.py:645
  28.9 1.1 %collective-permute-start.8 = (bf16[336,128]{1,0:T(8,128)(2,1)S(1)}, bf16[336,128]{1,0:T(8,128)(2,1)S(1)}, u32[]{:S(2)}, u32[]{:S(2)}) collective-permute-start(bf16[336,128]{1,0:T(8,128)(2,1)S(1)} %get-tuple-element.82), channel_id=1, source_target_pairs={{0,18},{1,19},{2,16},{3,17},{4,22},{5,23},{6,20},{7,21},{8,26},{9,... | collective-permute-start | bytes 258056 | tf_op jit(solution)/shard_map/ppermute | solution.py:514
  30.0 1.3 %collective-permute-start.9 = (bf16[336,128]{1,0:T(8,128)(2,1)S(1)}, bf16[336,128]{1,0:T(8,128)(2,1)S(1)}, u32[]{:S(2)}, u32[]{:S(2)}) collective-permute-start(bf16[336,128]{1,0:T(8,128)(2,1)S(1)} %get-tuple-element.83), channel_id=1, source_target_pairs={{0,16},{1,17},{2,18},{3,19},{4,20},{5,21},{6,22},{7,23},{8,24},{9,... | collective-permute-start | bytes 258056 | tf_op jit(solution)/shard_map/ppermute | solution.py:514
  31.3 1.5 %collective-permute-done.7.one_ref = bf16[336,128]{1,0:T(8,128)(2,1)S(1)} collective-permute-done((bf16[336,128]{1,0:T(8,128)(2,1)S(1)}, bf16[336,128]{1,0:T(8,128)(2,1)S(1)}, u32[]{:S(2)}, u32[]{:S(2)}) %collective-permute-start.7) | collective-permute-done | bytes 86048 | tf_op jit(solution)/shard_map/ppermute | solution.py:514
  32.8 1.8 %collective-permute-done.8.three_ref = bf16[336,128]{1,0:T(8,128)(2,1)S(1)} collective-permute-done((bf16[336,128]{1,0:T(8,128)(2,1)S(1)}, bf16[336,128]{1,0:T(8,128)(2,1)S(1)}, u32[]{:S(2)}, u32[]{:S(2)}) %collective-permute-start.8) | collective-permute-done | bytes 86048 | tf_op jit(solution)/shard_map/ppermute | solution.py:514
  34.6 1.4 %collective-permute-done.9.two_ref = bf16[336,128]{1,0:T(8,128)(2,1)S(1)} collective-permute-done((bf16[336,128]{1,0:T(8,128)(2,1)S(1)}, bf16[336,128]{1,0:T(8,128)(2,1)S(1)}, u32[]{:S(2)}, u32[]{:S(2)}) %collective-permute-start.9) | collective-permute-done | bytes 86048 | tf_op jit(solution)/shard_map/ppermute | solution.py:514
  36.1 1.7 %collective-permute-start.12 = (bf16[336,128]{1,0:T(8,128)(2,1)S(1)}, bf16[336,128]{1,0:T(8,128)(2,1)S(1)}, u32[]{:S(2)}, u32[]{:S(2)}) collective-permute-start(bf16[336,128]{1,0:T(8,128)(2,1)S(1)} %square_sum.1.own_ref), channel_id=1, source_target_pairs={{0,48},{1,49},{2,50},{3,51},{4,52},{5,53},{6,54},{7,55},{8,56},{9,... | collective-permute-start | bytes 258056 | tf_op jit(solution)/shard_map/ppermute | solution.py:514
  37.7 6.0 %collective-permute-start.11 = (bf16[336,128]{1,0:T(8,128)(2,1)S(1)}, bf16[336,128]{1,0:T(8,128)(2,1)S(1)}, u32[]{:S(2)}, u32[]{:S(2)}) collective-permute-start(bf16[336,128]{1,0:T(8,128)(2,1)S(1)} %square_sum.1.own_ref), channel_id=1, source_target_pairs={{0,62},{1,63},{2,52},{3,53},{4,50},{5,51},{6,56},{7,57},{8,54},{9,... | collective-permute-start | bytes 258056 | tf_op jit(solution)/shard_map/ppermute | solution.py:514
  43.7 1.9 %collective-permute-done.11.three_ref = bf16[336,128]{1,0:T(8,128)(2,1)S(1)} collective-permute-done((bf16[336,128]{1,0:T(8,128)(2,1)S(1)}, bf16[336,128]{1,0:T(8,128)(2,1)S(1)}, u32[]{:S(2)}, u32[]{:S(2)}) %collective-permute-start.11) | collective-permute-done | bytes 86048 | tf_op jit(solution)/shard_map/ppermute | solution.py:514
  45.6 2.7 %collective-permute-done.10.one_ref = bf16[336,128]{1,0:T(8,128)(2,1)S(1)} collective-permute-done((bf16[336,128]{1,0:T(8,128)(2,1)S(1)}, bf16[336,128]{1,0:T(8,128)(2,1)S(1)}, u32[]{:S(2)}, u32[]{:S(2)}) %collective-permute-start.10) | collective-permute-done | bytes 86048 | tf_op jit(solution)/shard_map/ppermute | solution.py:514
  48.3 2.0 %collective-permute-start.13 = (bf16[336,128]{1,0:T(8,128)(2,1)S(1)}, bf16[336,128]{1,0:T(8,128)(2,1)S(1)}, u32[]{:S(2)}, u32[]{:S(2)}) collective-permute-start(bf16[336,128]{1,0:T(8,128)(2,1)S(1)} %four_sum.1.left_ref), channel_id=1, source_target_pairs={{0,6},{1,7},{2,12},{3,13},{4,10},{5,11},{6,0},{7,1},{8,14},{9,15},... | collective-permute-start | bytes 258056 | tf_op jit(solution)/shard_map/ppermute | solution.py:514
  50.3 3.2 %collective-permute-done.13.right_ref = bf16[336,128]{1,0:T(8,128)(2,1)S(1)} collective-permute-done((bf16[336,128]{1,0:T(8,128)(2,1)S(1)}, bf16[336,128]{1,0:T(8,128)(2,1)S(1)}, u32[]{:S(2)}, u32[]{:S(2)}) %collective-permute-start.13) | collective-permute-done | bytes 86048 | tf_op jit(solution)/shard_map/ppermute | solution.py:514
  53.6 1.0 %collective-permute-start.16 = (bf16[336,128]{1,0:T(8,128)(2,1)S(1)}, bf16[336,128]{1,0:T(8,128)(2,1)S(1)}, u32[]{:S(2)}, u32[]{:S(2)}) collective-permute-start(bf16[336,128]{1,0:T(8,128)(2,1)S(1)} %pair_sum.1.refs_0_), channel_id=1, source_target_pairs={{0,16},{1,129},{2,18},{3,131},{4,20},{5,133},{6,22},{7,135},{8,24}... | collective-permute-start | bytes 258056 | tf_op jit(solution)/shard_map/ppermute | solution.py:542
  54.5 1.7 %collective-permute-start.15 = (bf16[336,128]{1,0:T(8,128)(2,1)S(1)}, bf16[336,128]{1,0:T(8,128)(2,1)S(1)}, u32[]{:S(2)}, u32[]{:S(2)}) collective-permute-start(bf16[336,128]{1,0:T(8,128)(2,1)S(1)} %pair_sum.1.refs_0_), channel_id=1, source_target_pairs={{0,18},{1,193},{2,16},{3,195},{4,22},{5,197},{6,20},{7,199},{8,26}... | collective-permute-start | bytes 258056 | tf_op jit(solution)/shard_map/ppermute | solution.py:542
  56.2 2.3 %collective-permute-done.16.refs_3_ = bf16[336,128]{1,0:T(8,128)(2,1)S(1)} collective-permute-done((bf16[336,128]{1,0:T(8,128)(2,1)S(1)}, bf16[336,128]{1,0:T(8,128)(2,1)S(1)}, u32[]{:S(2)}, u32[]{:S(2)}) %collective-permute-start.16) | collective-permute-done | bytes 86048 | tf_op jit(solution)/shard_map/ppermute | solution.py:542
  58.5 2.2 %collective-permute-done.14.refs_1_ = bf16[336,128]{1,0:T(8,128)(2,1)S(1)} collective-permute-done((bf16[336,128]{1,0:T(8,128)(2,1)S(1)}, bf16[336,128]{1,0:T(8,128)(2,1)S(1)}, u32[]{:S(2)}, u32[]{:S(2)}) %collective-permute-start.14) | collective-permute-done | bytes 86048 | tf_op jit(solution)/shard_map/ppermute | solution.py:542
  61.1 2.4 %collective-permute-start.17 = (bf16[1344,128]{1,0:T(8,128)(2,1)S(1)}, bf16[1344,128]{1,0:T(8,128)(2,1)S(1)}, u32[]{:S(2)}, u32[]{:S(2)}) collective-permute-start(bf16[1344,128]{1,0:T(8,128)(2,1)S(1)} %join.1.refs_0_), channel_id=1, source_target_pairs={{0,64},{1,3},{2,66},{3,1},{4,68},{5,7},{6,70},{7,5},{8,72},{9,11},... | collective-permute-start | bytes 1032200 | tf_op jit(solution)/shard_map/ppermute | solution.py:542
  63.5 0.9 %unpack.3 = (f32[512,2048]{1,0:T(8,128)}, f32[512,512]{1,0:T(8,128)}) custom-call(bf16[1344,128]{1,0:T(8,128)(2,1)S(1)} %join.1.refs_0_), custom_call_target="tpu_custom_call" | custom-call | flops 10000000000 | bytes 1000000 | tf_op jit(solution)/shard_map/unpack/pallas_call | solution.py:703
  64.4 4.5 %collective-permute-start.20 = (bf16[1344,128]{1,0:T(8,128)(2,1)S(1)}, bf16[1344,128]{1,0:T(8,128)(2,1)S(1)}, u32[]{:S(2)}, u32[]{:S(2)}) collective-permute-start(bf16[1344,128]{1,0:T(8,128)(2,1)S(1)} %join.1.refs_0_), channel_id=1, source_target_pairs={{0,1},{1,0},{2,3},{3,2},{4,5},{5,4},{6,7},{7,6},{8,9},{9,8},{10,11... | collective-permute-start | bytes 1032200 | tf_op jit(solution)/shard_map/ppermute | solution.py:514
  68.9 3.3 %collective-permute-done.17.refs_1_ = bf16[1344,128]{1,0:T(8,128)(2,1)S(1)} collective-permute-done((bf16[1344,128]{1,0:T(8,128)(2,1)S(1)}, bf16[1344,128]{1,0:T(8,128)(2,1)S(1)}, u32[]{:S(2)}, u32[]{:S(2)}) %collective-permute-start.17) | collective-permute-done | bytes 344096 | tf_op jit(solution)/shard_map/ppermute | solution.py:542
  72.2 4.7 %collective-permute-start.23 = (bf16[1344,128]{1,0:T(8,128)(2,1)S(1)}, bf16[1344,128]{1,0:T(8,128)(2,1)S(1)}, u32[]{:S(2)}, u32[]{:S(2)}) collective-permute-start(bf16[1344,128]{1,0:T(8,128)(2,1)S(1)} %collective-permute-done.19.refs_3_), channel_id=1, source_target_pairs={{0,1},{1,0},{2,3},{3,2},{4,5},{5,4},{6,7},{7,6},{8,9},{9,8},{10,11... | collective-permute-start | bytes 1032200 | tf_op jit(solution)/shard_map/ppermute | solution.py:514
  77.3 1.8 %unpack.4 = (f32[512,2048]{1,0:T(8,128)}, f32[512,512]{1,0:T(8,128)}) custom-call(bf16[1344,128]{1,0:T(8,128)(2,1)S(1)} %collective-permute-done.20.refs_0_.refs_4_, bf16[1344,128]{1,0:T(8,128)(2,1)S(1)} %collective-permute-done.17.refs_1_, bf16[1344,128]{1,0:T(8,128)(2,1)S(1)} %collective-permute-done.18.refs_2_, ...), custom_call_target="tpu_custom_call", output_to_operand_aliasing={{0}: (4, {}), {1}: (5, {})} | custom-call | flops 10000000000 | bytes 4000000 | tf_op jit(solution)/shard_map/unpack/pallas_call | solution.py:703
  79.2 2.1 %unpack.5 = (f32[512,2048]{1,0:T(8,128)}, f32[512,512]{1,0:T(8,128)}, f32[4,128]{1,0:T(4,128)}, f32[4,128]{1,0:T(4,128)}, f32[4,128]{1,0:T(4,128)}) custom-call(bf16[1344,128]{1,0:T(8,128)(2,1)S(1)} %join.1.refs_0_, bf16[1344,128]{1,0:T(8,128)(2,1)S(1)} %collective-permute-done.17.refs_1_, ...), custom_call_target="tpu_custom_call", output_to_operand_aliasing={{0}: (8, {}), {1}: (9, {})} | custom-call | flops 10000000000 | bytes 3000000 | tf_op jit(solution)/shard_map/unpack/pallas_call | solution.py:703
  (28 shorter events, 2.3 us)
Async XLA Ops:
  0.6 10.5 %collective-permute-start.5 = (bf16[128,512]{1,0:T(8,128)(2,1)}, bf16[128,512]{1,0:T(8,128)(2,1)S(1)}, u32[]{:S(2)}, u32[]{:S(2)}) collective-permute-start(bf16[128,512]{1,0:T(8,128)(2,1)} %bitcast.10), channel_id=1, source_target_pairs={{0,128},{64,192},{128,0},{192,64},{1,129},{65,193},{129,1},{193,65... | collective-permute-start | bytes 393224 | tf_op jit(solution)/shard_map/ppermute | solution.py:504
  4.3 7.1 %collective-permute-start.4 = (bf16[128,512]{1,0:T(8,128)(2,1)}, bf16[128,512]{1,0:T(8,128)(2,1)S(1)}, u32[]{:S(2)}, u32[]{:S(2)}) collective-permute-start(bf16[128,512]{1,0:T(8,128)(2,1)} %bitcast.11), channel_id=1, source_target_pairs={{0,192},{64,0},{128,64},{192,128},{1,193},{65,1},{129,65},{193,129... | collective-permute-start | bytes 393224 | tf_op jit(solution)/shard_map/ppermute | solution.py:504
  5.2 9.4 %collective-permute-start.3 = (bf16[128,512]{1,0:T(8,128)(2,1)}, bf16[128,512]{1,0:T(8,128)(2,1)S(1)}, u32[]{:S(2)}, u32[]{:S(2)}) collective-permute-start(bf16[128,512]{1,0:T(8,128)(2,1)} %bitcast.12), channel_id=1, source_target_pairs={{0,64},{64,128},{128,192},{192,0},{1,65},{65,129},{129,193},{193,1... | collective-permute-start | bytes 393224 | tf_op jit(solution)/shard_map/ppermute | solution.py:504
  7.7 11.5 %collective-permute-start.2 = (bf16[128,512]{1,0:T(8,128)(2,1)S(1)}, bf16[128,512]{1,0:T(8,128)(2,1)S(1)}, u32[]{:S(2)}, u32[]{:S(2)}) collective-permute-start(bf16[128,512]{1,0:T(8,128)(2,1)S(1)} %get-tuple-element.57.refs_0_.own_cot_ref), channel_id=1, source_target_pairs={{0,128},{64,192},{128,0},{192,64},{1,129},{65,193},{129,1},{193,65... | collective-permute-start | bytes 393224 | tf_op jit(solution)/shard_map/ppermute | solution.py:504
  8.4 10.8 %collective-permute-start.1 = (bf16[128,512]{1,0:T(8,128)(2,1)S(1)}, bf16[128,512]{1,0:T(8,128)(2,1)S(1)}, u32[]{:S(2)}, u32[]{:S(2)}) collective-permute-start(bf16[128,512]{1,0:T(8,128)(2,1)S(1)} %get-tuple-element.57.refs_0_.own_cot_ref), channel_id=1, source_target_pairs={{0,192},{64,0},{128,64},{192,128},{1,193},{65,1},{129,65},{193,129... | collective-permute-start | bytes 393224 | tf_op jit(solution)/shard_map/ppermute | solution.py:504
  11.1 8.0 %collective-permute-start = (bf16[128,512]{1,0:T(8,128)(2,1)S(1)}, bf16[128,512]{1,0:T(8,128)(2,1)S(1)}, u32[]{:S(2)}, u32[]{:S(2)}) collective-permute-start(bf16[128,512]{1,0:T(8,128)(2,1)S(1)} %get-tuple-element.57.refs_0_.own_cot_ref), channel_id=1, source_target_pairs={{0,64},{64,128},{128,192},{192,0},{1,65},{65,129},{129,193},{193,1... | collective-permute-start | bytes 393224 | tf_op jit(solution)/shard_map/ppermute | solution.py:504
  24.7 3.8 %collective-permute-start.6 = (bf16[1280,128]{1,0:T(8,128)(2,1)S(1)}, bf16[1280,128]{1,0:T(8,128)(2,1)S(1)}, u32[]{:S(2)}, u32[]{:S(2)}) collective-permute-start(bf16[1280,128]{1,0:T(8,128)(2,1)S(1)} %get-tuple-element.78), channel_id=1, source_target_pairs={{0,1},{1,0},{2,3},{3,2},{4,5},{5,4},{6,7},{7,6},{8,9},{9,8},{10,11... | collective-permute-start | bytes 983048 | tf_op jit(solution)/shard_map/ppermute | solution.py:514
  28.5 4.2 %collective-permute-start.7 = (bf16[336,128]{1,0:T(8,128)(2,1)S(1)}, bf16[336,128]{1,0:T(8,128)(2,1)S(1)}, u32[]{:S(2)}, u32[]{:S(2)}) collective-permute-start(bf16[336,128]{1,0:T(8,128)(2,1)S(1)} %get-tuple-element.81), channel_id=1, source_target_pairs={{0,2},{1,3},{2,0},{3,1},{4,6},{5,7},{6,4},{7,5},{8,10},{9,11},{10,... | collective-permute-start | bytes 258056 | tf_op jit(solution)/shard_map/ppermute | solution.py:514
  28.9 5.7 %collective-permute-start.8 = (bf16[336,128]{1,0:T(8,128)(2,1)S(1)}, bf16[336,128]{1,0:T(8,128)(2,1)S(1)}, u32[]{:S(2)}, u32[]{:S(2)}) collective-permute-start(bf16[336,128]{1,0:T(8,128)(2,1)S(1)} %get-tuple-element.82), channel_id=1, source_target_pairs={{0,18},{1,19},{2,16},{3,17},{4,22},{5,23},{6,20},{7,21},{8,26},{9,... | collective-permute-start | bytes 258056 | tf_op jit(solution)/shard_map/ppermute | solution.py:514
  30.0 6.0 %collective-permute-start.9 = (bf16[336,128]{1,0:T(8,128)(2,1)S(1)}, bf16[336,128]{1,0:T(8,128)(2,1)S(1)}, u32[]{:S(2)}, u32[]{:S(2)}) collective-permute-start(bf16[336,128]{1,0:T(8,128)(2,1)S(1)} %get-tuple-element.83), channel_id=1, source_target_pairs={{0,16},{1,17},{2,18},{3,19},{4,20},{5,21},{6,22},{7,23},{8,24},{9,... | collective-permute-start | bytes 258056 | tf_op jit(solution)/shard_map/ppermute | solution.py:514
  36.1 7.7 %collective-permute-start.12 = (bf16[336,128]{1,0:T(8,128)(2,1)S(1)}, bf16[336,128]{1,0:T(8,128)(2,1)S(1)}, u32[]{:S(2)}, u32[]{:S(2)}) collective-permute-start(bf16[336,128]{1,0:T(8,128)(2,1)S(1)} %square_sum.1.own_ref), channel_id=1, source_target_pairs={{0,48},{1,49},{2,50},{3,51},{4,52},{5,53},{6,54},{7,55},{8,56},{9,... | collective-permute-start | bytes 258056 | tf_op jit(solution)/shard_map/ppermute | solution.py:514
  37.7 7.8 %collective-permute-start.11 = (bf16[336,128]{1,0:T(8,128)(2,1)S(1)}, bf16[336,128]{1,0:T(8,128)(2,1)S(1)}, u32[]{:S(2)}, u32[]{:S(2)}) collective-permute-start(bf16[336,128]{1,0:T(8,128)(2,1)S(1)} %square_sum.1.own_ref), channel_id=1, source_target_pairs={{0,62},{1,63},{2,52},{3,53},{4,50},{5,51},{6,56},{7,57},{8,54},{9,... | collective-permute-start | bytes 258056 | tf_op jit(solution)/shard_map/ppermute | solution.py:514
  43.7 4.5 %collective-permute-start.10 = (bf16[336,128]{1,0:T(8,128)(2,1)S(1)}, bf16[336,128]{1,0:T(8,128)(2,1)S(1)}, u32[]{:S(2)}, u32[]{:S(2)}) collective-permute-start(bf16[336,128]{1,0:T(8,128)(2,1)S(1)} %square_sum.1.own_ref), channel_id=1, source_target_pairs={{0,14},{1,15},{2,4},{3,5},{4,2},{5,3},{6,8},{7,9},{8,6},{9,7},{10,... | collective-permute-start | bytes 258056 | tf_op jit(solution)/shard_map/ppermute | solution.py:514
  48.3 5.2 %collective-permute-start.13 = (bf16[336,128]{1,0:T(8,128)(2,1)S(1)}, bf16[336,128]{1,0:T(8,128)(2,1)S(1)}, u32[]{:S(2)}, u32[]{:S(2)}) collective-permute-start(bf16[336,128]{1,0:T(8,128)(2,1)S(1)} %four_sum.1.left_ref), channel_id=1, source_target_pairs={{0,6},{1,7},{2,12},{3,13},{4,10},{5,11},{6,0},{7,1},{8,14},{9,15},... | collective-permute-start | bytes 258056 | tf_op jit(solution)/shard_map/ppermute | solution.py:514
  53.6 4.9 %collective-permute-start.16 = (bf16[336,128]{1,0:T(8,128)(2,1)S(1)}, bf16[336,128]{1,0:T(8,128)(2,1)S(1)}, u32[]{:S(2)}, u32[]{:S(2)}) collective-permute-start(bf16[336,128]{1,0:T(8,128)(2,1)S(1)} %pair_sum.1.refs_0_), channel_id=1, source_target_pairs={{0,16},{1,129},{2,18},{3,131},{4,20},{5,133},{6,22},{7,135},{8,24}... | collective-permute-start | bytes 258056 | tf_op jit(solution)/shard_map/ppermute | solution.py:542
  54.5 4.0 %collective-permute-start.15 = (bf16[336,128]{1,0:T(8,128)(2,1)S(1)}, bf16[336,128]{1,0:T(8,128)(2,1)S(1)}, u32[]{:S(2)}, u32[]{:S(2)}) collective-permute-start(bf16[336,128]{1,0:T(8,128)(2,1)S(1)} %pair_sum.1.refs_0_), channel_id=1, source_target_pairs={{0,18},{1,193},{2,16},{3,195},{4,22},{5,197},{6,20},{7,199},{8,26}... | collective-permute-start | bytes 258056 | tf_op jit(solution)/shard_map/ppermute | solution.py:542
  56.2 4.5 %collective-permute-start.14 = (bf16[336,128]{1,0:T(8,128)(2,1)S(1)}, bf16[336,128]{1,0:T(8,128)(2,1)S(1)}, u32[]{:S(2)}, u32[]{:S(2)}) collective-permute-start(bf16[336,128]{1,0:T(8,128)(2,1)S(1)} %pair_sum.1.refs_0_), channel_id=1, source_target_pairs={{0,2},{1,65},{2,0},{3,67},{4,6},{5,69},{6,4},{7,71},{8,10},{9,73},... | collective-permute-start | bytes 258056 | tf_op jit(solution)/shard_map/ppermute | solution.py:542
  60.8 11.4 %collective-permute-start.19 = (bf16[1344,128]{1,0:T(8,128)(2,1)S(1)}, bf16[1344,128]{1,0:T(8,128)(2,1)S(1)}, u32[]{:S(2)}, u32[]{:S(2)}) collective-permute-start(bf16[1344,128]{1,0:T(8,128)(2,1)S(1)} %join.1.refs_0_), channel_id=1, source_target_pairs={{0,128},{1,17},{2,130},{3,19},{4,132},{5,21},{6,134},{7,23},{8,136... | collective-permute-start | bytes 1032200 | tf_op jit(solution)/shard_map/ppermute | solution.py:542
  61.1 11.0 %collective-permute-start.18 = (bf16[1344,128]{1,0:T(8,128)(2,1)S(1)}, bf16[1344,128]{1,0:T(8,128)(2,1)S(1)}, u32[]{:S(2)}, u32[]{:S(2)}) collective-permute-start(bf16[1344,128]{1,0:T(8,128)(2,1)S(1)} %join.1.refs_0_), channel_id=1, source_target_pairs={{0,192},{1,19},{2,194},{3,17},{4,196},{5,23},{6,198},{7,21},{8,200... | collective-permute-start | bytes 1032200 | tf_op jit(solution)/shard_map/ppermute | solution.py:542
  61.1 11.0 %collective-permute-start.17 = (bf16[1344,128]{1,0:T(8,128)(2,1)S(1)}, bf16[1344,128]{1,0:T(8,128)(2,1)S(1)}, u32[]{:S(2)}, u32[]{:S(2)}) collective-permute-start(bf16[1344,128]{1,0:T(8,128)(2,1)S(1)} %join.1.refs_0_), channel_id=1, source_target_pairs={{0,64},{1,3},{2,66},{3,1},{4,68},{5,7},{6,70},{7,5},{8,72},{9,11},... | collective-permute-start | bytes 1032200 | tf_op jit(solution)/shard_map/ppermute | solution.py:542
  64.4 12.9 %collective-permute-start.20 = (bf16[1344,128]{1,0:T(8,128)(2,1)S(1)}, bf16[1344,128]{1,0:T(8,128)(2,1)S(1)}, u32[]{:S(2)}, u32[]{:S(2)}) collective-permute-start(bf16[1344,128]{1,0:T(8,128)(2,1)S(1)} %join.1.refs_0_), channel_id=1, source_target_pairs={{0,1},{1,0},{2,3},{3,2},{4,5},{5,4},{6,7},{7,6},{8,9},{9,8},{10,11... | collective-permute-start | bytes 1032200 | tf_op jit(solution)/shard_map/ppermute | solution.py:514
  72.2 7.0 %collective-permute-start.23 = (bf16[1344,128]{1,0:T(8,128)(2,1)S(1)}, bf16[1344,128]{1,0:T(8,128)(2,1)S(1)}, u32[]{:S(2)}, u32[]{:S(2)}) collective-permute-start(bf16[1344,128]{1,0:T(8,128)(2,1)S(1)} %collective-permute-done.19.refs_3_), channel_id=1, source_target_pairs={{0,1},{1,0},{2,3},{3,2},{4,5},{5,4},{6,7},{7,6},{8,9},{9,8},{10,11... | collective-permute-start | bytes 1032200 | tf_op jit(solution)/shard_map/ppermute | solution.py:514
  76.8 2.4 %collective-permute-start.22 = (bf16[1344,128]{1,0:T(8,128)(2,1)S(1)}, bf16[1344,128]{1,0:T(8,128)(2,1)S(1)}, u32[]{:S(2)}, u32[]{:S(2)}) collective-permute-start(bf16[1344,128]{1,0:T(8,128)(2,1)S(1)} %collective-permute-done.18.refs_2_), channel_id=1, source_target_pairs={{0,1},{1,0},{2,3},{3,2},{4,5},{5,4},{6,7},{7,6},{8,9},{9,8},{10,11... | collective-permute-start | bytes 1032200 | tf_op jit(solution)/shard_map/ppermute | solution.py:514
  76.9 2.3 %collective-permute-start.21 = (bf16[1344,128]{1,0:T(8,128)(2,1)S(1)}, bf16[1344,128]{1,0:T(8,128)(2,1)S(1)}, u32[]{:S(2)}, u32[]{:S(2)}) collective-permute-start(bf16[1344,128]{1,0:T(8,128)(2,1)S(1)} %collective-permute-done.17.refs_1_), channel_id=1, source_target_pairs={{0,1},{1,0},{2,3},{3,2},{4,5},{5,4},{6,7},{7,6},{8,9},{9,8},{10,11... | collective-permute-start | bytes 1032200 | tf_op jit(solution)/shard_map/ppermute | solution.py:514

commit v4 on v3

--- a/solution.py
+++ b/solution.py
@@ -15,6 +15,9 @@
 SMALL = 12 * 1024 * 1024
 STEPS = (0, 1, 3, 2)
 UNPACK_FLOPS = 10**10
+FORWARD_GROUP = 4
+BACKWARD_GROUP = 2
+KEYS = 2
 HIDDEN = -1e9
 
 
@@ -171,32 +174,35 @@
     scale = 1.0 / math.sqrt(head_dim)
     in_gain = in_gain_ref[...]
     place_pieces(pieces, hist_s, size)
-    for i in range(size):
-        here = slice(i * rows, (i + 1) * rows)
-        ends = (i + 1) * rows
-        first = total - ends
-        normed, _ = normalize(hist_s[here, :].astype(F32))
-        scaled = (normed * in_gain).astype(BF)
-        scaled_ref[here, :] = scaled
-        for part in range(4):
-            projected = dot_nn(scaled, uvqk_ref[:, part * width : (part + 1) * width])
-            sig = sigmoid(projected)
-            activated = projected * sig
-            slope_ref[part, here, :] = sig + activated * (1.0 - sig)
-            if part == 0:
-                gate_ref[here, :] = activated
-            else:
-                vqk_ref[part - 1, here, :] = activated.astype(BF)
+    normed, _ = normalize(hist_s[...].astype(F32))
+    scaled_ref[...] = (normed * in_gain).astype(BF)
+    for part in (2, 3, 1, 0):
+        projected = dot_nn(scaled_ref[...], uvqk_ref[:, part * width : (part + 1) * width])
+        sig = sigmoid(projected)
+        activated = projected * sig
+        slope_ref[part] = sig + activated * (1.0 - sig)
+        if part == 0:
+            gate_ref[...] = activated
+        else:
+            vqk_ref[part - 1] = activated.astype(BF)
+    for i in range(0, size, FORWARD_GROUP):
+        here = slice(i * rows, (i + FORWARD_GROUP) * rows)
+        ends = (i + FORWARD_GROUP) * rows
         for h in range(heads):
             lanes = slice(h * head_dim, (h + 1) * head_dim)
-            scores = dot_nt(vqk_ref[1, here, lanes], vqk_ref[2, :ends, lanes]) * scale
-            scores = scores + tile_ref[h, :, first:]
-            sig = sigmoid(scores)
-            weights = scores * sig
-            score_slope_ref[h, here, :ends] = sig + weights * (1.0 - sig)
-            weights_low = weights.astype(BF)
-            weights_ref[h, here, :ends] = weights_low
-            mixed_ref[here, lanes] = dot_nn(weights_low, vqk_ref[0, :ends, lanes])
+            raw = dot_nt(vqk_ref[1, here, lanes], vqk_ref[2, :ends, lanes])
+            for n in range(FORWARD_GROUP):
+                block = slice((i + n) * rows, (i + n + 1) * rows)
+                seen = (i + n + 1) * rows
+                scores = raw[n * rows : (n + 1) * rows, :seen] * scale
+                scores = scores + tile_ref[h, :, total - seen :]
+                sig = sigmoid(scores)
+                weights = scores * sig
+                score_slope_ref[h, block, :seen] = sig + weights * (1.0 - sig)
+                weights_ref[h, block, :seen] = weights.astype(BF)
+                if n < FORWARD_GROUP - 1:
+                    weights_ref[h, block, seen:ends] = jnp.zeros((rows, ends - seen), BF)
+            mixed_ref[here, lanes] = dot_nn(weights_ref[h, here, :ends], vqk_ref[0, :ends, lanes])
 
 
 def backward_kernel(size, length_ref, *refs):
@@ -222,6 +228,7 @@
         grads_s,
         grad_mixed_s,
         proj_grad_s,
+        grad_gated_s,
     ) = refs[size:]
     rows, width = pieces[0].shape
     total = rows * size
@@ -236,35 +243,40 @@
     grad_out_gain = jnp.zeros((1, width), F32)
     for h in range(heads):
         diag_ref[h] = jnp.zeros((rows, total), F32)
-    for i in range(size):
-        here = slice(i * rows, (i + 1) * rows)
-        ends = (i + 1) * rows
-        first = total - ends
-        valid = (lax.broadcasted_iota(jnp.int32, (rows, 1), 0) + i * rows) < length
+    grad_gated_s[...] = dot_nt(cot_s[...], out_w_ref[...])
+    for i in range(0, size, BACKWARD_GROUP):
+        here = slice(i * rows, (i + BACKWARD_GROUP) * rows)
+        ends = (i + BACKWARD_GROUP) * rows
+        valid = (lax.broadcasted_iota(jnp.int32, (BACKWARD_GROUP * rows, 1), 0) + i * rows) < length
         mixed = jnp.where(valid, mixed_ref[here, :], 0.0)
         mixed_normed, inv_mixed = normalize(mixed)
         gating = gate_ref[here, :]
         gated_s[here, :] = (mixed_normed * out_gain * gating).astype(BF)
-        grad_gated = dot_nt(cot_s[here, :], out_w_ref[...])
+        grad_gated = grad_gated_s[here, :]
         times_normed = grad_gated * mixed_normed
         grad_out_gain = grad_out_gain + jnp.sum(times_normed * gating, axis=0, keepdims=True)
         proj_grad_s[0, here, :] = (times_normed * out_gain * slope_ref[0, here, :]).astype(BF)
         grad_mixed = norm_backward(grad_gated * out_gain * gating, mixed_normed, inv_mixed)
-        grad_mixed_low = jnp.where(valid, grad_mixed, 0.0).astype(BF)
-        grad_mixed_s[here, :] = grad_mixed_low
+        grad_mixed_s[here, :] = jnp.where(valid, grad_mixed, 0.0).astype(BF)
         for h in range(heads):
             lanes = slice(h * head_dim, (h + 1) * head_dim)
-            grad_weights = dot_nt(grad_mixed_low[:, lanes], vqk_ref[0, :ends, lanes])
-            grad_scores = grad_weights * score_slope_ref[h, here, :ends]
-            diag_ref[h, :, first:] += grad_scores
-            grad_scores_low = grad_scores.astype(BF)
-            grads_s[h, here, :ends] = grad_scores_low
-            grad_query = dot_nn(grad_scores_low, vqk_ref[2, :ends, lanes]) * scale
+            grad_weights = dot_nt(grad_mixed_s[here, lanes], vqk_ref[0, :ends, lanes])
+            for n in range(BACKWARD_GROUP):
+                block = slice((i + n) * rows, (i + n + 1) * rows)
+                seen = (i + n + 1) * rows
+                grad_scores = (
+                    grad_weights[n * rows : (n + 1) * rows, :seen] * score_slope_ref[h, block, :seen]
+                )
+                diag_ref[h, :, total - seen :] += grad_scores
+                grads_s[h, block, :seen] = grad_scores.astype(BF)
+                if n < BACKWARD_GROUP - 1:
+                    grads_s[h, block, seen:ends] = jnp.zeros((rows, ends - seen), BF)
+            grad_query = dot_nn(grads_s[h, here, :ends], vqk_ref[2, :ends, lanes]) * scale
             proj_grad_s[2, here, lanes] = (grad_query * slope_ref[2, here, lanes]).astype(BF)
     gain_ref[...] = grad_out_gain
 
-    for j in range(size):
-        here = slice(j * rows, (j + 1) * rows)
+    for j in range(0, size, KEYS):
+        here = slice(j * rows, (j + KEYS) * rows)
         later = slice(j * rows, total)
         for h in range(heads):
             lanes = slice(h * head_dim, (h + 1) * head_dim)
@@ -293,36 +305,31 @@
 
 
 def rows_kernel(
-    own_ref,
-    own_cot_ref,
-    in_gain_ref,
-    uvqk_ref,
-    out_w_ref,
-    own_gated_ref,
-    own_grad_ref,
-    diag_ref,
-    gain_ref,
-    onehot_ref,
-    output_ref,
-    grad_input_ref,
-    small_ref,
+    own_ref, own_cot_ref, in_gain_ref, out_w_ref, own_gated_ref, scaled_ref, output_ref, grad_ref
+):
+    wide = own_ref[...].astype(F32)
+    normed, inv_in = normalize(wide)
+    grad_normed = scaled_ref[...] * in_gain_ref[...]
+    grad_input = own_cot_ref[...].astype(F32) + norm_backward(grad_normed, normed, inv_in)
+    grad_ref[...] = grad_input.astype(BF)
+    output_ref[...] = (wide + dot_nn(own_gated_ref[...], out_w_ref[...])).astype(BF)
+
+
+def small_kernel(
+    own_ref, uvqk_ref, own_grad_ref, diag_ref, gain_ref, onehot_ref, scaled_ref, small_ref
 ):
     rows, width = own_ref.shape
     heads, _, total = diag_ref.shape
     buckets, span = onehot_ref.shape
     me = lax.axis_index("seq")
-    in_gain = in_gain_ref[...]
-    wide = own_ref[...].astype(F32)
-    normed, inv_in = normalize(wide)
+    normed, _ = normalize(own_ref[...].astype(F32))
     grad_scaled = jnp.zeros((rows, width), F32)
     for part in range(4):
         grad_scaled = grad_scaled + dot_nt(
             own_grad_ref[part], uvqk_ref[:, part * width : (part + 1) * width]
         )
     grad_in_gain = jnp.sum(grad_scaled * normed, axis=0, keepdims=True)
-    grad_input = own_cot_ref[...].astype(F32) + norm_backward(grad_scaled * in_gain, normed, inv_in)
-    grad_input_ref[...] = grad_input.astype(BF)
-    output_ref[...] = (wide + dot_nn(own_gated_ref[...], out_w_ref[...])).astype(BF)
+    scaled_ref[...] = grad_scaled
 
     onehot = onehot_ref[...]
     bias_sums = []
@@ -622,6 +629,7 @@
             pltpu.VMEM((heads, total, total), BF),
             pltpu.VMEM((total, width), BF),
             pltpu.VMEM((4, total, width), BF),
+            pltpu.VMEM((total, width), F32),
         ],
         compiler_params=params(LARGE),
         cost_estimate=cost(4 * 10**9, 10**7),
@@ -642,17 +650,13 @@
     )
 
     got = across(send)
-    output, grad_input, small = pl.pallas_call(
-        rows_kernel,
-        out_shape=[
-            shape((rows, width), BF),
-            shape((rows, width), BF),
-            shape((16, buckets), F32),
-        ],
+    grad_scaled, small = pl.pallas_call(
+        small_kernel,
+        out_shape=[shape((rows, width), F32), shape((16, buckets), F32)],
         compiler_params=params(SMALL),
         cost_estimate=cost(10**9, 3 * 10**6),
-        name="rows",
-    )(own, own_cot, in_gain, uvqk, out_w, own_gated, own_grad, diag, gain_term, onehot)
+        name="small",
+    )(own, uvqk, own_grad, diag, gain_term, onehot)
 
     part = half // 4
     size = 5 * part + 16
@@ -663,6 +667,14 @@
         compiler_params=params(SMALL),
         name="after_core",
     )(keep, got, small)
+    grad_scaled, mine, *parts = lax.optimization_barrier((grad_scaled, mine, *parts))
+    output, grad_input = pl.pallas_call(
+        rows_kernel,
+        out_shape=[shape((rows, width), BF), shape((rows, width), BF)],
+        compiler_params=params(SMALL),
+        cost_estimate=cost(2 * 10**9, 3 * 10**6),
+        name="rows",
+    )(own, own_cot, in_gain, out_w, own_gated, grad_scaled)
     parts = [
         along_batch(values, lambda y, z, c: (*in_square(y, z, step), c))
         for values, step in zip(parts, STEPS[1:])

time: 81.6 us -> 79.6 us (0.975)
  Pallas kernels: 18.9 us -> 16.8 us
  starting transfers between devices: 37.5 us -> 38.7 us
  waiting for transfers between devices: 23.5 us -> 22.4 us
    ppermute x6, waiting for transfers between devices: 7.8 us -> 5.5 us  [along_either(): return lax.ppermute(values, ('seq', 'batch'), pairs)]
    ppermute x12, starting transfers between devices: 24 us -> 25.5 us  [along_batch(): return lax.ppermute(values, 'batch', pairs)]
    pallas_call x1, Pallas kernels: 5.5 us -> 4.27 us  [shards(): pl.pallas_call(functools.partial(backward_kernel, seq_size), out_shape=[s...]
    pallas_call x1, Pallas kernels: 4.58 us -> 3.39 us  [shards(): pl.pallas_call(functools.partial(forward_kernel, seq_size), out_shape=[sh...]
    ppermute x12, waiting for transfers between devices: 12.5 us -> 13.6 us  [along_batch(): return lax.ppermute(values, 'batch', pairs)]
    pallas_call x0 -> x1, Pallas kernels: none -> 1.14 us  [shards(): pl.pallas_call(small_kernel, out_shape=[shape((rows, width), F32), shape(...]
    pallas_call x1, Pallas kernels: 1.84 us -> 0.99 us  [shards(): pl.pallas_call(rows_kernel, out_shape=[shape((rows, width), BF), shape((r...]
  transfers between devices with their start and end apart: 24 -> 24, of which waited for: 10 -> 11; matrix products, arithmetic and copies ran while one was open for 0% -> 0% of each run, Pallas kernels for 14% -> 13%
where the time goes in v4:
time: 79.6 us; the launch traced here: 79.5 us
  starting transfers between devices  38.7 us (49%)
  waiting for transfers between devices  22.4 us (28%)
  Pallas kernels  16.8 us (21%)
  between operations  1.6 us (2%)
    ppermute x12, starting transfers between devices, along_batch(): return lax.ppermute(values, 'batch', pairs)  25.5 us
    ppermute x12, waiting for transfers between devices, along_batch(): return lax.ppermute(values, 'batch', pairs)  13.6 us
    ppermute x6, starting transfers between devices, along_x(): lax.ppermute(values, 'seq', [(i, (i + step) % seq_size) for i in range(se...  8 us
    ppermute x6, waiting for transfers between devices, along_either(): return lax.ppermute(values, ('seq', 'batch'), pairs)  5.5 us
    ppermute x6, starting transfers between devices, along_either(): return lax.ppermute(values, ('seq', 'batch'), pairs)  5.19 us
    pallas_call x3, Pallas kernels, unpack_call(): pl.pallas_call(functools.partial(last_kernel if last else unpack_kernel,...  4.89 us
    pallas_call x1, Pallas kernels, shards(): pl.pallas_call(functools.partial(backward_kernel, seq_size), out_shape=[s...  4.27 us
    pallas_call x1, Pallas kernels, shards(): pl.pallas_call(functools.partial(forward_kernel, seq_size), out_shape=[sh...  3.39 us
  transfers between devices with their start and end apart: 24, of which 11 were waited for; matrix products, arithmetic and copies ran while one was open for 0% of the time, Pallas kernels for 13%

profile of v4, /device:TPU:1, one launch (start us, length us, event | category | flops | bytes accessed | tf_op | source)
XLA Modules:
  0.0 79.5 jit_solution(17747193550265440280)
XLA Ops:
  0.6 3.7 %collective-permute-start.5 = (bf16[128,512]{1,0:T(8,128)(2,1)}, bf16[128,512]{1,0:T(8,128)(2,1)S(1)}, u32[]{:S(2)}, u32[]{:S(2)}) collective-permute-start(bf16[128,512]{1,0:T(8,128)(2,1)} %bitcast.10), channel_id=1, source_target_pairs={{0,128},{64,192},{128,0},{192,64},{1,129},{65,193},{129,1},{193,65... | collective-permute-start | bytes 393224 | tf_op jit(solution)/shard_map/ppermute | solution.py:511
  4.3 0.9 %collective-permute-start.4 = (bf16[128,512]{1,0:T(8,128)(2,1)}, bf16[128,512]{1,0:T(8,128)(2,1)S(1)}, u32[]{:S(2)}, u32[]{:S(2)}) collective-permute-start(bf16[128,512]{1,0:T(8,128)(2,1)} %bitcast.11), channel_id=1, source_target_pairs={{0,192},{64,0},{128,64},{192,128},{1,193},{65,1},{129,65},{193,129... | collective-permute-start | bytes 393224 | tf_op jit(solution)/shard_map/ppermute | solution.py:511
  5.8 1.9 %prepare.1 = (bf16[128,512]{1,0:T(8,128)(2,1)S(1)}, bf16[128,512]{1,0:T(8,128)(2,1)S(1)}, f32[1,512]{1,0:T(1,128)S(1)}, f32[1,512]{1,0:T(1,128)S(1)}, bf16[512,2...) custom-call(s32[1,512]{1,0:T(1,128)} %bitcast.14, ...), custom_call_target="tpu_custom_call" | custom-call | flops 1000000000 | bytes 3000000 | tf_op jit(solution)/shard_map/prepare/pallas_call | solution.py:558
  8.4 2.1 %collective-permute-start.1 = (bf16[128,512]{1,0:T(8,128)(2,1)S(1)}, bf16[128,512]{1,0:T(8,128)(2,1)S(1)}, u32[]{:S(2)}, u32[]{:S(2)}) collective-permute-start(bf16[128,512]{1,0:T(8,128)(2,1)S(1)} %get-tuple-element.63.refs_0_.own_cot_ref), channel_id=1, source_target_pairs={{0,192},{64,0},{128,64},{192,128},{1,193},{65,1},{129,65},{193,129... | collective-permute-start | bytes 393224 | tf_op jit(solution)/shard_map/ppermute | solution.py:511
  11.2 3.2 %collective-permute-done.3.refs_1_ = bf16[128,512]{1,0:T(8,128)(2,1)S(1)} collective-permute-done((bf16[128,512]{1,0:T(8,128)(2,1)}, bf16[128,512]{1,0:T(8,128)(2,1)S(1)}, u32[]{:S(2)}, u32[]{:S(2)}) %collective-permute-start.3) | collective-permute-done | bytes 131104 | tf_op jit(solution)/shard_map/ppermute | solution.py:511
  14.5 3.4 %forward.1 = (bf16[512,512]{1,0:T(8,128)(2,1)S(1)}, f32[512,512]{1,0:T(8,128)S(1)}, f32[4,512,512]{2,1,0:T(8,128)S(1)}, bf16[3,512,512]{2,1,0:T(8,128)(2,1)S(1)}...) custom-call(bf16[128,512]{1,0:T(8,128)(2,1)S(1)} %get-tuple-element.62.refs_0_.own_ref, ...), custom_call_target="tpu_custom_call" | custom-call | flops 4000000000 | bytes 10000000 | tf_op jit(solution)/shard_map/forward/pallas_call | solution.py:596
  17.9 4.3 %backward.1 = (bf16[1280,128]{1,0:T(8,128)(2,1)S(1)}, f32[1280,128]{1,0:T(8,128)S(1)}, bf16[128,512]{1,0:T(8,128)(2,1)S(1)}, bf16[4,128,512]{2,1,0:T(8,128)(2,1)...) custom-call(s32[1]{0:T(128)S(6)} %copy.24.length_ref, ...), custom_call_target="tpu_custom_call" | custom-call | flops 4000000000 | bytes 10000000 | tf_op jit(solution)/shard_map/backward/pallas_call | solution.py:614
  22.2 2.2 %collective-permute-start.6 = (bf16[1280,128]{1,0:T(8,128)(2,1)S(1)}, bf16[1280,128]{1,0:T(8,128)(2,1)S(1)}, u32[]{:S(2)}, u32[]{:S(2)}) collective-permute-start(bf16[1280,128]{1,0:T(8,128)(2,1)S(1)} %get-tuple-element.83), channel_id=1, source_target_pairs={{0,1},{1,0},{2,3},{3,2},{4,5},{5,4},{6,7},{7,6},{8,9},{9,8},{10,11... | collective-permute-start | bytes 983048 | tf_op jit(solution)/shard_map/ppermute | solution.py:521
  24.4 1.1 %small.1 = (f32[128,512]{1,0:T(8,128)S(1)}, f32[16,128]{1,0:T(8,128)S(1)}) custom-call(bf16[128,512]{1,0:T(8,128)(2,1)S(1)} %get-tuple-element.62.refs_0_.own_ref, bf16[512,2048]{1,0:T(8,128)(2,1)S(1)} %get-tuple-element.68.refs_6_.uvqk_ref, bf16[4,128,512]{2,1,0:T(8,128)(2,1)S(1)} %get-tuple-element.77.own_grad_ref, ...), custom_call_target="tpu_custom_call" | custom-call | flops 1000000000 | bytes 3000000 | tf_op jit(solution)/shard_map/small/pallas_call | solution.py:653
  25.7 1.3 %collective-permute-start.7 = (bf16[336,128]{1,0:T(8,128)(2,1)S(1)}, bf16[336,128]{1,0:T(8,128)(2,1)S(1)}, u32[]{:S(2)}, u32[]{:S(2)}) collective-permute-start(bf16[336,128]{1,0:T(8,128)(2,1)S(1)} %get-tuple-element.93), channel_id=1, source_target_pairs={{0,2},{1,3},{2,0},{3,1},{4,6},{5,7},{6,4},{7,5},{8,10},{9,11},{10,... | collective-permute-start | bytes 258056 | tf_op jit(solution)/shard_map/ppermute | solution.py:521
  27.1 1.1 %collective-permute-start.8 = (bf16[336,128]{1,0:T(8,128)(2,1)S(1)}, bf16[336,128]{1,0:T(8,128)(2,1)S(1)}, u32[]{:S(2)}, u32[]{:S(2)}) collective-permute-start(bf16[336,128]{1,0:T(8,128)(2,1)S(1)} %get-tuple-element.94), channel_id=1, source_target_pairs={{0,18},{1,19},{2,16},{3,17},{4,22},{5,23},{6,20},{7,21},{8,26},{9,... | collective-permute-start | bytes 258056 | tf_op jit(solution)/shard_map/ppermute | solution.py:521
  28.5 1.1 %collective-permute-done.7.one_ref = bf16[336,128]{1,0:T(8,128)(2,1)S(1)} collective-permute-done((bf16[336,128]{1,0:T(8,128)(2,1)S(1)}, bf16[336,128]{1,0:T(8,128)(2,1)S(1)}, u32[]{:S(2)}, u32[]{:S(2)}) %collective-permute-start.7) | collective-permute-done | bytes 86048 | tf_op jit(solution)/shard_map/ppermute | solution.py:521
  29.6 2.8 %collective-permute-done.8.three_ref = bf16[336,128]{1,0:T(8,128)(2,1)S(1)} collective-permute-done((bf16[336,128]{1,0:T(8,128)(2,1)S(1)}, bf16[336,128]{1,0:T(8,128)(2,1)S(1)}, u32[]{:S(2)}, u32[]{:S(2)}) %collective-permute-start.8) | collective-permute-done | bytes 86048 | tf_op jit(solution)/shard_map/ppermute | solution.py:521
  32.4 1.5 %collective-permute-done.9.two_ref = bf16[336,128]{1,0:T(8,128)(2,1)S(1)} collective-permute-done((bf16[336,128]{1,0:T(8,128)(2,1)S(1)}, bf16[336,128]{1,0:T(8,128)(2,1)S(1)}, u32[]{:S(2)}, u32[]{:S(2)}) %collective-permute-start.9) | collective-permute-done | bytes 86048 | tf_op jit(solution)/shard_map/ppermute | solution.py:521
  34.0 1.9 %collective-permute-start.12 = (bf16[336,128]{1,0:T(8,128)(2,1)S(1)}, bf16[336,128]{1,0:T(8,128)(2,1)S(1)}, u32[]{:S(2)}, u32[]{:S(2)}) collective-permute-start(bf16[336,128]{1,0:T(8,128)(2,1)S(1)} %square_sum.1.own_ref), channel_id=1, source_target_pairs={{0,48},{1,49},{2,50},{3,51},{4,52},{5,53},{6,54},{7,55},{8,56},{9,... | collective-permute-start | bytes 258056 | tf_op jit(solution)/shard_map/ppermute | solution.py:521
  35.9 5.6 %collective-permute-start.11 = (bf16[336,128]{1,0:T(8,128)(2,1)S(1)}, bf16[336,128]{1,0:T(8,128)(2,1)S(1)}, u32[]{:S(2)}, u32[]{:S(2)}) collective-permute-start(bf16[336,128]{1,0:T(8,128)(2,1)S(1)} %square_sum.1.own_ref), channel_id=1, source_target_pairs={{0,62},{1,63},{2,52},{3,53},{4,50},{5,51},{6,56},{7,57},{8,54},{9,... | collective-permute-start | bytes 258056 | tf_op jit(solution)/shard_map/ppermute | solution.py:521
  41.5 1.9 %collective-permute-done.11.three_ref = bf16[336,128]{1,0:T(8,128)(2,1)S(1)} collective-permute-done((bf16[336,128]{1,0:T(8,128)(2,1)S(1)}, bf16[336,128]{1,0:T(8,128)(2,1)S(1)}, u32[]{:S(2)}, u32[]{:S(2)}) %collective-permute-start.11) | collective-permute-done | bytes 86048 | tf_op jit(solution)/shard_map/ppermute | solution.py:521
  43.3 2.7 %collective-permute-done.10.one_ref = bf16[336,128]{1,0:T(8,128)(2,1)S(1)} collective-permute-done((bf16[336,128]{1,0:T(8,128)(2,1)S(1)}, bf16[336,128]{1,0:T(8,128)(2,1)S(1)}, u32[]{:S(2)}, u32[]{:S(2)}) %collective-permute-start.10) | collective-permute-done | bytes 86048 | tf_op jit(solution)/shard_map/ppermute | solution.py:521
  46.1 2.0 %collective-permute-start.13 = (bf16[336,128]{1,0:T(8,128)(2,1)S(1)}, bf16[336,128]{1,0:T(8,128)(2,1)S(1)}, u32[]{:S(2)}, u32[]{:S(2)}) collective-permute-start(bf16[336,128]{1,0:T(8,128)(2,1)S(1)} %four_sum.1.left_ref), channel_id=1, source_target_pairs={{0,6},{1,7},{2,12},{3,13},{4,10},{5,11},{6,0},{7,1},{8,14},{9,15},... | collective-permute-start | bytes 258056 | tf_op jit(solution)/shard_map/ppermute | solution.py:521
  48.1 3.5 %collective-permute-done.13.right_ref = bf16[336,128]{1,0:T(8,128)(2,1)S(1)} collective-permute-done((bf16[336,128]{1,0:T(8,128)(2,1)S(1)}, bf16[336,128]{1,0:T(8,128)(2,1)S(1)}, u32[]{:S(2)}, u32[]{:S(2)}) %collective-permute-start.13) | collective-permute-done | bytes 86048 | tf_op jit(solution)/shard_map/ppermute | solution.py:521
  51.6 1.0 %collective-permute-start.16 = (bf16[336,128]{1,0:T(8,128)(2,1)S(1)}, bf16[336,128]{1,0:T(8,128)(2,1)S(1)}, u32[]{:S(2)}, u32[]{:S(2)}) collective-permute-start(bf16[336,128]{1,0:T(8,128)(2,1)S(1)} %pair_sum.1.refs_0_), channel_id=1, source_target_pairs={{0,16},{1,129},{2,18},{3,131},{4,20},{5,133},{6,22},{7,135},{8,24}... | collective-permute-start | bytes 258056 | tf_op jit(solution)/shard_map/ppermute | solution.py:549
  52.6 0.9 %collective-permute-start.15 = (bf16[336,128]{1,0:T(8,128)(2,1)S(1)}, bf16[336,128]{1,0:T(8,128)(2,1)S(1)}, u32[]{:S(2)}, u32[]{:S(2)}) collective-permute-start(bf16[336,128]{1,0:T(8,128)(2,1)S(1)} %pair_sum.1.refs_0_), channel_id=1, source_target_pairs={{0,18},{1,193},{2,16},{3,195},{4,22},{5,197},{6,20},{7,199},{8,26}... | collective-permute-start | bytes 258056 | tf_op jit(solution)/shard_map/ppermute | solution.py:549
  54.1 2.5 %collective-permute-done.16.refs_3_ = bf16[336,128]{1,0:T(8,128)(2,1)S(1)} collective-permute-done((bf16[336,128]{1,0:T(8,128)(2,1)S(1)}, bf16[336,128]{1,0:T(8,128)(2,1)S(1)}, u32[]{:S(2)}, u32[]{:S(2)}) %collective-permute-start.16) | collective-permute-done | bytes 86048 | tf_op jit(solution)/shard_map/ppermute | solution.py:549
  56.5 1.5 %collective-permute-done.14.refs_1_ = bf16[336,128]{1,0:T(8,128)(2,1)S(1)} collective-permute-done((bf16[336,128]{1,0:T(8,128)(2,1)S(1)}, bf16[336,128]{1,0:T(8,128)(2,1)S(1)}, u32[]{:S(2)}, u32[]{:S(2)}) %collective-permute-start.14) | collective-permute-done | bytes 86048 | tf_op jit(solution)/shard_map/ppermute | solution.py:549
  58.3 2.5 %collective-permute-start.17 = (bf16[1344,128]{1,0:T(8,128)(2,1)S(1)}, bf16[1344,128]{1,0:T(8,128)(2,1)S(1)}, u32[]{:S(2)}, u32[]{:S(2)}) collective-permute-start(bf16[1344,128]{1,0:T(8,128)(2,1)S(1)} %join.1.refs_0_), channel_id=1, source_target_pairs={{0,64},{1,3},{2,66},{3,1},{4,68},{5,7},{6,70},{7,5},{8,72},{9,11},... | collective-permute-start | bytes 1032200 | tf_op jit(solution)/shard_map/ppermute | solution.py:549
  60.8 0.9 %unpack.3 = (f32[512,2048]{1,0:T(8,128)}, f32[512,512]{1,0:T(8,128)}) custom-call(bf16[1344,128]{1,0:T(8,128)(2,1)S(1)} %join.1.refs_0_), custom_call_target="tpu_custom_call" | custom-call | flops 10000000000 | bytes 1000000 | tf_op jit(solution)/shard_map/unpack/pallas_call | solution.py:715
  61.7 5.2 %collective-permute-start.20 = (bf16[1344,128]{1,0:T(8,128)(2,1)S(1)}, bf16[1344,128]{1,0:T(8,128)(2,1)S(1)}, u32[]{:S(2)}, u32[]{:S(2)}) collective-permute-start(bf16[1344,128]{1,0:T(8,128)(2,1)S(1)} %join.1.refs_0_), channel_id=1, source_target_pairs={{0,1},{1,0},{2,3},{3,2},{4,5},{5,4},{6,7},{7,6},{8,9},{9,8},{10,11... | collective-permute-start | bytes 1032200 | tf_op jit(solution)/shard_map/ppermute | solution.py:521
  66.9 1.0 %rows.1 = (bf16[128,512]{1,0:T(8,128)(2,1)}, bf16[128,512]{1,0:T(8,128)(2,1)}) custom-call(bf16[128,512]{1,0:T(8,128)(2,1)S(1)} %get-tuple-element.62.refs_0_.own_ref, bf16[128,512]{1,0:T(8,128)(2,1)S(1)} %get-tuple-element.63.refs_0_.own_cot_ref, f32[1,512]{1,0:T(1,128)S(1)} %get-tuple-element.64.refs_5_.in_gain_ref, ...), custom_call_target="tpu_custom_call" | custom-call | flops 2000000000 | bytes 3000000 | tf_op jit(solution)/shard_map/rows/pallas_call | solution.py:671
  67.9 1.5 %collective-permute-done.17.refs_1_ = bf16[1344,128]{1,0:T(8,128)(2,1)S(1)} collective-permute-done((bf16[1344,128]{1,0:T(8,128)(2,1)S(1)}, bf16[1344,128]{1,0:T(8,128)(2,1)S(1)}, u32[]{:S(2)}, u32[]{:S(2)}) %collective-permute-start.17) | collective-permute-done | bytes 344096 | tf_op jit(solution)/shard_map/ppermute | solution.py:549
  69.5 5.4 %collective-permute-start.23 = (bf16[1344,128]{1,0:T(8,128)(2,1)S(1)}, bf16[1344,128]{1,0:T(8,128)(2,1)S(1)}, u32[]{:S(2)}, u32[]{:S(2)}) collective-permute-start(bf16[1344,128]{1,0:T(8,128)(2,1)S(1)} %collective-permute-done.19.refs_3_), channel_id=1, source_target_pairs={{0,1},{1,0},{2,3},{3,2},{4,5},{5,4},{6,7},{7,6},{8,9},{9,8},{10,11... | collective-permute-start | bytes 1032200 | tf_op jit(solution)/shard_map/ppermute | solution.py:521
  75.3 1.8 %unpack.4 = (f32[512,2048]{1,0:T(8,128)}, f32[512,512]{1,0:T(8,128)}) custom-call(bf16[1344,128]{1,0:T(8,128)(2,1)S(1)} %collective-permute-done.20.refs_0_.refs_4_, bf16[1344,128]{1,0:T(8,128)(2,1)S(1)} %collective-permute-done.17.refs_1_, bf16[1344,128]{1,0:T(8,128)(2,1)S(1)} %collective-permute-done.18.refs_2_, ...), custom_call_target="tpu_custom_call", output_to_operand_aliasing={{0}: (4, {}), {1}: (5, {})} | custom-call | flops 10000000000 | bytes 4000000 | tf_op jit(solution)/shard_map/unpack/pallas_call | solution.py:715
  77.2 2.1 %unpack.5 = (f32[512,2048]{1,0:T(8,128)}, f32[512,512]{1,0:T(8,128)}, f32[4,128]{1,0:T(4,128)}, f32[4,128]{1,0:T(4,128)}, f32[4,128]{1,0:T(4,128)}) custom-call(bf16[1344,128]{1,0:T(8,128)(2,1)S(1)} %join.1.refs_0_, bf16[1344,128]{1,0:T(8,128)(2,1)S(1)} %collective-permute-done.17.refs_1_, ...), custom_call_target="tpu_custom_call", output_to_operand_aliasing={{0}: (8, {}), {1}: (9, {})} | custom-call | flops 10000000000 | bytes 3000000 | tf_op jit(solution)/shard_map/unpack/pallas_call | solution.py:715
  (29 shorter events, 3.4 us)
Async XLA Ops:
  0.6 10.5 %collective-permute-start.5 = (bf16[128,512]{1,0:T(8,128)(2,1)}, bf16[128,512]{1,0:T(8,128)(2,1)S(1)}, u32[]{:S(2)}, u32[]{:S(2)}) collective-permute-start(bf16[128,512]{1,0:T(8,128)(2,1)} %bitcast.10), channel_id=1, source_target_pairs={{0,128},{64,192},{128,0},{192,64},{1,129},{65,193},{129,1},{193,65... | collective-permute-start | bytes 393224 | tf_op jit(solution)/shard_map/ppermute | solution.py:511
  4.3 6.9 %collective-permute-start.4 = (bf16[128,512]{1,0:T(8,128)(2,1)}, bf16[128,512]{1,0:T(8,128)(2,1)S(1)}, u32[]{:S(2)}, u32[]{:S(2)}) collective-permute-start(bf16[128,512]{1,0:T(8,128)(2,1)} %bitcast.11), channel_id=1, source_target_pairs={{0,192},{64,0},{128,64},{192,128},{1,193},{65,1},{129,65},{193,129... | collective-permute-start | bytes 393224 | tf_op jit(solution)/shard_map/ppermute | solution.py:511
  5.2 9.3 %collective-permute-start.3 = (bf16[128,512]{1,0:T(8,128)(2,1)}, bf16[128,512]{1,0:T(8,128)(2,1)S(1)}, u32[]{:S(2)}, u32[]{:S(2)}) collective-permute-start(bf16[128,512]{1,0:T(8,128)(2,1)} %bitcast.12), channel_id=1, source_target_pairs={{0,64},{64,128},{128,192},{192,0},{1,65},{65,129},{129,193},{193,1... | collective-permute-start | bytes 393224 | tf_op jit(solution)/shard_map/ppermute | solution.py:511
  7.7 10.2 %collective-permute-start.2 = (bf16[128,512]{1,0:T(8,128)(2,1)S(1)}, bf16[128,512]{1,0:T(8,128)(2,1)S(1)}, u32[]{:S(2)}, u32[]{:S(2)}) collective-permute-start(bf16[128,512]{1,0:T(8,128)(2,1)S(1)} %get-tuple-element.63.refs_0_.own_cot_ref), channel_id=1, source_target_pairs={{0,128},{64,192},{128,0},{192,64},{1,129},{65,193},{129,1},{193,65... | collective-permute-start | bytes 393224 | tf_op jit(solution)/shard_map/ppermute | solution.py:511
  8.4 9.5 %collective-permute-start.1 = (bf16[128,512]{1,0:T(8,128)(2,1)S(1)}, bf16[128,512]{1,0:T(8,128)(2,1)S(1)}, u32[]{:S(2)}, u32[]{:S(2)}) collective-permute-start(bf16[128,512]{1,0:T(8,128)(2,1)S(1)} %get-tuple-element.63.refs_0_.own_cot_ref), channel_id=1, source_target_pairs={{0,192},{64,0},{128,64},{192,128},{1,193},{65,1},{129,65},{193,129... | collective-permute-start | bytes 393224 | tf_op jit(solution)/shard_map/ppermute | solution.py:511
  11.1 6.8 %collective-permute-start = (bf16[128,512]{1,0:T(8,128)(2,1)S(1)}, bf16[128,512]{1,0:T(8,128)(2,1)S(1)}, u32[]{:S(2)}, u32[]{:S(2)}) collective-permute-start(bf16[128,512]{1,0:T(8,128)(2,1)S(1)} %get-tuple-element.63.refs_0_.own_cot_ref), channel_id=1, source_target_pairs={{0,64},{64,128},{128,192},{192,0},{1,65},{65,129},{129,193},{193,1... | collective-permute-start | bytes 393224 | tf_op jit(solution)/shard_map/ppermute | solution.py:511
  22.2 3.5 %collective-permute-start.6 = (bf16[1280,128]{1,0:T(8,128)(2,1)S(1)}, bf16[1280,128]{1,0:T(8,128)(2,1)S(1)}, u32[]{:S(2)}, u32[]{:S(2)}) collective-permute-start(bf16[1280,128]{1,0:T(8,128)(2,1)S(1)} %get-tuple-element.83), channel_id=1, source_target_pairs={{0,1},{1,0},{2,3},{3,2},{4,5},{5,4},{6,7},{7,6},{8,9},{9,8},{10,11... | collective-permute-start | bytes 983048 | tf_op jit(solution)/shard_map/ppermute | solution.py:521
  25.7 3.8 %collective-permute-start.7 = (bf16[336,128]{1,0:T(8,128)(2,1)S(1)}, bf16[336,128]{1,0:T(8,128)(2,1)S(1)}, u32[]{:S(2)}, u32[]{:S(2)}) collective-permute-start(bf16[336,128]{1,0:T(8,128)(2,1)S(1)} %get-tuple-element.93), channel_id=1, source_target_pairs={{0,2},{1,3},{2,0},{3,1},{4,6},{5,7},{6,4},{7,5},{8,10},{9,11},{10,... | collective-permute-start | bytes 258056 | tf_op jit(solution)/shard_map/ppermute | solution.py:521
  27.1 5.3 %collective-permute-start.8 = (bf16[336,128]{1,0:T(8,128)(2,1)S(1)}, bf16[336,128]{1,0:T(8,128)(2,1)S(1)}, u32[]{:S(2)}, u32[]{:S(2)}) collective-permute-start(bf16[336,128]{1,0:T(8,128)(2,1)S(1)} %get-tuple-element.94), channel_id=1, source_target_pairs={{0,18},{1,19},{2,16},{3,17},{4,22},{5,23},{6,20},{7,21},{8,26},{9,... | collective-permute-start | bytes 258056 | tf_op jit(solution)/shard_map/ppermute | solution.py:521
  28.2 5.7 %collective-permute-start.9 = (bf16[336,128]{1,0:T(8,128)(2,1)S(1)}, bf16[336,128]{1,0:T(8,128)(2,1)S(1)}, u32[]{:S(2)}, u32[]{:S(2)}) collective-permute-start(bf16[336,128]{1,0:T(8,128)(2,1)S(1)} %get-tuple-element.95), channel_id=1, source_target_pairs={{0,16},{1,17},{2,18},{3,19},{4,20},{5,21},{6,22},{7,23},{8,24},{9,... | collective-permute-start | bytes 258056 | tf_op jit(solution)/shard_map/ppermute | solution.py:521
  34.0 7.5 %collective-permute-start.12 = (bf16[336,128]{1,0:T(8,128)(2,1)S(1)}, bf16[336,128]{1,0:T(8,128)(2,1)S(1)}, u32[]{:S(2)}, u32[]{:S(2)}) collective-permute-start(bf16[336,128]{1,0:T(8,128)(2,1)S(1)} %square_sum.1.own_ref), channel_id=1, source_target_pairs={{0,48},{1,49},{2,50},{3,51},{4,52},{5,53},{6,54},{7,55},{8,56},{9,... | collective-permute-start | bytes 258056 | tf_op jit(solution)/shard_map/ppermute | solution.py:521
  35.9 7.4 %collective-permute-start.11 = (bf16[336,128]{1,0:T(8,128)(2,1)S(1)}, bf16[336,128]{1,0:T(8,128)(2,1)S(1)}, u32[]{:S(2)}, u32[]{:S(2)}) collective-permute-start(bf16[336,128]{1,0:T(8,128)(2,1)S(1)} %square_sum.1.own_ref), channel_id=1, source_target_pairs={{0,62},{1,63},{2,52},{3,53},{4,50},{5,51},{6,56},{7,57},{8,54},{9,... | collective-permute-start | bytes 258056 | tf_op jit(solution)/shard_map/ppermute | solution.py:521
  41.5 4.5 %collective-permute-start.10 = (bf16[336,128]{1,0:T(8,128)(2,1)S(1)}, bf16[336,128]{1,0:T(8,128)(2,1)S(1)}, u32[]{:S(2)}, u32[]{:S(2)}) collective-permute-start(bf16[336,128]{1,0:T(8,128)(2,1)S(1)} %square_sum.1.own_ref), channel_id=1, source_target_pairs={{0,14},{1,15},{2,4},{3,5},{4,2},{5,3},{6,8},{7,9},{8,6},{9,7},{10,... | collective-permute-start | bytes 258056 | tf_op jit(solution)/shard_map/ppermute | solution.py:521
  46.1 5.5 %collective-permute-start.13 = (bf16[336,128]{1,0:T(8,128)(2,1)S(1)}, bf16[336,128]{1,0:T(8,128)(2,1)S(1)}, u32[]{:S(2)}, u32[]{:S(2)}) collective-permute-start(bf16[336,128]{1,0:T(8,128)(2,1)S(1)} %four_sum.1.left_ref), channel_id=1, source_target_pairs={{0,6},{1,7},{2,12},{3,13},{4,10},{5,11},{6,0},{7,1},{8,14},{9,15},... | collective-permute-start | bytes 258056 | tf_op jit(solution)/shard_map/ppermute | solution.py:521
  51.6 4.9 %collective-permute-start.16 = (bf16[336,128]{1,0:T(8,128)(2,1)S(1)}, bf16[336,128]{1,0:T(8,128)(2,1)S(1)}, u32[]{:S(2)}, u32[]{:S(2)}) collective-permute-start(bf16[336,128]{1,0:T(8,128)(2,1)S(1)} %pair_sum.1.refs_0_), channel_id=1, source_target_pairs={{0,16},{1,129},{2,18},{3,131},{4,20},{5,133},{6,22},{7,135},{8,24}... | collective-permute-start | bytes 258056 | tf_op jit(solution)/shard_map/ppermute | solution.py:549
  52.6 3.9 %collective-permute-start.15 = (bf16[336,128]{1,0:T(8,128)(2,1)S(1)}, bf16[336,128]{1,0:T(8,128)(2,1)S(1)}, u32[]{:S(2)}, u32[]{:S(2)}) collective-permute-start(bf16[336,128]{1,0:T(8,128)(2,1)S(1)} %pair_sum.1.refs_0_), channel_id=1, source_target_pairs={{0,18},{1,193},{2,16},{3,195},{4,22},{5,197},{6,20},{7,199},{8,26}... | collective-permute-start | bytes 258056 | tf_op jit(solution)/shard_map/ppermute | solution.py:549
  53.5 4.5 %collective-permute-start.14 = (bf16[336,128]{1,0:T(8,128)(2,1)S(1)}, bf16[336,128]{1,0:T(8,128)(2,1)S(1)}, u32[]{:S(2)}, u32[]{:S(2)}) collective-permute-start(bf16[336,128]{1,0:T(8,128)(2,1)S(1)} %pair_sum.1.refs_0_), channel_id=1, source_target_pairs={{0,2},{1,65},{2,0},{3,67},{4,6},{5,69},{6,4},{7,71},{8,10},{9,73},... | collective-permute-start | bytes 258056 | tf_op jit(solution)/shard_map/ppermute | solution.py:549
  58.1 11.4 %collective-permute-start.19 = (bf16[1344,128]{1,0:T(8,128)(2,1)S(1)}, bf16[1344,128]{1,0:T(8,128)(2,1)S(1)}, u32[]{:S(2)}, u32[]{:S(2)}) collective-permute-start(bf16[1344,128]{1,0:T(8,128)(2,1)S(1)} %join.1.refs_0_), channel_id=1, source_target_pairs={{0,128},{1,17},{2,130},{3,19},{4,132},{5,21},{6,134},{7,23},{8,136... | collective-permute-start | bytes 1032200 | tf_op jit(solution)/shard_map/ppermute | solution.py:549
  58.2 11.3 %collective-permute-start.18 = (bf16[1344,128]{1,0:T(8,128)(2,1)S(1)}, bf16[1344,128]{1,0:T(8,128)(2,1)S(1)}, u32[]{:S(2)}, u32[]{:S(2)}) collective-permute-start(bf16[1344,128]{1,0:T(8,128)(2,1)S(1)} %join.1.refs_0_), channel_id=1, source_target_pairs={{0,192},{1,19},{2,194},{3,17},{4,196},{5,23},{6,198},{7,21},{8,200... | collective-permute-start | bytes 1032200 | tf_op jit(solution)/shard_map/ppermute | solution.py:549
  58.3 11.2 %collective-permute-start.17 = (bf16[1344,128]{1,0:T(8,128)(2,1)S(1)}, bf16[1344,128]{1,0:T(8,128)(2,1)S(1)}, u32[]{:S(2)}, u32[]{:S(2)}) collective-permute-start(bf16[1344,128]{1,0:T(8,128)(2,1)S(1)} %join.1.refs_0_), channel_id=1, source_target_pairs={{0,64},{1,3},{2,66},{3,1},{4,68},{5,7},{6,70},{7,5},{8,72},{9,11},... | collective-permute-start | bytes 1032200 | tf_op jit(solution)/shard_map/ppermute | solution.py:549
  61.7 13.6 %collective-permute-start.20 = (bf16[1344,128]{1,0:T(8,128)(2,1)S(1)}, bf16[1344,128]{1,0:T(8,128)(2,1)S(1)}, u32[]{:S(2)}, u32[]{:S(2)}) collective-permute-start(bf16[1344,128]{1,0:T(8,128)(2,1)S(1)} %join.1.refs_0_), channel_id=1, source_target_pairs={{0,1},{1,0},{2,3},{3,2},{4,5},{5,4},{6,7},{7,6},{8,9},{9,8},{10,11... | collective-permute-start | bytes 1032200 | tf_op jit(solution)/shard_map/ppermute | solution.py:521
  69.5 7.7 %collective-permute-start.23 = (bf16[1344,128]{1,0:T(8,128)(2,1)S(1)}, bf16[1344,128]{1,0:T(8,128)(2,1)S(1)}, u32[]{:S(2)}, u32[]{:S(2)}) collective-permute-start(bf16[1344,128]{1,0:T(8,128)(2,1)S(1)} %collective-permute-done.19.refs_3_), channel_id=1, source_target_pairs={{0,1},{1,0},{2,3},{3,2},{4,5},{5,4},{6,7},{7,6},{8,9},{9,8},{10,11... | collective-permute-start | bytes 1032200 | tf_op jit(solution)/shard_map/ppermute | solution.py:521
  74.8 2.4 %collective-permute-start.22 = (bf16[1344,128]{1,0:T(8,128)(2,1)S(1)}, bf16[1344,128]{1,0:T(8,128)(2,1)S(1)}, u32[]{:S(2)}, u32[]{:S(2)}) collective-permute-start(bf16[1344,128]{1,0:T(8,128)(2,1)S(1)} %collective-permute-done.18.refs_2_), channel_id=1, source_target_pairs={{0,1},{1,0},{2,3},{3,2},{4,5},{5,4},{6,7},{7,6},{8,9},{9,8},{10,11... | collective-permute-start | bytes 1032200 | tf_op jit(solution)/shard_map/ppermute | solution.py:521
  74.9 2.3 %collective-permute-start.21 = (bf16[1344,128]{1,0:T(8,128)(2,1)S(1)}, bf16[1344,128]{1,0:T(8,128)(2,1)S(1)}, u32[]{:S(2)}, u32[]{:S(2)}) collective-permute-start(bf16[1344,128]{1,0:T(8,128)(2,1)S(1)} %collective-permute-done.17.refs_1_), channel_id=1, source_target_pairs={{0,1},{1,0},{2,3},{3,2},{4,5},{5,4},{6,7},{7,6},{8,9},{9,8},{10,11... | collective-permute-start | bytes 1032200 | tf_op jit(solution)/shard_map/ppermute | solution.py:521

commit v5 on v4

--- a/solution.py
+++ b/solution.py
@@ -16,7 +16,7 @@
 STEPS = (0, 1, 3, 2)
 UNPACK_FLOPS = 10**10
 FORWARD_GROUP = 4
-BACKWARD_GROUP = 2
+BACKWARD_GROUP = 4
 KEYS = 2
 HIDDEN = -1e9
 
@@ -258,9 +258,9 @@
         proj_grad_s[0, here, :] = (times_normed * out_gain * slope_ref[0, here, :]).astype(BF)
         grad_mixed = norm_backward(grad_gated * out_gain * gating, mixed_normed, inv_mixed)
         grad_mixed_s[here, :] = jnp.where(valid, grad_mixed, 0.0).astype(BF)
-        for h in range(heads):
-            lanes = slice(h * head_dim, (h + 1) * head_dim)
-            grad_weights = dot_nt(grad_mixed_s[here, lanes], vqk_ref[0, :ends, lanes])
+        by_head = [slice(h * head_dim, (h + 1) * head_dim) for h in range(heads)]
+        products = [dot_nt(grad_mixed_s[here, lanes], vqk_ref[0, :ends, lanes]) for lanes in by_head]
+        for h, grad_weights in enumerate(products):
             for n in range(BACKWARD_GROUP):
                 block = slice((i + n) * rows, (i + n + 1) * rows)
                 seen = (i + n + 1) * rows
@@ -271,6 +271,7 @@
                 grads_s[h, block, :seen] = grad_scores.astype(BF)
                 if n < BACKWARD_GROUP - 1:
                     grads_s[h, block, seen:ends] = jnp.zeros((rows, ends - seen), BF)
+        for h, lanes in enumerate(by_head):
             grad_query = dot_nn(grads_s[h, here, :ends], vqk_ref[2, :ends, lanes]) * scale
             proj_grad_s[2, here, lanes] = (grad_query * slope_ref[2, here, lanes]).astype(BF)
     gain_ref[...] = grad_out_gain
@@ -455,8 +456,9 @@
 def last_kernel(factor, sources, kept, *refs):
     blocks = refs[:8]
     unpacked = refs[8 - len(sources) : 8 + kept]
-    uvqk_hbm, out_hbm, bias_ref, in_gain_ref, out_gain_ref = refs[8 + kept : 13 + kept]
-    copies = unpack(factor, sources, kept, *unpacked, uvqk_hbm, out_hbm, *refs[13 + kept :])
+    uvqk_hbm, out_hbm, *small_hbm = refs[8 + kept : 13 + kept]
+    *scratch, small_s, small_sems = refs[13 + kept :]
+    copies = unpack(factor, sources, kept, *unpacked, uvqk_hbm, out_hbm, *scratch)
     size = blocks[0].shape[0] // 4
     core = lax.rem(lax.axis_index("batch"), 2)
 
@@ -472,9 +474,10 @@
         return (zero + two) + (one + three)
 
     summed = (over_x(blocks[:4], core == 1) + over_x(blocks[4:], core == 0)) * factor
-    bias_ref[...] = summed[:4, :]
-    in_gain_ref[...] = summed[4:8, :]
-    out_gain_ref[...] = summed[8:12, :]
+    for n, target in enumerate(small_hbm):
+        small_s[n] = summed[4 * n : 4 * n + 4, :]
+        copies.append(pltpu.make_async_copy(small_s.at[n], target, small_sems.at[n]))
+        copies[-1].start()
     for copy in copies:
         copy.wait()
 
@@ -716,13 +719,14 @@
             functools.partial(last_kernel if last else unpack_kernel, factor, sources, len(kept)),
             out_shape=outs + [shape((4, buckets), F32)] * (3 if last else 0),
             in_specs=[vmem] * count + [hbm] * len(kept),
-            out_specs=[hbm] * 2 + [vmem] * (3 if last else 0),
+            out_specs=[hbm] * (5 if last else 2),
             input_output_aliases={count + n: n for n in range(len(kept))},
             scratch_shapes=[
                 pltpu.VMEM((slots, part, width), F32),
                 pltpu.VMEM((slots, part, buckets), F32),
                 pltpu.SemaphoreType.DMA((slots, 2)),
-            ],
+            ]
+            + ([pltpu.VMEM((3, 4, buckets), F32), pltpu.SemaphoreType.DMA((3,))] if last else []),
             compiler_params=params(SMALL),
             cost_estimate=cost(UNPACK_FLOPS, 10**6 * slots // 4),
             name="unpack",

time: 79.6 us -> 78.9 us (level)
  no operation moved by 1% of the time
where the time goes in v5:
time: 78.9 us; the launch traced here: 78.7 us
  starting transfers between devices  38.7 us (49%)
  waiting for transfers between devices  22.4 us (28%)
  Pallas kernels  16.1 us (20%)
  between operations  1.6 us (2%)
    ppermute x12, starting transfers between devices, along_batch(): return lax.ppermute(values, 'batch', pairs)  25.5 us
    ppermute x12, waiting for transfers between devices, along_batch(): return lax.ppermute(values, 'batch', pairs)  13.6 us
    ppermute x6, starting transfers between devices, along_x(): lax.ppermute(values, 'seq', [(i, (i + step) % seq_size) for i in range(se...  8 us
    ppermute x6, waiting for transfers between devices, along_either(): return lax.ppermute(values, ('seq', 'batch'), pairs)  5.49 us
    ppermute x6, starting transfers between devices, along_either(): return lax.ppermute(values, ('seq', 'batch'), pairs)  5.18 us
    pallas_call x3, Pallas kernels, unpack_call(): pl.pallas_call(functools.partial(last_kernel if last else unpack_kernel,...  4.33 us
    pallas_call x1, Pallas kernels, shards(): pl.pallas_call(functools.partial(backward_kernel, seq_size), out_shape=[s...  4.08 us
    pallas_call x1, Pallas kernels, shards(): pl.pallas_call(functools.partial(forward_kernel, seq_size), out_shape=[sh...  3.39 us
  transfers between devices with their start and end apart: 24, of which 11 were waited for; matrix products, arithmetic and copies ran while one was open for 0% of the time, Pallas kernels for 13%

profile of v5, /device:TPU:1, one launch (start us, length us, event | category | flops | bytes accessed | tf_op | source)
XLA Modules:
  0.0 78.7 jit_solution(244533626158237076)
XLA Ops:
  0.6 3.7 %collective-permute-start.5 = (bf16[128,512]{1,0:T(8,128)(2,1)}, bf16[128,512]{1,0:T(8,128)(2,1)S(1)}, u32[]{:S(2)}, u32[]{:S(2)}) collective-permute-start(bf16[128,512]{1,0:T(8,128)(2,1)} %bitcast.10), channel_id=1, source_target_pairs={{0,128},{64,192},{128,0},{192,64},{1,129},{65,193},{129,1},{193,65... | collective-permute-start | bytes 393224 | tf_op jit(solution)/shard_map/ppermute | solution.py:514
  4.3 0.9 %collective-permute-start.4 = (bf16[128,512]{1,0:T(8,128)(2,1)}, bf16[128,512]{1,0:T(8,128)(2,1)S(1)}, u32[]{:S(2)}, u32[]{:S(2)}) collective-permute-start(bf16[128,512]{1,0:T(8,128)(2,1)} %bitcast.11), channel_id=1, source_target_pairs={{0,192},{64,0},{128,64},{192,128},{1,193},{65,1},{129,65},{193,129... | collective-permute-start | bytes 393224 | tf_op jit(solution)/shard_map/ppermute | solution.py:514
  5.8 1.9 %prepare.1 = (bf16[128,512]{1,0:T(8,128)(2,1)S(1)}, bf16[128,512]{1,0:T(8,128)(2,1)S(1)}, f32[1,512]{1,0:T(1,128)S(1)}, f32[1,512]{1,0:T(1,128)S(1)}, bf16[512,2...) custom-call(s32[1,512]{1,0:T(1,128)} %bitcast.14, ...), custom_call_target="tpu_custom_call" | custom-call | flops 1000000000 | bytes 3000000 | tf_op jit(solution)/shard_map/prepare/pallas_call | solution.py:561
  8.4 2.1 %collective-permute-start.1 = (bf16[128,512]{1,0:T(8,128)(2,1)S(1)}, bf16[128,512]{1,0:T(8,128)(2,1)S(1)}, u32[]{:S(2)}, u32[]{:S(2)}) collective-permute-start(bf16[128,512]{1,0:T(8,128)(2,1)S(1)} %get-tuple-element.63.refs_0_.own_cot_ref), channel_id=1, source_target_pairs={{0,192},{64,0},{128,64},{192,128},{1,193},{65,1},{129,65},{193,129... | collective-permute-start | bytes 393224 | tf_op jit(solution)/shard_map/ppermute | solution.py:514
  11.2 3.2 %collective-permute-done.3.refs_1_ = bf16[128,512]{1,0:T(8,128)(2,1)S(1)} collective-permute-done((bf16[128,512]{1,0:T(8,128)(2,1)}, bf16[128,512]{1,0:T(8,128)(2,1)S(1)}, u32[]{:S(2)}, u32[]{:S(2)}) %collective-permute-start.3) | collective-permute-done | bytes 131104 | tf_op jit(solution)/shard_map/ppermute | solution.py:514
  14.5 3.4 %forward.1 = (bf16[512,512]{1,0:T(8,128)(2,1)S(1)}, f32[512,512]{1,0:T(8,128)S(1)}, f32[4,512,512]{2,1,0:T(8,128)S(1)}, bf16[3,512,512]{2,1,0:T(8,128)(2,1)S(1)}...) custom-call(bf16[128,512]{1,0:T(8,128)(2,1)S(1)} %get-tuple-element.62.refs_0_.own_ref, ...), custom_call_target="tpu_custom_call" | custom-call | flops 4000000000 | bytes 10000000 | tf_op jit(solution)/shard_map/forward/pallas_call | solution.py:599
  17.9 4.1 %backward.1 = (bf16[1280,128]{1,0:T(8,128)(2,1)S(1)}, f32[1280,128]{1,0:T(8,128)S(1)}, bf16[128,512]{1,0:T(8,128)(2,1)S(1)}, bf16[4,128,512]{2,1,0:T(8,128)(2,1)...) custom-call(s32[1]{0:T(128)S(6)} %copy.24.length_ref, ...), custom_call_target="tpu_custom_call" | custom-call | flops 4000000000 | bytes 10000000 | tf_op jit(solution)/shard_map/backward/pallas_call | solution.py:617
  22.0 2.2 %collective-permute-start.6 = (bf16[1280,128]{1,0:T(8,128)(2,1)S(1)}, bf16[1280,128]{1,0:T(8,128)(2,1)S(1)}, u32[]{:S(2)}, u32[]{:S(2)}) collective-permute-start(bf16[1280,128]{1,0:T(8,128)(2,1)S(1)} %get-tuple-element.83), channel_id=1, source_target_pairs={{0,1},{1,0},{2,3},{3,2},{4,5},{5,4},{6,7},{7,6},{8,9},{9,8},{10,11... | collective-permute-start | bytes 983048 | tf_op jit(solution)/shard_map/ppermute | solution.py:524
  24.2 1.1 %small.1 = (f32[128,512]{1,0:T(8,128)S(1)}, f32[16,128]{1,0:T(8,128)S(1)}) custom-call(bf16[128,512]{1,0:T(8,128)(2,1)S(1)} %get-tuple-element.62.refs_0_.own_ref, bf16[512,2048]{1,0:T(8,128)(2,1)S(1)} %get-tuple-element.68.refs_6_.uvqk_ref, bf16[4,128,512]{2,1,0:T(8,128)(2,1)S(1)} %get-tuple-element.77.own_grad_ref, ...), custom_call_target="tpu_custom_call" | custom-call | flops 1000000000 | bytes 3000000 | tf_op jit(solution)/shard_map/small/pallas_call | solution.py:656
  25.5 1.3 %collective-permute-start.7 = (bf16[336,128]{1,0:T(8,128)(2,1)S(1)}, bf16[336,128]{1,0:T(8,128)(2,1)S(1)}, u32[]{:S(2)}, u32[]{:S(2)}) collective-permute-start(bf16[336,128]{1,0:T(8,128)(2,1)S(1)} %get-tuple-element.93), channel_id=1, source_target_pairs={{0,2},{1,3},{2,0},{3,1},{4,6},{5,7},{6,4},{7,5},{8,10},{9,11},{10,... | collective-permute-start | bytes 258056 | tf_op jit(solution)/shard_map/ppermute | solution.py:524
  26.9 1.1 %collective-permute-start.8 = (bf16[336,128]{1,0:T(8,128)(2,1)S(1)}, bf16[336,128]{1,0:T(8,128)(2,1)S(1)}, u32[]{:S(2)}, u32[]{:S(2)}) collective-permute-start(bf16[336,128]{1,0:T(8,128)(2,1)S(1)} %get-tuple-element.94), channel_id=1, source_target_pairs={{0,18},{1,19},{2,16},{3,17},{4,22},{5,23},{6,20},{7,21},{8,26},{9,... | collective-permute-start | bytes 258056 | tf_op jit(solution)/shard_map/ppermute | solution.py:524
  28.3 1.1 %collective-permute-done.7.one_ref = bf16[336,128]{1,0:T(8,128)(2,1)S(1)} collective-permute-done((bf16[336,128]{1,0:T(8,128)(2,1)S(1)}, bf16[336,128]{1,0:T(8,128)(2,1)S(1)}, u32[]{:S(2)}, u32[]{:S(2)}) %collective-permute-start.7) | collective-permute-done | bytes 86048 | tf_op jit(solution)/shard_map/ppermute | solution.py:524
  29.4 2.8 %collective-permute-done.8.three_ref = bf16[336,128]{1,0:T(8,128)(2,1)S(1)} collective-permute-done((bf16[336,128]{1,0:T(8,128)(2,1)S(1)}, bf16[336,128]{1,0:T(8,128)(2,1)S(1)}, u32[]{:S(2)}, u32[]{:S(2)}) %collective-permute-start.8) | collective-permute-done | bytes 86048 | tf_op jit(solution)/shard_map/ppermute | solution.py:524
  32.2 1.5 %collective-permute-done.9.two_ref = bf16[336,128]{1,0:T(8,128)(2,1)S(1)} collective-permute-done((bf16[336,128]{1,0:T(8,128)(2,1)S(1)}, bf16[336,128]{1,0:T(8,128)(2,1)S(1)}, u32[]{:S(2)}, u32[]{:S(2)}) %collective-permute-start.9) | collective-permute-done | bytes 86048 | tf_op jit(solution)/shard_map/ppermute | solution.py:524
  33.8 1.9 %collective-permute-start.12 = (bf16[336,128]{1,0:T(8,128)(2,1)S(1)}, bf16[336,128]{1,0:T(8,128)(2,1)S(1)}, u32[]{:S(2)}, u32[]{:S(2)}) collective-permute-start(bf16[336,128]{1,0:T(8,128)(2,1)S(1)} %square_sum.1.own_ref), channel_id=1, source_target_pairs={{0,48},{1,49},{2,50},{3,51},{4,52},{5,53},{6,54},{7,55},{8,56},{9,... | collective-permute-start | bytes 258056 | tf_op jit(solution)/shard_map/ppermute | solution.py:524
  35.7 5.6 %collective-permute-start.11 = (bf16[336,128]{1,0:T(8,128)(2,1)S(1)}, bf16[336,128]{1,0:T(8,128)(2,1)S(1)}, u32[]{:S(2)}, u32[]{:S(2)}) collective-permute-start(bf16[336,128]{1,0:T(8,128)(2,1)S(1)} %square_sum.1.own_ref), channel_id=1, source_target_pairs={{0,62},{1,63},{2,52},{3,53},{4,50},{5,51},{6,56},{7,57},{8,54},{9,... | collective-permute-start | bytes 258056 | tf_op jit(solution)/shard_map/ppermute | solution.py:524
  41.3 1.9 %collective-permute-done.11.three_ref = bf16[336,128]{1,0:T(8,128)(2,1)S(1)} collective-permute-done((bf16[336,128]{1,0:T(8,128)(2,1)S(1)}, bf16[336,128]{1,0:T(8,128)(2,1)S(1)}, u32[]{:S(2)}, u32[]{:S(2)}) %collective-permute-start.11) | collective-permute-done | bytes 86048 | tf_op jit(solution)/shard_map/ppermute | solution.py:524
  43.1 2.7 %collective-permute-done.10.one_ref = bf16[336,128]{1,0:T(8,128)(2,1)S(1)} collective-permute-done((bf16[336,128]{1,0:T(8,128)(2,1)S(1)}, bf16[336,128]{1,0:T(8,128)(2,1)S(1)}, u32[]{:S(2)}, u32[]{:S(2)}) %collective-permute-start.10) | collective-permute-done | bytes 86048 | tf_op jit(solution)/shard_map/ppermute | solution.py:524
  45.9 2.0 %collective-permute-start.13 = (bf16[336,128]{1,0:T(8,128)(2,1)S(1)}, bf16[336,128]{1,0:T(8,128)(2,1)S(1)}, u32[]{:S(2)}, u32[]{:S(2)}) collective-permute-start(bf16[336,128]{1,0:T(8,128)(2,1)S(1)} %four_sum.1.left_ref), channel_id=1, source_target_pairs={{0,6},{1,7},{2,12},{3,13},{4,10},{5,11},{6,0},{7,1},{8,14},{9,15},... | collective-permute-start | bytes 258056 | tf_op jit(solution)/shard_map/ppermute | solution.py:524
  47.9 3.5 %collective-permute-done.13.right_ref = bf16[336,128]{1,0:T(8,128)(2,1)S(1)} collective-permute-done((bf16[336,128]{1,0:T(8,128)(2,1)S(1)}, bf16[336,128]{1,0:T(8,128)(2,1)S(1)}, u32[]{:S(2)}, u32[]{:S(2)}) %collective-permute-start.13) | collective-permute-done | bytes 86048 | tf_op jit(solution)/shard_map/ppermute | solution.py:524
  51.4 1.0 %collective-permute-start.16 = (bf16[336,128]{1,0:T(8,128)(2,1)S(1)}, bf16[336,128]{1,0:T(8,128)(2,1)S(1)}, u32[]{:S(2)}, u32[]{:S(2)}) collective-permute-start(bf16[336,128]{1,0:T(8,128)(2,1)S(1)} %pair_sum.1.refs_0_), channel_id=1, source_target_pairs={{0,16},{1,129},{2,18},{3,131},{4,20},{5,133},{6,22},{7,135},{8,24}... | collective-permute-start | bytes 258056 | tf_op jit(solution)/shard_map/ppermute | solution.py:552
  52.4 0.9 %collective-permute-start.15 = (bf16[336,128]{1,0:T(8,128)(2,1)S(1)}, bf16[336,128]{1,0:T(8,128)(2,1)S(1)}, u32[]{:S(2)}, u32[]{:S(2)}) collective-permute-start(bf16[336,128]{1,0:T(8,128)(2,1)S(1)} %pair_sum.1.refs_0_), channel_id=1, source_target_pairs={{0,18},{1,193},{2,16},{3,195},{4,22},{5,197},{6,20},{7,199},{8,26}... | collective-permute-start | bytes 258056 | tf_op jit(solution)/shard_map/ppermute | solution.py:552
  53.9 2.5 %collective-permute-done.16.refs_3_ = bf16[336,128]{1,0:T(8,128)(2,1)S(1)} collective-permute-done((bf16[336,128]{1,0:T(8,128)(2,1)S(1)}, bf16[336,128]{1,0:T(8,128)(2,1)S(1)}, u32[]{:S(2)}, u32[]{:S(2)}) %collective-permute-start.16) | collective-permute-done | bytes 86048 | tf_op jit(solution)/shard_map/ppermute | solution.py:552
  56.3 1.5 %collective-permute-done.14.refs_1_ = bf16[336,128]{1,0:T(8,128)(2,1)S(1)} collective-permute-done((bf16[336,128]{1,0:T(8,128)(2,1)S(1)}, bf16[336,128]{1,0:T(8,128)(2,1)S(1)}, u32[]{:S(2)}, u32[]{:S(2)}) %collective-permute-start.14) | collective-permute-done | bytes 86048 | tf_op jit(solution)/shard_map/ppermute | solution.py:552
  58.1 2.5 %collective-permute-start.17 = (bf16[1344,128]{1,0:T(8,128)(2,1)S(1)}, bf16[1344,128]{1,0:T(8,128)(2,1)S(1)}, u32[]{:S(2)}, u32[]{:S(2)}) collective-permute-start(bf16[1344,128]{1,0:T(8,128)(2,1)S(1)} %join.1.refs_0_), channel_id=1, source_target_pairs={{0,64},{1,3},{2,66},{3,1},{4,68},{5,7},{6,70},{7,5},{8,72},{9,11},... | collective-permute-start | bytes 1032200 | tf_op jit(solution)/shard_map/ppermute | solution.py:552
  60.6 0.9 %unpack.3 = (f32[512,2048]{1,0:T(8,128)}, f32[512,512]{1,0:T(8,128)}) custom-call(bf16[1344,128]{1,0:T(8,128)(2,1)S(1)} %join.1.refs_0_), custom_call_target="tpu_custom_call" | custom-call | flops 10000000000 | bytes 1000000 | tf_op jit(solution)/shard_map/unpack/pallas_call | solution.py:718
  61.5 5.2 %collective-permute-start.20 = (bf16[1344,128]{1,0:T(8,128)(2,1)S(1)}, bf16[1344,128]{1,0:T(8,128)(2,1)S(1)}, u32[]{:S(2)}, u32[]{:S(2)}) collective-permute-start(bf16[1344,128]{1,0:T(8,128)(2,1)S(1)} %join.1.refs_0_), channel_id=1, source_target_pairs={{0,1},{1,0},{2,3},{3,2},{4,5},{5,4},{6,7},{7,6},{8,9},{9,8},{10,11... | collective-permute-start | bytes 1032200 | tf_op jit(solution)/shard_map/ppermute | solution.py:524
  66.7 1.0 %rows.1 = (bf16[128,512]{1,0:T(8,128)(2,1)}, bf16[128,512]{1,0:T(8,128)(2,1)}) custom-call(bf16[128,512]{1,0:T(8,128)(2,1)S(1)} %get-tuple-element.62.refs_0_.own_ref, bf16[128,512]{1,0:T(8,128)(2,1)S(1)} %get-tuple-element.63.refs_0_.own_cot_ref, f32[1,512]{1,0:T(1,128)S(1)} %get-tuple-element.64.refs_5_.in_gain_ref, ...), custom_call_target="tpu_custom_call" | custom-call | flops 2000000000 | bytes 3000000 | tf_op jit(solution)/shard_map/rows/pallas_call | solution.py:674
  67.7 1.5 %collective-permute-done.17.refs_1_ = bf16[1344,128]{1,0:T(8,128)(2,1)S(1)} collective-permute-done((bf16[1344,128]{1,0:T(8,128)(2,1)S(1)}, bf16[1344,128]{1,0:T(8,128)(2,1)S(1)}, u32[]{:S(2)}, u32[]{:S(2)}) %collective-permute-start.17) | collective-permute-done | bytes 344096 | tf_op jit(solution)/shard_map/ppermute | solution.py:552
  69.3 5.4 %collective-permute-start.23 = (bf16[1344,128]{1,0:T(8,128)(2,1)S(1)}, bf16[1344,128]{1,0:T(8,128)(2,1)S(1)}, u32[]{:S(2)}, u32[]{:S(2)}) collective-permute-start(bf16[1344,128]{1,0:T(8,128)(2,1)S(1)} %collective-permute-done.19.refs_3_), channel_id=1, source_target_pairs={{0,1},{1,0},{2,3},{3,2},{4,5},{5,4},{6,7},{7,6},{8,9},{9,8},{10,11... | collective-permute-start | bytes 1032200 | tf_op jit(solution)/shard_map/ppermute | solution.py:524
  75.1 1.8 %unpack.4 = (f32[512,2048]{1,0:T(8,128)}, f32[512,512]{1,0:T(8,128)}) custom-call(bf16[1344,128]{1,0:T(8,128)(2,1)S(1)} %collective-permute-done.20.refs_0_.refs_4_, bf16[1344,128]{1,0:T(8,128)(2,1)S(1)} %collective-permute-done.17.refs_1_, bf16[1344,128]{1,0:T(8,128)(2,1)S(1)} %collective-permute-done.18.refs_2_, ...), custom_call_target="tpu_custom_call", output_to_operand_aliasing={{0}: (4, {}), {1}: (5, {})} | custom-call | flops 10000000000 | bytes 4000000 | tf_op jit(solution)/shard_map/unpack/pallas_call | solution.py:718
  77.0 1.6 %unpack.5 = (f32[512,2048]{1,0:T(8,128)}, f32[512,512]{1,0:T(8,128)}, f32[4,128]{1,0:T(4,128)}, f32[4,128]{1,0:T(4,128)}, f32[4,128]{1,0:T(4,128)}) custom-call(bf16[1344,128]{1,0:T(8,128)(2,1)S(1)} %join.1.refs_0_, bf16[1344,128]{1,0:T(8,128)(2,1)S(1)} %collective-permute-done.17.refs_1_, ...), custom_call_target="tpu_custom_call", output_to_operand_aliasing={{0}: (8, {}), {1}: (9, {})} | custom-call | flops 10000000000 | bytes 3000000 | tf_op jit(solution)/shard_map/unpack/pallas_call | solution.py:718
  (29 shorter events, 3.4 us)
Async XLA Ops:
  0.6 10.5 %collective-permute-start.5 = (bf16[128,512]{1,0:T(8,128)(2,1)}, bf16[128,512]{1,0:T(8,128)(2,1)S(1)}, u32[]{:S(2)}, u32[]{:S(2)}) collective-permute-start(bf16[128,512]{1,0:T(8,128)(2,1)} %bitcast.10), channel_id=1, source_target_pairs={{0,128},{64,192},{128,0},{192,64},{1,129},{65,193},{129,1},{193,65... | collective-permute-start | bytes 393224 | tf_op jit(solution)/shard_map/ppermute | solution.py:514
  4.3 6.9 %collective-permute-start.4 = (bf16[128,512]{1,0:T(8,128)(2,1)}, bf16[128,512]{1,0:T(8,128)(2,1)S(1)}, u32[]{:S(2)}, u32[]{:S(2)}) collective-permute-start(bf16[128,512]{1,0:T(8,128)(2,1)} %bitcast.11), channel_id=1, source_target_pairs={{0,192},{64,0},{128,64},{192,128},{1,193},{65,1},{129,65},{193,129... | collective-permute-start | bytes 393224 | tf_op jit(solution)/shard_map/ppermute | solution.py:514
  5.2 9.3 %collective-permute-start.3 = (bf16[128,512]{1,0:T(8,128)(2,1)}, bf16[128,512]{1,0:T(8,128)(2,1)S(1)}, u32[]{:S(2)}, u32[]{:S(2)}) collective-permute-start(bf16[128,512]{1,0:T(8,128)(2,1)} %bitcast.12), channel_id=1, source_target_pairs={{0,64},{64,128},{128,192},{192,0},{1,65},{65,129},{129,193},{193,1... | collective-permute-start | bytes 393224 | tf_op jit(solution)/shard_map/ppermute | solution.py:514
  7.7 10.2 %collective-permute-start.2 = (bf16[128,512]{1,0:T(8,128)(2,1)S(1)}, bf16[128,512]{1,0:T(8,128)(2,1)S(1)}, u32[]{:S(2)}, u32[]{:S(2)}) collective-permute-start(bf16[128,512]{1,0:T(8,128)(2,1)S(1)} %get-tuple-element.63.refs_0_.own_cot_ref), channel_id=1, source_target_pairs={{0,128},{64,192},{128,0},{192,64},{1,129},{65,193},{129,1},{193,65... | collective-permute-start | bytes 393224 | tf_op jit(solution)/shard_map/ppermute | solution.py:514
  8.4 9.5 %collective-permute-start.1 = (bf16[128,512]{1,0:T(8,128)(2,1)S(1)}, bf16[128,512]{1,0:T(8,128)(2,1)S(1)}, u32[]{:S(2)}, u32[]{:S(2)}) collective-permute-start(bf16[128,512]{1,0:T(8,128)(2,1)S(1)} %get-tuple-element.63.refs_0_.own_cot_ref), channel_id=1, source_target_pairs={{0,192},{64,0},{128,64},{192,128},{1,193},{65,1},{129,65},{193,129... | collective-permute-start | bytes 393224 | tf_op jit(solution)/shard_map/ppermute | solution.py:514
  11.1 6.8 %collective-permute-start = (bf16[128,512]{1,0:T(8,128)(2,1)S(1)}, bf16[128,512]{1,0:T(8,128)(2,1)S(1)}, u32[]{:S(2)}, u32[]{:S(2)}) collective-permute-start(bf16[128,512]{1,0:T(8,128)(2,1)S(1)} %get-tuple-element.63.refs_0_.own_cot_ref), channel_id=1, source_target_pairs={{0,64},{64,128},{128,192},{192,0},{1,65},{65,129},{129,193},{193,1... | collective-permute-start | bytes 393224 | tf_op jit(solution)/shard_map/ppermute | solution.py:514
  22.0 3.5 %collective-permute-start.6 = (bf16[1280,128]{1,0:T(8,128)(2,1)S(1)}, bf16[1280,128]{1,0:T(8,128)(2,1)S(1)}, u32[]{:S(2)}, u32[]{:S(2)}) collective-permute-start(bf16[1280,128]{1,0:T(8,128)(2,1)S(1)} %get-tuple-element.83), channel_id=1, source_target_pairs={{0,1},{1,0},{2,3},{3,2},{4,5},{5,4},{6,7},{7,6},{8,9},{9,8},{10,11... | collective-permute-start | bytes 983048 | tf_op jit(solution)/shard_map/ppermute | solution.py:524
  25.5 3.8 %collective-permute-start.7 = (bf16[336,128]{1,0:T(8,128)(2,1)S(1)}, bf16[336,128]{1,0:T(8,128)(2,1)S(1)}, u32[]{:S(2)}, u32[]{:S(2)}) collective-permute-start(bf16[336,128]{1,0:T(8,128)(2,1)S(1)} %get-tuple-element.93), channel_id=1, source_target_pairs={{0,2},{1,3},{2,0},{3,1},{4,6},{5,7},{6,4},{7,5},{8,10},{9,11},{10,... | collective-permute-start | bytes 258056 | tf_op jit(solution)/shard_map/ppermute | solution.py:524
  26.9 5.3 %collective-permute-start.8 = (bf16[336,128]{1,0:T(8,128)(2,1)S(1)}, bf16[336,128]{1,0:T(8,128)(2,1)S(1)}, u32[]{:S(2)}, u32[]{:S(2)}) collective-permute-start(bf16[336,128]{1,0:T(8,128)(2,1)S(1)} %get-tuple-element.94), channel_id=1, source_target_pairs={{0,18},{1,19},{2,16},{3,17},{4,22},{5,23},{6,20},{7,21},{8,26},{9,... | collective-permute-start | bytes 258056 | tf_op jit(solution)/shard_map/ppermute | solution.py:524
  28.0 5.7 %collective-permute-start.9 = (bf16[336,128]{1,0:T(8,128)(2,1)S(1)}, bf16[336,128]{1,0:T(8,128)(2,1)S(1)}, u32[]{:S(2)}, u32[]{:S(2)}) collective-permute-start(bf16[336,128]{1,0:T(8,128)(2,1)S(1)} %get-tuple-element.95), channel_id=1, source_target_pairs={{0,16},{1,17},{2,18},{3,19},{4,20},{5,21},{6,22},{7,23},{8,24},{9,... | collective-permute-start | bytes 258056 | tf_op jit(solution)/shard_map/ppermute | solution.py:524
  33.8 7.5 %collective-permute-start.12 = (bf16[336,128]{1,0:T(8,128)(2,1)S(1)}, bf16[336,128]{1,0:T(8,128)(2,1)S(1)}, u32[]{:S(2)}, u32[]{:S(2)}) collective-permute-start(bf16[336,128]{1,0:T(8,128)(2,1)S(1)} %square_sum.1.own_ref), channel_id=1, source_target_pairs={{0,48},{1,49},{2,50},{3,51},{4,52},{5,53},{6,54},{7,55},{8,56},{9,... | collective-permute-start | bytes 258056 | tf_op jit(solution)/shard_map/ppermute | solution.py:524
  35.7 7.4 %collective-permute-start.11 = (bf16[336,128]{1,0:T(8,128)(2,1)S(1)}, bf16[336,128]{1,0:T(8,128)(2,1)S(1)}, u32[]{:S(2)}, u32[]{:S(2)}) collective-permute-start(bf16[336,128]{1,0:T(8,128)(2,1)S(1)} %square_sum.1.own_ref), channel_id=1, source_target_pairs={{0,62},{1,63},{2,52},{3,53},{4,50},{5,51},{6,56},{7,57},{8,54},{9,... | collective-permute-start | bytes 258056 | tf_op jit(solution)/shard_map/ppermute | solution.py:524
  41.3 4.5 %collective-permute-start.10 = (bf16[336,128]{1,0:T(8,128)(2,1)S(1)}, bf16[336,128]{1,0:T(8,128)(2,1)S(1)}, u32[]{:S(2)}, u32[]{:S(2)}) collective-permute-start(bf16[336,128]{1,0:T(8,128)(2,1)S(1)} %square_sum.1.own_ref), channel_id=1, source_target_pairs={{0,14},{1,15},{2,4},{3,5},{4,2},{5,3},{6,8},{7,9},{8,6},{9,7},{10,... | collective-permute-start | bytes 258056 | tf_op jit(solution)/shard_map/ppermute | solution.py:524
  45.9 5.5 %collective-permute-start.13 = (bf16[336,128]{1,0:T(8,128)(2,1)S(1)}, bf16[336,128]{1,0:T(8,128)(2,1)S(1)}, u32[]{:S(2)}, u32[]{:S(2)}) collective-permute-start(bf16[336,128]{1,0:T(8,128)(2,1)S(1)} %four_sum.1.left_ref), channel_id=1, source_target_pairs={{0,6},{1,7},{2,12},{3,13},{4,10},{5,11},{6,0},{7,1},{8,14},{9,15},... | collective-permute-start | bytes 258056 | tf_op jit(solution)/shard_map/ppermute | solution.py:524
  51.4 4.9 %collective-permute-start.16 = (bf16[336,128]{1,0:T(8,128)(2,1)S(1)}, bf16[336,128]{1,0:T(8,128)(2,1)S(1)}, u32[]{:S(2)}, u32[]{:S(2)}) collective-permute-start(bf16[336,128]{1,0:T(8,128)(2,1)S(1)} %pair_sum.1.refs_0_), channel_id=1, source_target_pairs={{0,16},{1,129},{2,18},{3,131},{4,20},{5,133},{6,22},{7,135},{8,24}... | collective-permute-start | bytes 258056 | tf_op jit(solution)/shard_map/ppermute | solution.py:552
  52.4 3.9 %collective-permute-start.15 = (bf16[336,128]{1,0:T(8,128)(2,1)S(1)}, bf16[336,128]{1,0:T(8,128)(2,1)S(1)}, u32[]{:S(2)}, u32[]{:S(2)}) collective-permute-start(bf16[336,128]{1,0:T(8,128)(2,1)S(1)} %pair_sum.1.refs_0_), channel_id=1, source_target_pairs={{0,18},{1,193},{2,16},{3,195},{4,22},{5,197},{6,20},{7,199},{8,26}... | collective-permute-start | bytes 258056 | tf_op jit(solution)/shard_map/ppermute | solution.py:552
  53.3 4.5 %collective-permute-start.14 = (bf16[336,128]{1,0:T(8,128)(2,1)S(1)}, bf16[336,128]{1,0:T(8,128)(2,1)S(1)}, u32[]{:S(2)}, u32[]{:S(2)}) collective-permute-start(bf16[336,128]{1,0:T(8,128)(2,1)S(1)} %pair_sum.1.refs_0_), channel_id=1, source_target_pairs={{0,2},{1,65},{2,0},{3,67},{4,6},{5,69},{6,4},{7,71},{8,10},{9,73},... | collective-permute-start | bytes 258056 | tf_op jit(solution)/shard_map/ppermute | solution.py:552
  57.8 11.4 %collective-permute-start.19 = (bf16[1344,128]{1,0:T(8,128)(2,1)S(1)}, bf16[1344,128]{1,0:T(8,128)(2,1)S(1)}, u32[]{:S(2)}, u32[]{:S(2)}) collective-permute-start(bf16[1344,128]{1,0:T(8,128)(2,1)S(1)} %join.1.refs_0_), channel_id=1, source_target_pairs={{0,128},{1,17},{2,130},{3,19},{4,132},{5,21},{6,134},{7,23},{8,136... | collective-permute-start | bytes 1032200 | tf_op jit(solution)/shard_map/ppermute | solution.py:552
  58.0 11.3 %collective-permute-start.18 = (bf16[1344,128]{1,0:T(8,128)(2,1)S(1)}, bf16[1344,128]{1,0:T(8,128)(2,1)S(1)}, u32[]{:S(2)}, u32[]{:S(2)}) collective-permute-start(bf16[1344,128]{1,0:T(8,128)(2,1)S(1)} %join.1.refs_0_), channel_id=1, source_target_pairs={{0,192},{1,19},{2,194},{3,17},{4,196},{5,23},{6,198},{7,21},{8,200... | collective-permute-start | bytes 1032200 | tf_op jit(solution)/shard_map/ppermute | solution.py:552
  58.1 11.2 %collective-permute-start.17 = (bf16[1344,128]{1,0:T(8,128)(2,1)S(1)}, bf16[1344,128]{1,0:T(8,128)(2,1)S(1)}, u32[]{:S(2)}, u32[]{:S(2)}) collective-permute-start(bf16[1344,128]{1,0:T(8,128)(2,1)S(1)} %join.1.refs_0_), channel_id=1, source_target_pairs={{0,64},{1,3},{2,66},{3,1},{4,68},{5,7},{6,70},{7,5},{8,72},{9,11},... | collective-permute-start | bytes 1032200 | tf_op jit(solution)/shard_map/ppermute | solution.py:552
  61.5 13.6 %collective-permute-start.20 = (bf16[1344,128]{1,0:T(8,128)(2,1)S(1)}, bf16[1344,128]{1,0:T(8,128)(2,1)S(1)}, u32[]{:S(2)}, u32[]{:S(2)}) collective-permute-start(bf16[1344,128]{1,0:T(8,128)(2,1)S(1)} %join.1.refs_0_), channel_id=1, source_target_pairs={{0,1},{1,0},{2,3},{3,2},{4,5},{5,4},{6,7},{7,6},{8,9},{9,8},{10,11... | collective-permute-start | bytes 1032200 | tf_op jit(solution)/shard_map/ppermute | solution.py:524
  69.3 7.7 %collective-permute-start.23 = (bf16[1344,128]{1,0:T(8,128)(2,1)S(1)}, bf16[1344,128]{1,0:T(8,128)(2,1)S(1)}, u32[]{:S(2)}, u32[]{:S(2)}) collective-permute-start(bf16[1344,128]{1,0:T(8,128)(2,1)S(1)} %collective-permute-done.19.refs_3_), channel_id=1, source_target_pairs={{0,1},{1,0},{2,3},{3,2},{4,5},{5,4},{6,7},{7,6},{8,9},{9,8},{10,11... | collective-permute-start | bytes 1032200 | tf_op jit(solution)/shard_map/ppermute | solution.py:524
  74.6 2.4 %collective-permute-start.22 = (bf16[1344,128]{1,0:T(8,128)(2,1)S(1)}, bf16[1344,128]{1,0:T(8,128)(2,1)S(1)}, u32[]{:S(2)}, u32[]{:S(2)}) collective-permute-start(bf16[1344,128]{1,0:T(8,128)(2,1)S(1)} %collective-permute-done.18.refs_2_), channel_id=1, source_target_pairs={{0,1},{1,0},{2,3},{3,2},{4,5},{5,4},{6,7},{7,6},{8,9},{9,8},{10,11... | collective-permute-start | bytes 1032200 | tf_op jit(solution)/shard_map/ppermute | solution.py:524
  74.7 2.3 %collective-permute-start.21 = (bf16[1344,128]{1,0:T(8,128)(2,1)S(1)}, bf16[1344,128]{1,0:T(8,128)(2,1)S(1)}, u32[]{:S(2)}, u32[]{:S(2)}) collective-permute-start(bf16[1344,128]{1,0:T(8,128)(2,1)S(1)} %collective-permute-done.17.refs_1_), channel_id=1, source_target_pairs={{0,1},{1,0},{2,3},{3,2},{4,5},{5,4},{6,7},{7,6},{8,9},{9,8},{10,11... | collective-permute-start | bytes 1032200 | tf_op jit(solution)/shard_map/ppermute | solution.py:524

commit v6 on v5

--- a/solution.py
+++ b/solution.py
@@ -733,13 +733,12 @@
         )(*blocks, *kept)
 
     moved = {step: along_either(joined, step, 0) for step in STEPS[1:]}
-    kept = unpack_call(((False, 0),), ())
-    again, kept = lax.optimization_barrier((joined, kept))
-    others[0] = across(again)
+    others[0] = across(joined)
+    kept = unpack_call(((False, 0), (True, 0)), ())
     for step in STEPS[1:]:
         columns[step], kept = lax.optimization_barrier((moved[step], kept))
         others[step] = across(columns[step])
-    kept = unpack_call(((True, 0), (False, 1), (False, 3), (False, 2)), kept)
+    kept = unpack_call(((False, 1), (False, 3), (False, 2)), kept)
     grad_uvqk, grad_out_weight, grad_bias, grad_in_gain, grad_out_gain = unpack_call(
         ((True, 1), (True, 3), (True, 2)), kept, last=True
     )

time: 78.9 us -> 79.8 us (1.011)
  waiting for transfers between devices: 22.4 us -> 28.5 us
  starting transfers between devices: 38.7 us -> 33.5 us
    ppermute x6, waiting for transfers between devices: 5.49 us -> 11.4 us  [along_either(): return lax.ppermute(values, ('seq', 'batch'), pairs)]
    ppermute x12, starting transfers between devices: 25.5 us -> 20.4 us  [along_batch(): return lax.ppermute(values, 'batch', pairs)]
  transfers between devices with their start and end apart: 24 -> 24, of which waited for: 11 -> 12; matrix products, arithmetic and copies ran while one was open for 0% -> 0% of each run, Pallas kernels for 13% -> 13%
where the time goes in v6:
time: 79.8 us; the launch traced here: 79.6 us
  starting transfers between devices  33.5 us (42%)
  waiting for transfers between devices  28.5 us (36%)
  Pallas kernels  16.1 us (20%)
  between operations  1.59 us (2%)
    ppermute x12, starting transfers between devices, along_batch(): return lax.ppermute(values, 'batch', pairs)  20.4 us
    ppermute x12, waiting for transfers between devices, along_batch(): return lax.ppermute(values, 'batch', pairs)  13.8 us
    ppermute x6, waiting for transfers between devices, along_either(): return lax.ppermute(values, ('seq', 'batch'), pairs)  11.4 us
    ppermute x6, starting transfers between devices, along_x(): lax.ppermute(values, 'seq', [(i, (i + step) % seq_size) for i in range(se...  8 us
    ppermute x6, starting transfers between devices, along_either(): return lax.ppermute(values, ('seq', 'batch'), pairs)  5.1 us
    pallas_call x3, Pallas kernels, unpack_call(): pl.pallas_call(functools.partial(last_kernel if last else unpack_kernel,...  4.33 us
    pallas_call x1, Pallas kernels, shards(): pl.pallas_call(functools.partial(backward_kernel, seq_size), out_shape=[s...  4.08 us
    pallas_call x1, Pallas kernels, shards(): pl.pallas_call(functools.partial(forward_kernel, seq_size), out_shape=[sh...  3.39 us
  transfers between devices with their start and end apart: 24, of which 12 were waited for; matrix products, arithmetic and copies ran while one was open for 0% of the time, Pallas kernels for 13%

profile of v6, /device:TPU:1, one launch (start us, length us, event | category | flops | bytes accessed | tf_op | source)
XLA Modules:
  0.0 79.6 jit_solution(1201066280235918274)
XLA Ops:
  0.6 3.7 %collective-permute-start.5 = (bf16[128,512]{1,0:T(8,128)(2,1)}, bf16[128,512]{1,0:T(8,128)(2,1)S(1)}, u32[]{:S(2)}, u32[]{:S(2)}) collective-permute-start(bf16[128,512]{1,0:T(8,128)(2,1)} %bitcast.10), channel_id=1, source_target_pairs={{0,128},{64,192},{128,0},{192,64},{1,129},{65,193},{129,1},{193,65... | collective-permute-start | bytes 393224 | tf_op jit(solution)/shard_map/ppermute | solution.py:514
  4.3 0.9 %collective-permute-start.4 = (bf16[128,512]{1,0:T(8,128)(2,1)}, bf16[128,512]{1,0:T(8,128)(2,1)S(1)}, u32[]{:S(2)}, u32[]{:S(2)}) collective-permute-start(bf16[128,512]{1,0:T(8,128)(2,1)} %bitcast.11), channel_id=1, source_target_pairs={{0,192},{64,0},{128,64},{192,128},{1,193},{65,1},{129,65},{193,129... | collective-permute-start | bytes 393224 | tf_op jit(solution)/shard_map/ppermute | solution.py:514
  5.8 1.9 %prepare.1 = (bf16[128,512]{1,0:T(8,128)(2,1)S(1)}, bf16[128,512]{1,0:T(8,128)(2,1)S(1)}, f32[1,512]{1,0:T(1,128)S(1)}, f32[1,512]{1,0:T(1,128)S(1)}, bf16[512,2...) custom-call(s32[1,512]{1,0:T(1,128)} %bitcast.14, ...), custom_call_target="tpu_custom_call" | custom-call | flops 1000000000 | bytes 3000000 | tf_op jit(solution)/shard_map/prepare/pallas_call | solution.py:561
  8.4 2.1 %collective-permute-start.1 = (bf16[128,512]{1,0:T(8,128)(2,1)S(1)}, bf16[128,512]{1,0:T(8,128)(2,1)S(1)}, u32[]{:S(2)}, u32[]{:S(2)}) collective-permute-start(bf16[128,512]{1,0:T(8,128)(2,1)S(1)} %get-tuple-element.60.refs_0_.own_cot_ref), channel_id=1, source_target_pairs={{0,192},{64,0},{128,64},{192,128},{1,193},{65,1},{129,65},{193,129... | collective-permute-start | bytes 393224 | tf_op jit(solution)/shard_map/ppermute | solution.py:514
  11.2 3.2 %collective-permute-done.3.refs_1_ = bf16[128,512]{1,0:T(8,128)(2,1)S(1)} collective-permute-done((bf16[128,512]{1,0:T(8,128)(2,1)}, bf16[128,512]{1,0:T(8,128)(2,1)S(1)}, u32[]{:S(2)}, u32[]{:S(2)}) %collective-permute-start.3) | collective-permute-done | bytes 131104 | tf_op jit(solution)/shard_map/ppermute | solution.py:514
  14.5 3.4 %forward.1 = (bf16[512,512]{1,0:T(8,128)(2,1)S(1)}, f32[512,512]{1,0:T(8,128)S(1)}, f32[4,512,512]{2,1,0:T(8,128)S(1)}, bf16[3,512,512]{2,1,0:T(8,128)(2,1)S(1)}...) custom-call(bf16[128,512]{1,0:T(8,128)(2,1)S(1)} %get-tuple-element.59.refs_0_.own_ref, ...), custom_call_target="tpu_custom_call" | custom-call | flops 4000000000 | bytes 10000000 | tf_op jit(solution)/shard_map/forward/pallas_call | solution.py:599
  17.9 4.1 %backward.1 = (bf16[1280,128]{1,0:T(8,128)(2,1)S(1)}, f32[1280,128]{1,0:T(8,128)S(1)}, bf16[128,512]{1,0:T(8,128)(2,1)S(1)}, bf16[4,128,512]{2,1,0:T(8,128)(2,1)...) custom-call(s32[1]{0:T(128)S(6)} %copy.24.length_ref, ...), custom_call_target="tpu_custom_call" | custom-call | flops 4000000000 | bytes 10000000 | tf_op jit(solution)/shard_map/backward/pallas_call | solution.py:617
  22.0 2.2 %collective-permute-start.6 = (bf16[1280,128]{1,0:T(8,128)(2,1)S(1)}, bf16[1280,128]{1,0:T(8,128)(2,1)S(1)}, u32[]{:S(2)}, u32[]{:S(2)}) collective-permute-start(bf16[1280,128]{1,0:T(8,128)(2,1)S(1)} %get-tuple-element.80), channel_id=1, source_target_pairs={{0,1},{1,0},{2,3},{3,2},{4,5},{5,4},{6,7},{7,6},{8,9},{9,8},{10,11... | collective-permute-start | bytes 983048 | tf_op jit(solution)/shard_map/ppermute | solution.py:524
  24.2 1.1 %small.1 = (f32[128,512]{1,0:T(8,128)S(1)}, f32[16,128]{1,0:T(8,128)S(1)}) custom-call(bf16[128,512]{1,0:T(8,128)(2,1)S(1)} %get-tuple-element.59.refs_0_.own_ref, bf16[512,2048]{1,0:T(8,128)(2,1)S(1)} %get-tuple-element.65.refs_6_.uvqk_ref, bf16[4,128,512]{2,1,0:T(8,128)(2,1)S(1)} %get-tuple-element.74.own_grad_ref, ...), custom_call_target="tpu_custom_call" | custom-call | flops 1000000000 | bytes 3000000 | tf_op jit(solution)/shard_map/small/pallas_call | solution.py:656
  25.5 1.3 %collective-permute-start.7 = (bf16[336,128]{1,0:T(8,128)(2,1)S(1)}, bf16[336,128]{1,0:T(8,128)(2,1)S(1)}, u32[]{:S(2)}, u32[]{:S(2)}) collective-permute-start(bf16[336,128]{1,0:T(8,128)(2,1)S(1)} %get-tuple-element.90), channel_id=1, source_target_pairs={{0,2},{1,3},{2,0},{3,1},{4,6},{5,7},{6,4},{7,5},{8,10},{9,11},{10,... | collective-permute-start | bytes 258056 | tf_op jit(solution)/shard_map/ppermute | solution.py:524
  26.9 1.1 %collective-permute-start.8 = (bf16[336,128]{1,0:T(8,128)(2,1)S(1)}, bf16[336,128]{1,0:T(8,128)(2,1)S(1)}, u32[]{:S(2)}, u32[]{:S(2)}) collective-permute-start(bf16[336,128]{1,0:T(8,128)(2,1)S(1)} %get-tuple-element.91), channel_id=1, source_target_pairs={{0,18},{1,19},{2,16},{3,17},{4,22},{5,23},{6,20},{7,21},{8,26},{9,... | collective-permute-start | bytes 258056 | tf_op jit(solution)/shard_map/ppermute | solution.py:524
  28.3 1.1 %collective-permute-done.7.one_ref = bf16[336,128]{1,0:T(8,128)(2,1)S(1)} collective-permute-done((bf16[336,128]{1,0:T(8,128)(2,1)S(1)}, bf16[336,128]{1,0:T(8,128)(2,1)S(1)}, u32[]{:S(2)}, u32[]{:S(2)}) %collective-permute-start.7) | collective-permute-done | bytes 86048 | tf_op jit(solution)/shard_map/ppermute | solution.py:524
  29.4 2.8 %collective-permute-done.8.three_ref = bf16[336,128]{1,0:T(8,128)(2,1)S(1)} collective-permute-done((bf16[336,128]{1,0:T(8,128)(2,1)S(1)}, bf16[336,128]{1,0:T(8,128)(2,1)S(1)}, u32[]{:S(2)}, u32[]{:S(2)}) %collective-permute-start.8) | collective-permute-done | bytes 86048 | tf_op jit(solution)/shard_map/ppermute | solution.py:524
  32.2 1.5 %collective-permute-done.9.two_ref = bf16[336,128]{1,0:T(8,128)(2,1)S(1)} collective-permute-done((bf16[336,128]{1,0:T(8,128)(2,1)S(1)}, bf16[336,128]{1,0:T(8,128)(2,1)S(1)}, u32[]{:S(2)}, u32[]{:S(2)}) %collective-permute-start.9) | collective-permute-done | bytes 86048 | tf_op jit(solution)/shard_map/ppermute | solution.py:524
  33.8 1.9 %collective-permute-start.12 = (bf16[336,128]{1,0:T(8,128)(2,1)S(1)}, bf16[336,128]{1,0:T(8,128)(2,1)S(1)}, u32[]{:S(2)}, u32[]{:S(2)}) collective-permute-start(bf16[336,128]{1,0:T(8,128)(2,1)S(1)} %square_sum.1.own_ref), channel_id=1, source_target_pairs={{0,48},{1,49},{2,50},{3,51},{4,52},{5,53},{6,54},{7,55},{8,56},{9,... | collective-permute-start | bytes 258056 | tf_op jit(solution)/shard_map/ppermute | solution.py:524
  35.7 5.6 %collective-permute-start.11 = (bf16[336,128]{1,0:T(8,128)(2,1)S(1)}, bf16[336,128]{1,0:T(8,128)(2,1)S(1)}, u32[]{:S(2)}, u32[]{:S(2)}) collective-permute-start(bf16[336,128]{1,0:T(8,128)(2,1)S(1)} %square_sum.1.own_ref), channel_id=1, source_target_pairs={{0,62},{1,63},{2,52},{3,53},{4,50},{5,51},{6,56},{7,57},{8,54},{9,... | collective-permute-start | bytes 258056 | tf_op jit(solution)/shard_map/ppermute | solution.py:524
  41.3 1.9 %collective-permute-done.11.three_ref = bf16[336,128]{1,0:T(8,128)(2,1)S(1)} collective-permute-done((bf16[336,128]{1,0:T(8,128)(2,1)S(1)}, bf16[336,128]{1,0:T(8,128)(2,1)S(1)}, u32[]{:S(2)}, u32[]{:S(2)}) %collective-permute-start.11) | collective-permute-done | bytes 86048 | tf_op jit(solution)/shard_map/ppermute | solution.py:524
  43.1 2.7 %collective-permute-done.10.one_ref = bf16[336,128]{1,0:T(8,128)(2,1)S(1)} collective-permute-done((bf16[336,128]{1,0:T(8,128)(2,1)S(1)}, bf16[336,128]{1,0:T(8,128)(2,1)S(1)}, u32[]{:S(2)}, u32[]{:S(2)}) %collective-permute-start.10) | collective-permute-done | bytes 86048 | tf_op jit(solution)/shard_map/ppermute | solution.py:524
  45.9 2.0 %collective-permute-start.13 = (bf16[336,128]{1,0:T(8,128)(2,1)S(1)}, bf16[336,128]{1,0:T(8,128)(2,1)S(1)}, u32[]{:S(2)}, u32[]{:S(2)}) collective-permute-start(bf16[336,128]{1,0:T(8,128)(2,1)S(1)} %four_sum.1.left_ref), channel_id=1, source_target_pairs={{0,6},{1,7},{2,12},{3,13},{4,10},{5,11},{6,0},{7,1},{8,14},{9,15},... | collective-permute-start | bytes 258056 | tf_op jit(solution)/shard_map/ppermute | solution.py:524
  47.9 3.5 %collective-permute-done.13.right_ref = bf16[336,128]{1,0:T(8,128)(2,1)S(1)} collective-permute-done((bf16[336,128]{1,0:T(8,128)(2,1)S(1)}, bf16[336,128]{1,0:T(8,128)(2,1)S(1)}, u32[]{:S(2)}, u32[]{:S(2)}) %collective-permute-start.13) | collective-permute-done | bytes 86048 | tf_op jit(solution)/shard_map/ppermute | solution.py:524
  51.4 1.0 %collective-permute-start.16 = (bf16[336,128]{1,0:T(8,128)(2,1)S(1)}, bf16[336,128]{1,0:T(8,128)(2,1)S(1)}, u32[]{:S(2)}, u32[]{:S(2)}) collective-permute-start(bf16[336,128]{1,0:T(8,128)(2,1)S(1)} %pair_sum.1.refs_0_), channel_id=1, source_target_pairs={{0,16},{1,129},{2,18},{3,131},{4,20},{5,133},{6,22},{7,135},{8,24}... | collective-permute-start | bytes 258056 | tf_op jit(solution)/shard_map/ppermute | solution.py:552
  52.4 0.9 %collective-permute-start.15 = (bf16[336,128]{1,0:T(8,128)(2,1)S(1)}, bf16[336,128]{1,0:T(8,128)(2,1)S(1)}, u32[]{:S(2)}, u32[]{:S(2)}) collective-permute-start(bf16[336,128]{1,0:T(8,128)(2,1)S(1)} %pair_sum.1.refs_0_), channel_id=1, source_target_pairs={{0,18},{1,193},{2,16},{3,195},{4,22},{5,197},{6,20},{7,199},{8,26}... | collective-permute-start | bytes 258056 | tf_op jit(solution)/shard_map/ppermute | solution.py:552
  53.9 2.5 %collective-permute-done.16.refs_3_ = bf16[336,128]{1,0:T(8,128)(2,1)S(1)} collective-permute-done((bf16[336,128]{1,0:T(8,128)(2,1)S(1)}, bf16[336,128]{1,0:T(8,128)(2,1)S(1)}, u32[]{:S(2)}, u32[]{:S(2)}) %collective-permute-start.16) | collective-permute-done | bytes 86048 | tf_op jit(solution)/shard_map/ppermute | solution.py:552
  56.3 1.5 %collective-permute-done.14.refs_1_ = bf16[336,128]{1,0:T(8,128)(2,1)S(1)} collective-permute-done((bf16[336,128]{1,0:T(8,128)(2,1)S(1)}, bf16[336,128]{1,0:T(8,128)(2,1)S(1)}, u32[]{:S(2)}, u32[]{:S(2)}) %collective-permute-start.14) | collective-permute-done | bytes 86048 | tf_op jit(solution)/shard_map/ppermute | solution.py:552
  57.8 4.3 %collective-permute-start.18 = (bf16[1344,128]{1,0:T(8,128)(2,1)S(1)}, bf16[1344,128]{1,0:T(8,128)(2,1)S(1)}, u32[]{:S(2)}, u32[]{:S(2)}) collective-permute-start(bf16[1344,128]{1,0:T(8,128)(2,1)S(1)} %join.1.refs_0_), channel_id=1, source_target_pairs={{0,1},{1,0},{2,3},{3,2},{4,5},{5,4},{6,7},{7,6},{8,9},{9,8},{10,11... | collective-permute-start | bytes 1032200 | tf_op jit(solution)/shard_map/ppermute | solution.py:524
  62.2 1.0 %rows.1 = (bf16[128,512]{1,0:T(8,128)(2,1)}, bf16[128,512]{1,0:T(8,128)(2,1)}) custom-call(bf16[128,512]{1,0:T(8,128)(2,1)S(1)} %get-tuple-element.59.refs_0_.own_ref, bf16[128,512]{1,0:T(8,128)(2,1)S(1)} %get-tuple-element.60.refs_0_.own_cot_ref, f32[1,512]{1,0:T(1,128)S(1)} %get-tuple-element.61.refs_5_.in_gain_ref, ...), custom_call_target="tpu_custom_call" | custom-call | flops 2000000000 | bytes 3000000 | tf_op jit(solution)/shard_map/rows/pallas_call | solution.py:674
  63.4 1.7 %collective-permute-start.19 = (bf16[1344,128]{1,0:T(8,128)(2,1)S(1)}, bf16[1344,128]{1,0:T(8,128)(2,1)S(1)}, u32[]{:S(2)}, u32[]{:S(2)}) collective-permute-start(bf16[1344,128]{1,0:T(8,128)(2,1)S(1)} %join.1.refs_0_), channel_id=1, source_target_pairs={{0,192},{1,19},{2,194},{3,17},{4,196},{5,23},{6,198},{7,21},{8,200... | collective-permute-start | bytes 1032200 | tf_op jit(solution)/shard_map/ppermute | solution.py:552
  65.8 1.2 %unpack.3 = (f32[512,2048]{1,0:T(8,128)}, f32[512,512]{1,0:T(8,128)}) custom-call(bf16[1344,128]{1,0:T(8,128)(2,1)S(1)} %join.1.refs_0_, bf16[1344,128]{1,0:T(8,128)(2,1)S(1)} %collective-permute-done.18.refs_1_.refs_4_), custom_call_target="tpu_custom_call" | custom-call | flops 10000000000 | bytes 2000000 | tf_op jit(solution)/shard_map/unpack/pallas_call | solution.py:718
  67.1 7.4 %collective-permute-done.17.refs_0_.refs_1_ = bf16[1344,128]{1,0:T(8,128)(2,1)S(1)} collective-permute-done((bf16[1344,128]{1,0:T(8,128)(2,1)S(1)}, bf16[1344,128]{1,0:T(8,128)(2,1)S(1)}, u32[]{:S(2)}, u32[]{:S(2)}) %collective-permute-start.17) | collective-permute-done | bytes 344096 | tf_op jit(solution)/shard_map/ppermute | solution.py:552
  74.5 1.1 %collective-permute-start.23 = (bf16[1344,128]{1,0:T(8,128)(2,1)S(1)}, bf16[1344,128]{1,0:T(8,128)(2,1)S(1)}, u32[]{:S(2)}, u32[]{:S(2)}) collective-permute-start(bf16[1344,128]{1,0:T(8,128)(2,1)S(1)} %collective-permute-done.20.refs_2_.refs_3_), channel_id=1, source_target_pairs={{0,1},{1,0},{2,3},{3,2},{4,5},{5,4},{6,7},{7,6},{8,9},{9,8},{10,11... | collective-permute-start | bytes 1032200 | tf_op jit(solution)/shard_map/ppermute | solution.py:524
  76.1 1.5 %unpack.4 = (f32[512,2048]{1,0:T(8,128)}, f32[512,512]{1,0:T(8,128)}) custom-call(bf16[1344,128]{1,0:T(8,128)(2,1)S(1)} %collective-permute-done.17.refs_0_.refs_1_, bf16[1344,128]{1,0:T(8,128)(2,1)S(1)} %collective-permute-done.19.refs_1_.refs_2_, ...), custom_call_target="tpu_custom_call", output_to_operand_aliasing={{0}: (3, {}), {1}: (4, {})} | custom-call | flops 10000000000 | bytes 3000000 | tf_op jit(solution)/shard_map/unpack/pallas_call | solution.py:718
  77.9 1.6 %unpack.5 = (f32[512,2048]{1,0:T(8,128)}, f32[512,512]{1,0:T(8,128)}, f32[4,128]{1,0:T(4,128)}, f32[4,128]{1,0:T(4,128)}, f32[4,128]{1,0:T(4,128)}) custom-call(bf16[1344,128]{1,0:T(8,128)(2,1)S(1)} %join.1.refs_0_, bf16[1344,128]{1,0:T(8,128)(2,1)S(1)} %collective-permute-done.17.refs_0_.refs_1_, ...), custom_call_target="tpu_custom_call", output_to_operand_aliasing={{0}: (8, {}), {1}: (9, {})} | custom-call | flops 10000000000 | bytes 3000000 | tf_op jit(solution)/shard_map/unpack/pallas_call | solution.py:718
  (29 shorter events, 4.3 us)
Async XLA Ops:
  0.6 10.5 %collective-permute-start.5 = (bf16[128,512]{1,0:T(8,128)(2,1)}, bf16[128,512]{1,0:T(8,128)(2,1)S(1)}, u32[]{:S(2)}, u32[]{:S(2)}) collective-permute-start(bf16[128,512]{1,0:T(8,128)(2,1)} %bitcast.10), channel_id=1, source_target_pairs={{0,128},{64,192},{128,0},{192,64},{1,129},{65,193},{129,1},{193,65... | collective-permute-start | bytes 393224 | tf_op jit(solution)/shard_map/ppermute | solution.py:514
  4.3 6.9 %collective-permute-start.4 = (bf16[128,512]{1,0:T(8,128)(2,1)}, bf16[128,512]{1,0:T(8,128)(2,1)S(1)}, u32[]{:S(2)}, u32[]{:S(2)}) collective-permute-start(bf16[128,512]{1,0:T(8,128)(2,1)} %bitcast.11), channel_id=1, source_target_pairs={{0,192},{64,0},{128,64},{192,128},{1,193},{65,1},{129,65},{193,129... | collective-permute-start | bytes 393224 | tf_op jit(solution)/shard_map/ppermute | solution.py:514
  5.2 9.3 %collective-permute-start.3 = (bf16[128,512]{1,0:T(8,128)(2,1)}, bf16[128,512]{1,0:T(8,128)(2,1)S(1)}, u32[]{:S(2)}, u32[]{:S(2)}) collective-permute-start(bf16[128,512]{1,0:T(8,128)(2,1)} %bitcast.12), channel_id=1, source_target_pairs={{0,64},{64,128},{128,192},{192,0},{1,65},{65,129},{129,193},{193,1... | collective-permute-start | bytes 393224 | tf_op jit(solution)/shard_map/ppermute | solution.py:514
  7.7 10.2 %collective-permute-start.2 = (bf16[128,512]{1,0:T(8,128)(2,1)S(1)}, bf16[128,512]{1,0:T(8,128)(2,1)S(1)}, u32[]{:S(2)}, u32[]{:S(2)}) collective-permute-start(bf16[128,512]{1,0:T(8,128)(2,1)S(1)} %get-tuple-element.60.refs_0_.own_cot_ref), channel_id=1, source_target_pairs={{0,128},{64,192},{128,0},{192,64},{1,129},{65,193},{129,1},{193,65... | collective-permute-start | bytes 393224 | tf_op jit(solution)/shard_map/ppermute | solution.py:514
  8.4 9.5 %collective-permute-start.1 = (bf16[128,512]{1,0:T(8,128)(2,1)S(1)}, bf16[128,512]{1,0:T(8,128)(2,1)S(1)}, u32[]{:S(2)}, u32[]{:S(2)}) collective-permute-start(bf16[128,512]{1,0:T(8,128)(2,1)S(1)} %get-tuple-element.60.refs_0_.own_cot_ref), channel_id=1, source_target_pairs={{0,192},{64,0},{128,64},{192,128},{1,193},{65,1},{129,65},{193,129... | collective-permute-start | bytes 393224 | tf_op jit(solution)/shard_map/ppermute | solution.py:514
  11.1 6.8 %collective-permute-start = (bf16[128,512]{1,0:T(8,128)(2,1)S(1)}, bf16[128,512]{1,0:T(8,128)(2,1)S(1)}, u32[]{:S(2)}, u32[]{:S(2)}) collective-permute-start(bf16[128,512]{1,0:T(8,128)(2,1)S(1)} %get-tuple-element.60.refs_0_.own_cot_ref), channel_id=1, source_target_pairs={{0,64},{64,128},{128,192},{192,0},{1,65},{65,129},{129,193},{193,1... | collective-permute-start | bytes 393224 | tf_op jit(solution)/shard_map/ppermute | solution.py:514
  22.0 3.5 %collective-permute-start.6 = (bf16[1280,128]{1,0:T(8,128)(2,1)S(1)}, bf16[1280,128]{1,0:T(8,128)(2,1)S(1)}, u32[]{:S(2)}, u32[]{:S(2)}) collective-permute-start(bf16[1280,128]{1,0:T(8,128)(2,1)S(1)} %get-tuple-element.80), channel_id=1, source_target_pairs={{0,1},{1,0},{2,3},{3,2},{4,5},{5,4},{6,7},{7,6},{8,9},{9,8},{10,11... | collective-permute-start | bytes 983048 | tf_op jit(solution)/shard_map/ppermute | solution.py:524
  25.5 3.8 %collective-permute-start.7 = (bf16[336,128]{1,0:T(8,128)(2,1)S(1)}, bf16[336,128]{1,0:T(8,128)(2,1)S(1)}, u32[]{:S(2)}, u32[]{:S(2)}) collective-permute-start(bf16[336,128]{1,0:T(8,128)(2,1)S(1)} %get-tuple-element.90), channel_id=1, source_target_pairs={{0,2},{1,3},{2,0},{3,1},{4,6},{5,7},{6,4},{7,5},{8,10},{9,11},{10,... | collective-permute-start | bytes 258056 | tf_op jit(solution)/shard_map/ppermute | solution.py:524
  26.9 5.3 %collective-permute-start.8 = (bf16[336,128]{1,0:T(8,128)(2,1)S(1)}, bf16[336,128]{1,0:T(8,128)(2,1)S(1)}, u32[]{:S(2)}, u32[]{:S(2)}) collective-permute-start(bf16[336,128]{1,0:T(8,128)(2,1)S(1)} %get-tuple-element.91), channel_id=1, source_target_pairs={{0,18},{1,19},{2,16},{3,17},{4,22},{5,23},{6,20},{7,21},{8,26},{9,... | collective-permute-start | bytes 258056 | tf_op jit(solution)/shard_map/ppermute | solution.py:524
  28.0 5.7 %collective-permute-start.9 = (bf16[336,128]{1,0:T(8,128)(2,1)S(1)}, bf16[336,128]{1,0:T(8,128)(2,1)S(1)}, u32[]{:S(2)}, u32[]{:S(2)}) collective-permute-start(bf16[336,128]{1,0:T(8,128)(2,1)S(1)} %get-tuple-element.92), channel_id=1, source_target_pairs={{0,16},{1,17},{2,18},{3,19},{4,20},{5,21},{6,22},{7,23},{8,24},{9,... | collective-permute-start | bytes 258056 | tf_op jit(solution)/shard_map/ppermute | solution.py:524
  33.8 7.5 %collective-permute-start.12 = (bf16[336,128]{1,0:T(8,128)(2,1)S(1)}, bf16[336,128]{1,0:T(8,128)(2,1)S(1)}, u32[]{:S(2)}, u32[]{:S(2)}) collective-permute-start(bf16[336,128]{1,0:T(8,128)(2,1)S(1)} %square_sum.1.own_ref), channel_id=1, source_target_pairs={{0,48},{1,49},{2,50},{3,51},{4,52},{5,53},{6,54},{7,55},{8,56},{9,... | collective-permute-start | bytes 258056 | tf_op jit(solution)/shard_map/ppermute | solution.py:524
  35.7 7.4 %collective-permute-start.11 = (bf16[336,128]{1,0:T(8,128)(2,1)S(1)}, bf16[336,128]{1,0:T(8,128)(2,1)S(1)}, u32[]{:S(2)}, u32[]{:S(2)}) collective-permute-start(bf16[336,128]{1,0:T(8,128)(2,1)S(1)} %square_sum.1.own_ref), channel_id=1, source_target_pairs={{0,62},{1,63},{2,52},{3,53},{4,50},{5,51},{6,56},{7,57},{8,54},{9,... | collective-permute-start | bytes 258056 | tf_op jit(solution)/shard_map/ppermute | solution.py:524
  41.3 4.5 %collective-permute-start.10 = (bf16[336,128]{1,0:T(8,128)(2,1)S(1)}, bf16[336,128]{1,0:T(8,128)(2,1)S(1)}, u32[]{:S(2)}, u32[]{:S(2)}) collective-permute-start(bf16[336,128]{1,0:T(8,128)(2,1)S(1)} %square_sum.1.own_ref), channel_id=1, source_target_pairs={{0,14},{1,15},{2,4},{3,5},{4,2},{5,3},{6,8},{7,9},{8,6},{9,7},{10,... | collective-permute-start | bytes 258056 | tf_op jit(solution)/shard_map/ppermute | solution.py:524
  45.9 5.5 %collective-permute-start.13 = (bf16[336,128]{1,0:T(8,128)(2,1)S(1)}, bf16[336,128]{1,0:T(8,128)(2,1)S(1)}, u32[]{:S(2)}, u32[]{:S(2)}) collective-permute-start(bf16[336,128]{1,0:T(8,128)(2,1)S(1)} %four_sum.1.left_ref), channel_id=1, source_target_pairs={{0,6},{1,7},{2,12},{3,13},{4,10},{5,11},{6,0},{7,1},{8,14},{9,15},... | collective-permute-start | bytes 258056 | tf_op jit(solution)/shard_map/ppermute | solution.py:524
  51.4 4.9 %collective-permute-start.16 = (bf16[336,128]{1,0:T(8,128)(2,1)S(1)}, bf16[336,128]{1,0:T(8,128)(2,1)S(1)}, u32[]{:S(2)}, u32[]{:S(2)}) collective-permute-start(bf16[336,128]{1,0:T(8,128)(2,1)S(1)} %pair_sum.1.refs_0_), channel_id=1, source_target_pairs={{0,16},{1,129},{2,18},{3,131},{4,20},{5,133},{6,22},{7,135},{8,24}... | collective-permute-start | bytes 258056 | tf_op jit(solution)/shard_map/ppermute | solution.py:552
  52.4 3.9 %collective-permute-start.15 = (bf16[336,128]{1,0:T(8,128)(2,1)S(1)}, bf16[336,128]{1,0:T(8,128)(2,1)S(1)}, u32[]{:S(2)}, u32[]{:S(2)}) collective-permute-start(bf16[336,128]{1,0:T(8,128)(2,1)S(1)} %pair_sum.1.refs_0_), channel_id=1, source_target_pairs={{0,18},{1,193},{2,16},{3,195},{4,22},{5,197},{6,20},{7,199},{8,26}... | collective-permute-start | bytes 258056 | tf_op jit(solution)/shard_map/ppermute | solution.py:552
  53.3 4.5 %collective-permute-start.14 = (bf16[336,128]{1,0:T(8,128)(2,1)S(1)}, bf16[336,128]{1,0:T(8,128)(2,1)S(1)}, u32[]{:S(2)}, u32[]{:S(2)}) collective-permute-start(bf16[336,128]{1,0:T(8,128)(2,1)S(1)} %pair_sum.1.refs_0_), channel_id=1, source_target_pairs={{0,2},{1,65},{2,0},{3,67},{4,6},{5,69},{6,4},{7,71},{8,10},{9,73},... | collective-permute-start | bytes 258056 | tf_op jit(solution)/shard_map/ppermute | solution.py:552
  57.8 8.0 %collective-permute-start.18 = (bf16[1344,128]{1,0:T(8,128)(2,1)S(1)}, bf16[1344,128]{1,0:T(8,128)(2,1)S(1)}, u32[]{:S(2)}, u32[]{:S(2)}) collective-permute-start(bf16[1344,128]{1,0:T(8,128)(2,1)S(1)} %join.1.refs_0_), channel_id=1, source_target_pairs={{0,1},{1,0},{2,3},{3,2},{4,5},{5,4},{6,7},{7,6},{8,9},{9,8},{10,11... | collective-permute-start | bytes 1032200 | tf_op jit(solution)/shard_map/ppermute | solution.py:524
  63.2 11.3 %collective-permute-start.20 = (bf16[1344,128]{1,0:T(8,128)(2,1)S(1)}, bf16[1344,128]{1,0:T(8,128)(2,1)S(1)}, u32[]{:S(2)}, u32[]{:S(2)}) collective-permute-start(bf16[1344,128]{1,0:T(8,128)(2,1)S(1)} %join.1.refs_0_), channel_id=1, source_target_pairs={{0,128},{1,17},{2,130},{3,19},{4,132},{5,21},{6,134},{7,23},{8,136... | collective-permute-start | bytes 1032200 | tf_op jit(solution)/shard_map/ppermute | solution.py:552
  63.4 11.0 %collective-permute-start.19 = (bf16[1344,128]{1,0:T(8,128)(2,1)S(1)}, bf16[1344,128]{1,0:T(8,128)(2,1)S(1)}, u32[]{:S(2)}, u32[]{:S(2)}) collective-permute-start(bf16[1344,128]{1,0:T(8,128)(2,1)S(1)} %join.1.refs_0_), channel_id=1, source_target_pairs={{0,192},{1,19},{2,194},{3,17},{4,196},{5,23},{6,198},{7,21},{8,200... | collective-permute-start | bytes 1032200 | tf_op jit(solution)/shard_map/ppermute | solution.py:552
  65.2 9.3 %collective-permute-start.17 = (bf16[1344,128]{1,0:T(8,128)(2,1)S(1)}, bf16[1344,128]{1,0:T(8,128)(2,1)S(1)}, u32[]{:S(2)}, u32[]{:S(2)}) collective-permute-start(bf16[1344,128]{1,0:T(8,128)(2,1)S(1)} %join.1.refs_0_), channel_id=1, source_target_pairs={{0,64},{1,3},{2,66},{3,1},{4,68},{5,7},{6,70},{7,5},{8,72},{9,11},... | collective-permute-start | bytes 1032200 | tf_op jit(solution)/shard_map/ppermute | solution.py:552
  74.5 3.2 %collective-permute-start.23 = (bf16[1344,128]{1,0:T(8,128)(2,1)S(1)}, bf16[1344,128]{1,0:T(8,128)(2,1)S(1)}, u32[]{:S(2)}, u32[]{:S(2)}) collective-permute-start(bf16[1344,128]{1,0:T(8,128)(2,1)S(1)} %collective-permute-done.20.refs_2_.refs_3_), channel_id=1, source_target_pairs={{0,1},{1,0},{2,3},{3,2},{4,5},{5,4},{6,7},{7,6},{8,9},{9,8},{10,11... | collective-permute-start | bytes 1032200 | tf_op jit(solution)/shard_map/ppermute | solution.py:524
  75.6 2.1 %collective-permute-start.22 = (bf16[1344,128]{1,0:T(8,128)(2,1)S(1)}, bf16[1344,128]{1,0:T(8,128)(2,1)S(1)}, u32[]{:S(2)}, u32[]{:S(2)}) collective-permute-start(bf16[1344,128]{1,0:T(8,128)(2,1)S(1)} %collective-permute-done.19.refs_1_.refs_2_), channel_id=1, source_target_pairs={{0,1},{1,0},{2,3},{3,2},{4,5},{5,4},{6,7},{7,6},{8,9},{9,8},{10,11... | collective-permute-start | bytes 1032200 | tf_op jit(solution)/shard_map/ppermute | solution.py:524
  75.7 2.2 %collective-permute-start.21 = (bf16[1344,128]{1,0:T(8,128)(2,1)S(1)}, bf16[1344,128]{1,0:T(8,128)(2,1)S(1)}, u32[]{:S(2)}, u32[]{:S(2)}) collective-permute-start(bf16[1344,128]{1,0:T(8,128)(2,1)S(1)} %collective-permute-done.17.refs_0_.refs_1_), channel_id=1, source_target_pairs={{0,1},{1,0},{2,3},{3,2},{4,5},{5,4},{6,7},{7,6},{8,9},{9,8},{10,11... | collective-permute-start | bytes 1032200 | tf_op jit(solution)/shard_map/ppermute | solution.py:524
